TPU v7x, 32 devices: a whole 2x2x4 slice. The times are simulated.
32 devices in a mesh: parts: 2 (over x), sector: 8 (over z, y), term: 2 (over core).
Axes of the slice: x: 2, y: 2, z: 4, core: 2. Of those that a mesh axis runs over, the one named last changes fastest.
Arguments:
- wavefunction: bfloat16 [512, 128, 128], P(('parts', 'sector')), parts along dimension 0, may hold values from -12 to 12
- left_sector: int32 [512], P(('parts', 'sector')), parts along dimension 0, may hold values from 0 to 63, as said below
- right_sector: int32 [512], P(('parts', 'sector')), parts along dimension 0, may hold values from 0 to 63, as said below
- phys_index: int32 [512], P(('parts', 'sector')), parts along dimension 0, may hold values from 0 to 15
- left_environment: bfloat16 [28, 64, 128, 128], P(('parts', 'term'), 'sector'), parts along dimension 0, may hold values from -0.5 to 0.5
- right_environment: bfloat16 [28, 64, 128, 128], P(('parts', 'term'), 'sector'), parts along dimension 0, may hold values from -0.5 to 0.5
- term_weights: bfloat16 [28, 16], P(('parts', 'term')), parts along dimension 0, may hold values from -1.5 to 1.5
Outputs:
- image: float32 [512, 128, 128], P(('parts', 'sector')), parts along dimension 0
- correction: float32 [512, 128, 128], P(('parts', 'sector')), parts along dimension 0
- rayleigh: float32 [2], P('parts'), parts along dimension 0
There are 2 independent parts, one for each index of `parts`. A program takes and returns all parts, laid end to end along the dimension named above; each array names one. Nothing has to cross between parts.
Inputs may be any that keep to these rules, and one draw needn't show every extreme that they name: `left_sector`: for every device of the sector axis, the blocks of one device have at most 8 left sectors lying on it; in every draw one device is named exactly 8 times by the blocks of every device. `right_sector`: block k's right sector lies on device k // 32, among sectors (k // 32) * 8 to (k // 32) * 8 + 7.
All inputs are finite; a program needn't handle non-finite values.
Results may differ from a plain program's by a relative error of at most 0.0048.
Values may be sent and summed in bfloat16 or wider, within the bound.
No kernel may reach another device: no remote copies, remote signals or barrier semaphores. Data moves between devices by JAX's collectives and lax.ppermute only.
A program may use at most 128 MiB of HBM per device.

v0:
```python
import jax
import jax.numpy as jnp
from jax import lax
from jax.sharding import PartitionSpec as P


def on_device(
    wavefunction,
    left_sector,
    right_sector,
    phys_index,
    left_environment,
    right_environment,
    term_weights,
):
    blocks = wavefunction.shape[0]
    sector_dim = wavefunction.shape[1]
    sector_count = lax.axis_size("sector")
    per_device = right_environment.shape[1]
    capacity = 2 * max(1, blocks // sector_count)
    own_index = lax.axis_index("sector")
    right_local = right_sector - own_index * per_device
    target = left_sector // per_device
    positions = jnp.arange(blocks)
    earlier = (target[None, :] == target[:, None]) & (positions[None, :] < positions[:, None])
    placement_order = jnp.sum(earlier.astype(jnp.int32), axis=1)
    physical_selector_matrix = (
        phys_index[:, None] == jnp.arange(term_weights.shape[1])[None, :]
    ).astype(jnp.bfloat16)
    slot_index = target * capacity + placement_order
    slot_count = sector_count * capacity
    selector_f = (jnp.arange(slot_count)[:, None] == slot_index[None, :]).astype(jnp.float32)
    wanted = jnp.dot(
        selector_f, (left_sector % per_device).astype(jnp.float32), precision=lax.Precision.HIGHEST
    ).astype(jnp.int32)
    requests = lax.all_to_all(
        wanted.reshape(sector_count, capacity), "sector", split_axis=0, concat_axis=0, tiled=True
    )
    picked = jnp.take(left_environment, requests.reshape(-1), axis=1)
    picked = jnp.moveaxis(picked, 0, 1).reshape(
        sector_count, capacity, left_environment.shape[0], sector_dim, sector_dim
    )
    fetched = lax.all_to_all(picked, "sector", split_axis=0, concat_axis=0, tiled=True)
    left_blocks = jnp.take(
        fetched.reshape(slot_count, left_environment.shape[0], sector_dim, sector_dim),
        slot_index,
        axis=0,
    )
    right_taken = jnp.take(right_environment, right_local, axis=1)
    block_weights = jnp.dot(
        physical_selector_matrix, term_weights.T, preferred_element_type=jnp.float32
    )
    environment_product = jnp.einsum(
        "kab,tkcb->ktac", wavefunction, right_taken, preferred_element_type=jnp.float32
    )
    carried = (environment_product * block_weights[:, :, None, None]).astype(jnp.bfloat16)
    image_partial_result = jnp.einsum(
        "ktij,ktjc->kic", left_blocks, carried, preferred_element_type=jnp.float32
    )
    image = lax.psum(image_partial_result, "term")
    wave_f32 = wavefunction.astype(jnp.float32)
    norm_wave = jnp.sum(wave_f32 * wave_f32)
    correlation = jnp.sum(wave_f32 * image)
    entries = blocks * sector_count * sector_dim * sector_dim
    norm_all, correlation_all = lax.psum((norm_wave, correlation), "sector")
    rayleigh = correlation_all / norm_all
    residual = image - rayleigh * wave_f32
    norm_resid = lax.psum(jnp.sum(residual * residual), "sector")
    correction = residual * lax.rsqrt(norm_resid / entries + 1e-06)
    return (image, correction, jnp.reshape(rayleigh, (1,)))


def solution(mesh):
    placed = (
        P(("parts", "sector"), None, None),
        P(("parts", "sector")),
        P(("parts", "sector")),
        P(("parts", "sector")),
        P(("parts", "term"), "sector", None, None),
        P(("parts", "term"), "sector", None, None),
        P(("parts", "term"), None),
    )
    return jax.shard_map(
        on_device,
        mesh=mesh,
        in_specs=placed,
        out_specs=(
            P(("parts", "sector"), None, None),
            P(("parts", "sector"), None, None),
            P("parts"),
        ),
        check_vma=False,
    )
```

profile of v0, /device:TPU:0, one launch (start us, length us, event | category | flops | bytes accessed | tf_op | source)
XLA Modules:
  0.0 469.2 jit_solution(449200237347254024)
XLA Ops:
  7.2 0.0 copy-start
  7.2 0.8 and_select_fusion.1
  8.0 0.2 convert_reduce_fusion
  8.2 0.7 compare_and_fusion.2
  8.8 0.8 fusion.24
  9.6 0.1 all_to_all.9
  9.7 13.6 %all_to_all.14 = s32[8,1,8]{2,1,0:T(1,128)S(1)} all-to-all(s32[8,1,8]{2,1,0:T(1,128)S(1)} %bitcast.40), channel_id=1, replica_groups=mesh['parts'=2,'sector'=8,'term'=2] {'sector'}, dimensions={0} | all-to-all | bytes 512 | tf_op jit(solution)/shard_map/all_to_all | solution.py:36
  23.3 0.1 reshape.76
  23.4 0.5 broadcast.110
  23.9 0.7 reduce.5
  24.5 0.1 reshape.75
  24.6 0.0 copy-done
  24.6 7.8 %gather_fusion = bf16[64,7,128,128]{3,2,1,0:T(8,128)(2,1)} fusion(bf16[7,8,128,128]{3,2,1,0:T(8,128)(2,1)S(1)} %copy-done, s32[1024]{0:T(1024)S(1)} %pad_clamp_fusion.2), kind=kCustom, calls=%fused_computation | custom fusion | bytes 29360384 | tf_op jit(solution)/shard_map/jit(_take)/gather | solution.py:39
  32.5 13.5 %broadcast_select_fusion = bf16[64,7,128,128]{3,2,1,0:T(8,128)(2,1)} fusion(bf16[64,7,128,128]{3,2,1,0:T(8,128)(2,1)} %gather_fusion, pred[64]{0:T(512)(128)(4,1)S(1)} %compare_and_fusion.1), kind=kLoop, calls=%fused_computation.4 | loop fusion | flops 7340032 | bytes 29360192 | tf_op jit(solution)/shard_map/jit(_take)/select_n | solution.py:39
  46.0 0.0 copy-start.4
  46.0 0.0 copy-start.2
  46.0 5.7 %all-to-all-start.1 = ((bf16[8,8,7,128,128]{4,3,2,1,0:T(8,128)(2,1)}), bf16[8,8,7,128,128]{4,3,2,1,0:T(8,128)(2,1)}, u32[]{:S(2)}, u32[]{:S(2)}) async-start(bf16[8,8,7,128,128]{4,3,2,1,0:T(8,128)(2,1)} %bitcast.38), calls=%async_computation.1 | async-start | bytes 29360128 | tf_op jit(solution)/shard_map/all_to_all | solution.py:43
  51.7 0.0 all-reduce.3.cloned.1.call-start
  51.8 0.0 copy-done.4
  51.8 0.0 copy-done.2
  51.8 0.0 copy-start.5
  51.8 0.0 copy-start.6
  51.8 4.5 gather_fusion.2
  56.3 0.0 copy-done.5
  56.3 0.0 copy-done.6
  56.3 0.2 fusion.29
  56.5 311.9 %all-to-all-done.1 = bf16[8,8,7,128,128]{4,3,2,1,0:T(8,128)(2,1)} async-done(((bf16[8,8,7,128,128]{4,3,2,1,0:T(8,128)(2,1)}), bf16[8,8,7,128,128]{4,3,2,1,0:T(8,128)(2,1)}, u32[]{:S(2)}, u32[]{:S(2)}) %all-to-all-start.1) | async-done | bytes 14680096 | tf_op jit(solution)/shard_map/all_to_all | solution.py:43
  368.4 0.0 copy-start.3
  368.4 9.7 %gather_fusion.1 = bf16[32,7,128,128]{3,2,1,0:T(8,128)(2,1)} fusion(bf16[64,7,128,128]{3,2,1,0:T(8,128)(2,1)} %bitcast.5, s32[1024]{0:T(1024)S(1)} %pad_clamp_fusion.1), kind=kCustom, calls=%fused_computation.1 | custom fusion | bytes 14680192 | tf_op jit(solution)/shard_map/jit(_take)/gather | solution.py:44
  378.1 0.0 copy-done.3
  378.1 8.8 %fusion.16 = f32[32,128,128]{2,1,0:T(8,128)} fusion(f32[32,7]{1,0:T(8,128)S(1)} %fusion.29, bf16[32,7,128,128]{3,2,1,0:T(8,128)(2,1)} %gather_fusion.2, pred[32]{0:T(512)(128)(4,1)S(1)} %get-tuple-element.9, bf16[32,7,128,128]{3,2,1,0:T(8,128)(2,1)} %gather_fusion.1, pred[32]{0:T(512)(128)(4,1)S(1)} %get-tuple-element.7, bf16[32,128,128]{2,1,0:T(8,128)(2,1)S(1)} %copy-done.3), kind=kOutput, calls=%fused_computation.21 | convolution fusion | flops 1893728256 | bytes 17826752 | tf_op jit(solution)/shard_map/ktij,ktjc->kic/dot_general | solution.py:57
  386.9 0.0 all-reduce.3.cloned.1.call-update
  386.9 0.0 copy-start.1
  386.9 20.3 %all-reduce.3.cloned.1.call-done = f32[32,128,128]{2,1,0:T(8,128)} async-done(((f32[32,128,128]{2,1,0:T(8,128)}), f32[32,128,128]{2,1,0:T(8,128)}) %all-reduce.3.cloned.1.call-update) | async-done | bytes 2097168 | tf_op jit(solution)/shard_map/psum | solution.py:60
  407.2 2.7 fusion.14
  410.0 22.2 %all-reduce = (f32[]{:T(128)}, f32[]{:T(128)}) all-reduce(f32[]{:T(128)} %get-tuple-element.4, f32[]{:T(128)} %get-tuple-element.3), channel_id=1, replica_groups=mesh['parts'=2,'sector'=8,'term'=2] {'sector'}, use_global_device_ids=true, to_apply=%region_3.4 | all-reduce | flops 2 | bytes 16 | tf_op jit(solution)/shard_map/psum | solution.py:65
  433.6 2.7 multiply_reduce_fusion
  436.3 17.7 %psum.31 = f32[]{:T(128)} all-reduce(f32[]{:T(128)} %multiply_reduce_fusion), channel_id=1, replica_groups=mesh['parts'=2,'sector'=8,'term'=2] {'sector'}, use_global_device_ids=true, to_apply=%region_7.8 | all-reduce | flops 1 | bytes 8 | tf_op jit(solution)/shard_map/psum | solution.py:68
  454.7 3.3 fusion.23
  458.1 3.1 copy.19
  461.2 0.0 copy-done.1
  (7 shorter events, 0.1 us)
Async XLA Ops:
  7.2 17.5 %copy-start = (bf16[7,8,128,128]{3,2,1,0:T(8,128)(2,1)S(1)}, bf16[7,8,128,128]{3,2,1,0:T(8,128)(2,1)}, u32[]{:S(2)}) copy-start(bf16[7,8,128,128]{3,2,1,0:T(8,128)(2,1)} %param.11) | copy-start | bytes 5505028
  46.0 5.7 %copy-start.4 = (s32[32]{0:T(128)S(1)}, s32[32]{0:T(128)}, u32[]{:S(2)}) copy-start(s32[32]{0:T(128)} %param.9) | copy-start | bytes 388
  46.0 5.8 %copy-start.2 = (bf16[7,8,128,128]{3,2,1,0:T(8,128)(2,1)S(1)}, bf16[7,8,128,128]{3,2,1,0:T(8,128)(2,1)}, u32[]{:S(2)}) copy-start(bf16[7,8,128,128]{3,2,1,0:T(8,128)(2,1)} %param.12) | copy-start | bytes 5505028
  46.0 322.4 %all-to-all-start.1 = ((bf16[8,8,7,128,128]{4,3,2,1,0:T(8,128)(2,1)}), bf16[8,8,7,128,128]{4,3,2,1,0:T(8,128)(2,1)}, u32[]{:S(2)}, u32[]{:S(2)}) async-start(bf16[8,8,7,128,128]{4,3,2,1,0:T(8,128)(2,1)} %bitcast.38), calls=%async_computation.1 | async-start | bytes 29360128 | tf_op jit(solution)/shard_map/all_to_all | solution.py:43
  51.7 355.5 %all-reduce.3.cloned.1.call-start = ((), (), s32[]{:S(2)}) async-start(), calls=%async_computation.2 | async-start | bytes 4194304 | tf_op jit(solution)/shard_map/psum | solution.py:60
  51.8 4.5 copy-start.5
  51.8 4.5 copy-start.6
  368.4 9.7 %copy-start.3 = (bf16[32,128,128]{2,1,0:T(8,128)(2,1)S(1)}, bf16[32,128,128]{2,1,0:T(8,128)(2,1)}, u32[]{:S(2)}) copy-start(bf16[32,128,128]{2,1,0:T(8,128)(2,1)} %param.7) | copy-start | bytes 3145732
  386.9 74.3 %copy-start.1 = (bf16[7,8,128,128]{3,2,1,0:T(8,128)(2,1)S(1)}, bf16[7,8,128,128]{3,2,1,0:T(8,128)(2,1)}, u32[]{:S(2)}) copy-start(bf16[7,8,128,128]{3,2,1,0:T(8,128)(2,1)} %param.11) | copy-start | bytes 5505028
Sparse Core Ops, SparseCore 0:
  387.0 20.1 all-reduce.2
where the time goes:
time: 470 us; the launch traced here: 469 us
  waiting for transfers between devices  332 us (71%)
  blocking collectives  53.6 us (11%)
  local copies, waits for them, and re-layouts  25.9 us (6%)
  other arithmetic  24.7 us (5%)
  between operations  17.3 us (4%)
  matrix products  9.72 us (2%)
  starting transfers between devices  5.72 us (1%)
    all_to_all x1, waiting for transfers between devices, on_device(): lax.all_to_all(picked, 'sector', split_axis=0, concat_axis=0, tiled=True)  312 us
    psum x1, blocking collectives, on_device(): norm_all, correlation_all = lax.psum((norm_wave, correlation), 'sector')  22.2 us
    psum x1, waiting for transfers between devices, on_device(): image = lax.psum(image_partial_result, 'term')  20.3 us
    psum x1, blocking collectives, on_device(): norm_resid = lax.psum(jnp.sum(residual * residual), 'sector')  17.7 us
    all_to_all x1, blocking collectives, on_device(): lax.all_to_all(wanted.reshape(sector_count, capacity), 'sector', split_ax...  13.6 us
    select_n x2, other arithmetic, on_device(): picked = jnp.take(left_environment, requests.reshape(-1), axis=1)  13.5 us
    gather x1, local copies, waits for them, and re-layouts, on_device(): jnp.take(fetched.reshape(slot_count, left_environment.shape[0], sector_di...  9.69 us
  transfers between devices with their start and end apart: 2, of which 2 were waited for; matrix products, arithmetic and copies ran while one was open for 1% of the time, Pallas kernels for 0%

commit v1 on v0

--- a/solution.py
+++ b/solution.py
@@ -1,10 +1,17 @@
+import functools
+
 import jax
 import jax.numpy as jnp
 from jax import lax
+from jax.experimental import pallas as pl
+from jax.experimental.pallas import tpu as pltpu
 from jax.sharding import PartitionSpec as P
 
-
-def on_device(
+BOTH = ("sector", "term")
+VMEM_LIMIT = 48 * 2**20
+
+
+def on_device_any(
     wavefunction,
     left_sector,
     right_sector,
@@ -70,6 +77,473 @@
     return (image, correction, jnp.reshape(rayleigh, (1,)))
 
 
+def pairs_of(target, chosen=lambda z, y, c: True):
+    found = []
+    for z in range(4):
+        for y in range(2):
+            for c in range(2):
+                if chosen(z, y, c):
+                    to = target(z, y, c)
+                    if 0 <= to[0] < 4:
+                        found.append(((z * 2 + y) * 2 + c, (to[0] * 2 + to[1]) * 2 + to[2]))
+    return found
+
+
+def inner(z, y, c):
+    return z in (1, 2)
+
+
+def outer(z, y, c):
+    return z in (0, 3)
+
+
+DIAGONAL = pairs_of(lambda z, y, c: (z, 1 - y, 1 - c), lambda z, y, c: y != c)
+CORE = pairs_of(lambda z, y, c: (z, y, 1 - c))
+CORE_INNER = pairs_of(lambda z, y, c: (z, y, 1 - c), inner)
+COLUMN = pairs_of(lambda z, y, c: (z, 1 - y, c))
+COLUMN_INNER = pairs_of(lambda z, y, c: (z, 1 - y, c), inner)
+UP = pairs_of(lambda z, y, c: (z + 1, y, c))
+DOWN = pairs_of(lambda z, y, c: (z - 1, y, c))
+UP_INNER = pairs_of(lambda z, y, c: (z + 1, y, c), inner)
+DOWN_INNER = pairs_of(lambda z, y, c: (z - 1, y, c), inner)
+GUEST = pairs_of(lambda z, y, c: (1 if z == 0 else 2, y, c), outer)
+GUEST_BACK = pairs_of(lambda z, y, c: (0 if z == 1 else 3, y, c), inner)
+NEAR = pairs_of(lambda z, y, c: (z ^ 1, y, c))
+FAR = pairs_of(lambda z, y, c: (z ^ 2, y, c))
+
+
+def move(array, pairs):
+    return lax.ppermute(array, BOTH, pairs)
+
+
+def carried_of(wave, right, weights):
+    terms, dim, _ = right.shape
+    product = lax.dot_general(
+        wave,
+        right.reshape(terms * dim, dim),
+        (((1,), (1,)), ((), ())),
+        preferred_element_type=jnp.float32,
+    )
+    return (product * weights).astype(jnp.bfloat16)
+
+
+def applied(left, carried):
+    terms, dim, _ = left.shape
+    lefts = jnp.concatenate([left[t] for t in range(terms)], axis=1)
+    stacked = jnp.concatenate(
+        [carried[:, t * dim : (t + 1) * dim] for t in range(terms)], axis=0
+    )
+    return jnp.dot(lefts, stacked, preferred_element_type=jnp.float32)
+
+
+def near_kernel(
+    table, weights, wave_own, wave_other, right_mine, right_sib, left_mine, left_below, left_above,
+    own_out, other_out, wave, right, left, sems,
+):
+    blocks = own_out.shape[0]
+    copies = [
+        pltpu.make_async_copy(source, target, sems.at[n])
+        for n, (source, target) in enumerate(
+            (
+                (wave_own, wave.at[0]),
+                (wave_other, wave.at[1]),
+                (right_mine, right.at[0]),
+                (right_sib, right.at[1]),
+                (left_mine, left.at[0]),
+                (left_below, left.at[1]),
+                (left_above, left.at[2]),
+            )
+        )
+    ]
+    for copy in copies:
+        copy.start()
+    own_out[...] = jnp.zeros_like(own_out)
+    other_out[...] = jnp.zeros_like(other_out)
+    for copy in copies:
+        copy.wait()
+    for relation in range(2):
+
+        @pl.loop(0, blocks)
+        def _(slot):
+            row = relation * blocks + slot
+            stage = table[row, 0]
+
+            @pl.when((stage >= 0) & (stage < 3))
+            def _():
+                block_right = right[table[row, 3], :, table[row, 4]]
+                carried = carried_of(
+                    wave[relation, table[row, 1]], block_right, weights[pl.ds(row, 1), :]
+                )
+                result = applied(left[stage, :, table[row, 2]], carried)
+                if relation == 0:
+                    own_out[slot] = result
+                else:
+                    other_out[slot] = result.astype(jnp.bfloat16)
+
+
+def carry_kernel(
+    table, weights, wave_own, wave_other, wave_guest, right_mine, right_sib, guest_mine, guest_sib,
+    out, wave, guest, right, sems,
+):
+    slots = guest.shape[0]
+    copies = [
+        pltpu.make_async_copy(source, target, sems.at[n])
+        for n, (source, target) in enumerate(
+            (
+                (wave_own, wave.at[0]),
+                (wave_other, wave.at[1]),
+                (wave_guest, guest),
+                (right_mine, right.at[0]),
+                (right_sib, right.at[1]),
+                (guest_mine, right.at[2]),
+                (guest_sib, right.at[3]),
+            )
+        )
+    ]
+    for copy in copies:
+        copy.start()
+    for copy in copies:
+        copy.wait()
+
+    @pl.loop(0, slots)
+    def _(row):
+        @pl.when(table[row, 0] == 3)
+        def _():
+            block_right = right[table[row, 3], :, table[row, 4]]
+            relation = row // (slots // 2)
+            out[row] = carried_of(
+                wave[relation, table[row, 1]], block_right, weights[pl.ds(row, 1), :]
+            )
+
+    @pl.loop(slots, 2 * slots)
+    def _(row):
+        @pl.when(table[row, 0] == 3)
+        def _():
+            block_right = right[2 + table[row, 3], :, table[row, 4]]
+            out[row] = carried_of(guest[row - slots], block_right, weights[pl.ds(row, 1), :])
+
+
+def far_kernel(
+    table, low, carried, left_two_below, left_two_above, own, other,
+    own_out, other_out, guest_own_out, guest_other_out, held, left, sems, left_sem,
+):
+    half = own_out.shape[0]
+    rows = 4 * half
+
+    @pl.when(low[0] == 1)
+    def _():
+        pltpu.make_async_copy(left_two_above, left, left_sem.at[0]).start()
+
+    @pl.when(low[0] == 0)
+    def _():
+        pltpu.make_async_copy(left_two_below, left, left_sem.at[0]).start()
+
+    for row in range(rows):
+
+        @pl.when(table[row, 0] == 3)
+        def _():
+            pltpu.make_async_copy(carried.at[row], held.at[row], sems.at[row]).start()
+
+    own_out[...] = own[...]
+    other_out[...] = other[...]
+    guest_own_out[...] = jnp.zeros_like(guest_own_out)
+    guest_other_out[...] = jnp.zeros_like(guest_other_out)
+    pltpu.make_async_copy(left_two_above, left, left_sem.at[0]).wait()
+    for part, target in ((2, guest_own_out), (3, guest_other_out), (0, own_out), (1, other_out)):
+
+        @pl.loop(0, half)
+        def _(slot):
+            row = part * half + slot
+
+            @pl.when(table[row, 0] == 3)
+            def _():
+                pltpu.make_async_copy(carried.at[row], held.at[row], sems.at[row]).wait()
+                result = applied(left[:, table[row, 2]], held[row])
+                target[slot] = result.astype(target.dtype)
+
+
+def pick_kernel(table, first, second, out):
+    slots = out.shape[0]
+    half = slots // 2
+
+    @pl.loop(0, half)
+    def _(slot):
+        out[slot] = first[table[slot, 1]]
+        out[half + slot] = second[table[half + slot, 1]]
+
+
+def gather_kernel(
+    table, first_own, last_own, guest_own, first_sib, last_sib, guest_sib, wave, image, sums
+):
+    blocks = image.shape[0]
+    zero = jnp.zeros((8, 128), jnp.float32)
+
+    def folded(value):
+        return jnp.sum(value.reshape(-1, 8, 128), axis=0)
+
+    def place(k, totals):
+        for code, source in enumerate(
+            (first_own, last_own, guest_own, first_sib, last_sib, guest_sib)
+        ):
+
+            @pl.when(table[k, 0] == code)
+            def _():
+                image[k] = source[table[k, 1]].astype(jnp.float32)
+
+        value = wave[k].astype(jnp.float32)
+        return totals[0] + folded(value * value), totals[1] + folded(value * image[k])
+
+    norm_map, correlation_map = lax.fori_loop(0, blocks, place, (zero, zero))
+    norm = jnp.sum(norm_map, keepdims=True)
+    correlation = jnp.sum(correlation_map, keepdims=True)
+    ratio = jnp.where(norm > 0, correlation / jnp.where(norm > 0, norm, 1.0), 0.0)
+
+    def rest(k, total):
+        residual = image[k] - ratio * wave[k].astype(jnp.float32)
+        return total + folded(residual * residual)
+
+    resid = jnp.sum(lax.fori_loop(0, blocks, rest, zero), keepdims=True)
+    line = lax.broadcasted_iota(jnp.int32, (8, 128), 0)
+    sums[...] = jnp.where(
+        line == 0, norm, jnp.where(line == 1, correlation, jnp.where(line == 2, resid, 0.0))
+    )
+
+
+def ratio_of(norm, correlation):
+    return jnp.where(norm > 0, correlation / jnp.where(norm > 0, norm, 1.0), 0.0)
+
+
+def merged(one, two):
+    low, high = jnp.minimum(one[0], two[0]), jnp.maximum(one[0], two[0])
+    norm = one[0] + two[0]
+    gap = ratio_of(one[0], one[1]) - ratio_of(two[0], two[1])
+    shared = low * jnp.where(norm > 0, high / jnp.where(norm > 0, norm, 1.0), 0.0)
+    return jnp.stack([norm, one[1] + two[1], one[2] + two[2] + gap * gap * shared])
+
+
+def ranks(key):
+    at = jnp.arange(key.shape[-1])
+    mine, others = key[..., :, None], key[..., None, :]
+    before = (others < mine) | ((others == mine) & (at[None, :] < at[:, None]))
+    return jnp.sum(before.astype(jnp.int32), axis=-1)
+
+
+def call(kernel, out_shape, in_spaces, out_spaces, scratch, flops, bytes_accessed):
+    return pl.pallas_call(
+        kernel,
+        out_shape=out_shape,
+        in_specs=[pl.BlockSpec(memory_space=space) for space in in_spaces],
+        out_specs=jax.tree.map(lambda space: pl.BlockSpec(memory_space=space), out_spaces),
+        scratch_shapes=scratch,
+        compiler_params=pltpu.CompilerParams(vmem_limit_bytes=VMEM_LIMIT),
+        cost_estimate=pl.CostEstimate(
+            flops=flops, bytes_accessed=bytes_accessed, transcendentals=0
+        ),
+    )
+
+
+def on_device(
+    wavefunction,
+    left_sector,
+    right_sector,
+    phys_index,
+    left_environment,
+    right_environment,
+    term_weights,
+):
+    blocks, dim, _ = wavefunction.shape
+    terms, per_device = left_environment.shape[:2]
+    most = 2 * max(1, blocks // 8)
+    first_slots = blocks - most
+    index = lax.axis_index("sector")
+    z, y, c = index // 2, index % 2, lax.axis_index("term")
+    straight = y == c
+
+    def mine_of(own, swapped):
+        return jnp.where(straight, own, swapped)
+
+    left_swapped = move(left_environment, DIAGONAL)
+    left_mine = mine_of(left_environment, left_swapped)
+    left_below = move(left_mine, UP)
+    left_above = move(left_mine, DOWN)
+    right_held, _ = lax.optimization_barrier((right_environment, left_swapped))
+    right_mine = mine_of(right_environment, move(right_held, DIAGONAL))
+    left_two_below = move(left_below, UP_INNER)
+    left_two_above = move(left_above, DOWN_INNER)
+
+    info = jnp.stack([left_sector, right_sector - index * per_device, phys_index])
+    info_other = move(info, COLUMN)
+    half = blocks // 2
+    wave_half = lax.dynamic_slice_in_dim(wavefunction, c * half, half, 0)
+    wave_half = move(wave_half, COLUMN)
+    wave_sib = move(wave_half, CORE)
+    wave_other = jnp.concatenate(
+        [jnp.where(c == 0, wave_half, wave_sib), jnp.where(c == 0, wave_sib, wave_half)]
+    )
+    weights_sib = move(term_weights, CORE)
+    weights_mine = mine_of(term_weights, weights_sib)
+    right_sib = move(right_mine, CORE)
+
+    infos = jnp.stack([info, info_other, info])
+    left_device = infos[:, 0] // per_device
+    parity = jnp.stack([c, c, 1 - c])[:, None]
+    step = left_device // 2 - z
+    stage = jnp.where(
+        step == 0, 0, jnp.where(step == -1, 1, jnp.where(step == 1, 2, 3))
+    )
+    here = left_device % 2 == parity
+    guest = here & (jnp.abs(step) == 3)
+    stage = jnp.where(here & ~guest, stage, -1)
+    key = jnp.where(stage < 0, 0, jnp.where(stage == 3, 2, 1))
+    place = ranks(key)
+    guest_place = ranks(jnp.where(guest, 0, 1))
+    side = jnp.where(jnp.arange(2) == 0, y, 1 - y)
+    right_from = jnp.broadcast_to((side != c).astype(jnp.int32)[:, None], (2, blocks))
+    at = jnp.broadcast_to(jnp.arange(blocks)[None], (2, blocks))
+    fields = jnp.stack(
+        [stage[:2], at, infos[:2, 0] % per_device, right_from, infos[:2, 1], infos[:2, 2]], axis=-1
+    )
+
+    def ordered(places, count, values):
+        chosen = (jnp.arange(count)[None, :, None] == places[:, None, :]).astype(jnp.float32)
+        return jnp.einsum(
+            "rsk,rkf->rsf", chosen, values.astype(jnp.float32), precision=lax.Precision.HIGHEST
+        ).astype(jnp.int32)
+
+    table = ordered(place[:2], blocks, fields)
+    guest_fields = jnp.concatenate(
+        [jnp.where(guest[:2], 3, -1)[:, :, None], fields[:, :, 1:]], axis=-1
+    )
+    guest_table = ordered(guest_place[:2], most, guest_fields).reshape(2 * most, -1)
+    far_table = table[:, first_slots:].reshape(2 * most, -1)
+    table = table.reshape(2 * blocks, -1)
+
+    def weight_rows(tab):
+        state = (tab[:, 5][:, None] == jnp.arange(term_weights.shape[1])[None, :]).astype(
+            jnp.bfloat16
+        )
+        rows = jnp.dot(state, weights_mine.T, preferred_element_type=jnp.float32)
+        return jnp.broadcast_to(rows[:, :, None], rows.shape + (dim,)).reshape(-1, terms * dim)
+
+    ANY, VMEM, SMEM = pl.ANY, pltpu.VMEM, pltpu.SMEM
+    bf16, f32 = jnp.bfloat16, jnp.float32
+    square = (dim, dim)
+    env = (terms, per_device) + square
+    wave_guest = call(
+        pick_kernel,
+        jax.ShapeDtypeStruct((2 * most,) + square, bf16),
+        [SMEM, VMEM, VMEM],
+        VMEM,
+        [],
+        0,
+        4 * 2**20,
+    )(guest_table, wavefunction, wave_other)
+    is_outer = (z == 0) | (z == 3)
+    guest_table = jnp.where(is_outer, guest_table, -1)
+    wave_guest = move(wave_guest, GUEST)
+    guest_got = move(guest_table, GUEST)
+    right_guest = move(right_mine, GUEST)
+    right_guest_sib = move(right_guest, CORE_INNER)
+    late_table = jnp.concatenate([far_table, jnp.where(is_outer, -1, guest_got)])
+
+    own, other = call(
+        near_kernel,
+        (
+            jax.ShapeDtypeStruct((blocks,) + square, f32),
+            jax.ShapeDtypeStruct((blocks,) + square, bf16),
+        ),
+        [SMEM, VMEM] + [ANY] * 7,
+        (VMEM, VMEM),
+        [
+            pltpu.VMEM((2, blocks) + square, bf16),
+            pltpu.VMEM((2,) + env, bf16),
+            pltpu.VMEM((3,) + env, bf16),
+            pltpu.SemaphoreType.DMA((7,)),
+        ],
+        4 * 24 * terms * dim**3,
+        14 * 2**20,
+    )(
+        table, weight_rows(table), wavefunction, wave_other, right_mine, right_sib,
+        left_mine, left_below, left_above,
+    )
+    first_got = move(other[:first_slots], COLUMN)
+    first_own = own[:first_slots] + first_got.astype(f32)
+    first_sib = move(first_own, CORE)
+
+    carried = call(
+        carry_kernel,
+        jax.ShapeDtypeStruct((4 * most, dim, terms * dim), bf16),
+        [SMEM, VMEM] + [ANY] * 7,
+        VMEM,
+        [
+            pltpu.VMEM((2, blocks) + square, bf16),
+            pltpu.VMEM((2 * most,) + square, bf16),
+            pltpu.VMEM((4,) + env, bf16),
+            pltpu.SemaphoreType.DMA((7,)),
+        ],
+        2 * 16 * terms * dim**3,
+        18 * 2**20,
+    )(
+        late_table, weight_rows(late_table), wavefunction, wave_other, wave_guest,
+        right_mine, right_sib, right_guest, right_guest_sib,
+    )
+    low = (z < 2).astype(jnp.int32).reshape(1)
+    last = jax.ShapeDtypeStruct((most,) + square, f32)
+    last_sent = jax.ShapeDtypeStruct((most,) + square, bf16)
+    last_own, last_other, guest_own, guest_other = call(
+        far_kernel,
+        (last, last_sent, last, last_sent),
+        [SMEM, SMEM] + [ANY] * 3 + [VMEM] * 2,
+        (VMEM,) * 4,
+        [
+            pltpu.VMEM((4 * most, dim, terms * dim), bf16),
+            pltpu.VMEM(env, bf16),
+            pltpu.SemaphoreType.DMA((4 * most,)),
+            pltpu.SemaphoreType.DMA((1,)),
+        ],
+        2 * 16 * terms * dim**3,
+        8 * 2**20,
+    )(
+        late_table, low, carried, left_two_below, left_two_above,
+        own[first_slots:], other[first_slots:],
+    )
+    guest_full = guest_own + move(guest_other, COLUMN_INNER).astype(f32)
+    guest_home = move(guest_full.astype(bf16), GUEST_BACK)
+    last_full = last_own + move(last_other, COLUMN).astype(f32)
+    last_sib = move(last_full, CORE)
+    guest_sib = move(guest_home, CORE)
+
+    home = stage[0::2], place[0::2], guest[0::2], guest_place[0::2], here[0::2]
+
+    def source_of(which):
+        _, placed, is_guest, guest_at, _ = (value[which] for value in home)
+        code = jnp.where(is_guest, 2, jnp.where(placed < first_slots, 0, 1))
+        slot = jnp.where(is_guest, guest_at, jnp.where(placed < first_slots, placed, placed - first_slots))
+        return jnp.stack([code + 3 * which, slot], axis=-1)
+
+    sources = jnp.where(home[4][0][:, None], source_of(0), source_of(1))
+    image, sums = call(
+        gather_kernel,
+        (
+            jax.ShapeDtypeStruct((blocks,) + square, f32),
+            jax.ShapeDtypeStruct((8, 128), f32),
+        ),
+        [SMEM] + [VMEM] * 7,
+        (VMEM, VMEM),
+        [],
+        blocks * 8 * dim * dim,
+        8 * 2**20,
+    )(sources, first_own, last_full, guest_home, first_sib, last_sib, guest_sib, wavefunction)
+    totals = sums[:3]
+    for pairs in (COLUMN, NEAR, FAR):
+        totals = merged(totals, move(totals, pairs))
+    rayleigh = totals[1, :1] / totals[0, :1]
+    entries = blocks * 8 * dim * dim
+    scale = lax.rsqrt(totals[2, :1] / entries + 1e-06)
+    residual = image - rayleigh[:, None, None] * wavefunction.astype(f32)
+    return image, residual * scale[:, None, None], rayleigh
+
+
 def solution(mesh):
     placed = (
         P(("parts", "sector"), None, None),
@@ -80,8 +554,9 @@
         P(("parts", "term"), "sector", None, None),
         P(("parts", "term"), None),
     )
+    paired = mesh.shape["sector"] == 8 and mesh.shape["term"] == 2
     return jax.shard_map(
-        on_device,
+        on_device if paired else on_device_any,
         mesh=mesh,
         in_specs=placed,
         out_specs=(

time: 470 us -> 249 us (0.53)
  waiting for transfers between devices: 332 us -> 115 us
  starting transfers between devices: 5.72 us -> 76.2 us
  blocking collectives: 53.6 us -> 0 us
  Pallas kernels: 0 us -> 36.8 us
  local copies, waits for them, and re-layouts: 25.9 us -> 4.48 us
  between operations: 17.3 us -> 2.32 us
  other arithmetic: 24.7 us -> 12.8 us
  matrix products: 9.72 us -> 0.65 us
    all_to_all x1 -> x0, waiting for transfers between devices: 312 us -> none  [on_device(): lax.all_to_all(picked, 'sector', split_axis=0, concat_axis=0, tiled=True)]
    ppermute x0 -> x25, waiting for transfers between devices: none -> 115 us  [move(): return lax.ppermute(array, BOTH, pairs)]
    ppermute x0 -> x25, starting transfers between devices: none -> 76.2 us  [move(): return lax.ppermute(array, BOTH, pairs)]
    psum x2 -> x0, blocking collectives: 40 us -> none  [the longest x1 22.2 us: on_device(): norm_all, correlation_all = lax.psum((norm_wave, correlation), 'sector')]
    pallas_call x0 -> x5, Pallas kernels: none -> 36.8 us  [the longest x1 15.3 us: on_device(): call(near_kernel, (jax.ShapeDtypeStruct((blocks,) + square, f32), jax.Sha...]
    gather x3 -> x0, local copies, waits for them, and re-layouts: 22 us -> none  [the longest x1 9.69 us: on_device(): jnp.take(fetched.reshape(slot_count, left_environment.shape[0], sector_di...]
    psum x1 -> x0, waiting for transfers between devices: 20.3 us -> none  [on_device(): image = lax.psum(image_partial_result, 'term')]
    all_to_all x1 -> x0, blocking collectives: 13.6 us -> none  [on_device(): lax.all_to_all(wanted.reshape(sector_count, capacity), 'sector', split_ax...]
  transfers between devices with their start and end apart: 2 -> 25, of which waited for: 2 -> 13; matrix products, arithmetic and copies ran while one was open for 1% -> 6% of each run, Pallas kernels for 0% -> 12%
where the time goes in v1:
time: 249 us
  waiting for transfers between devices  115 us (46%)
  starting transfers between devices  76.2 us (31%)
  Pallas kernels  36.8 us (15%)
  other arithmetic  12.8 us (5%)
  local copies, waits for them, and re-layouts  4.48 us (2%)
    ppermute x25, waiting for transfers between devices, move(): return lax.ppermute(array, BOTH, pairs)  115 us
    ppermute x25, starting transfers between devices, move(): return lax.ppermute(array, BOTH, pairs)  76.2 us
    pallas_call x1, Pallas kernels, on_device(): call(near_kernel, (jax.ShapeDtypeStruct((blocks,) + square, f32), jax.Sha...  15.3 us
    pallas_call x1, Pallas kernels, on_device(): call(carry_kernel, jax.ShapeDtypeStruct((4 * most, dim, terms * dim), bf1...  8.98 us
    pallas_call x1, Pallas kernels, on_device(): call(gather_kernel, (jax.ShapeDtypeStruct((blocks,) + square, f32), jax.S...  6.41 us
  transfers between devices with their start and end apart: 25, of which 13 were waited for; matrix products, arithmetic and copies ran while one was open for 6% of the time, Pallas kernels for 12%

profile of v1, /device:TPU:0, one launch (start us, length us, event | category | flops | bytes accessed | tf_op | source)
XLA Modules:
  0.0 248.6 jit_solution(1894397473542659145)
XLA Ops:
  0.6 1.9 collective-permute-start.4
  2.5 1.9 collective-permute-start.5
  4.4 0.7 subtract_bitcast_fusion
  5.1 0.7 pad_add_fusion.1
  5.8 26.0 %collective-permute-start = (s32[3,32]{1,0:T(4,128)S(1)}, s32[3,32]{1,0:T(4,128)S(1)}, u32[]{:S(2)}, u32[]{:S(2)}) collective-permute-start(s32[3,32]{1,0:T(4,128)S(1)} %get-tuple-element.52), channel_id=1, source_target_pairs={{0,2},{1,3},{2,0},{3,1},{4,6},{5,7},{6,4},{7,5},{8,10},{9,11},{10,... | collective-permute-start | bytes 1160 | tf_op jit(solution)/shard_map/ppermute | solution.py:116
  32.0 1.1 constant_dynamic-slice_fusion
  33.1 18.7 %collective-permute-done = s32[3,32]{1,0:T(4,128)S(1)} collective-permute-done((s32[3,32]{1,0:T(4,128)S(1)}, s32[3,32]{1,0:T(4,128)S(1)}, u32[]{:S(2)}, u32[]{:S(2)}) %collective-permute-start) | collective-permute-done | bytes 416 | tf_op jit(solution)/shard_map/ppermute | solution.py:116
  51.9 1.8 broadcast_select_fusion.left_mine
  53.8 4.9 %collective-permute-start.7 = (bf16[7,8,128,128]{3,2,1,0:T(8,128)(2,1)S(1)}, bf16[7,8,128,128]{3,2,1,0:T(8,128)(2,1)}, u32[]{:S(2)}, u32[]{:S(2)}) collective-permute-start(bf16[7,8,128,128]{3,2,1,0:T(8,128)(2,1)S(1)} %broadcast_select_fusion.left_mine), channel_id=1, source_target_pairs={{0,4},{1,5},{2,6},{3,7},{4,8},{5,9},{6,10},{7,11},{8,12},{9,13},{1... | collective-permute-start | bytes 5505032 | tf_op jit(solution)/shard_map/ppermute | solution.py:116
  58.7 1.3 collective-permute-start.8
  60.0 1.4 broadcast_select_fusion.1.right_mine
  61.5 5.8 %collective-permute-start.12 = (bf16[7,8,128,128]{3,2,1,0:T(8,128)(2,1)}, bf16[7,8,128,128]{3,2,1,0:T(8,128)(2,1)}, u32[]{:S(2)}, u32[]{:S(2)}) collective-permute-start(bf16[7,8,128,128]{3,2,1,0:T(8,128)(2,1)} %broadcast_select_fusion.1.right_mine), channel_id=1, source_target_pairs={{0,4},{1,5},{2,6},{3,7},{12,8},{13,9},{14,10},{15,11},{16,20},{17,... | collective-permute-start | bytes 5505032 | tf_op jit(solution)/shard_map/ppermute | solution.py:116
  67.5 1.2 collective-permute-start.2
  68.7 0.3 convert_reduce_fusion.1
  69.4 12.6 %collective-permute-done.2 = bf16[16,128,128]{2,1,0:T(8,128)(2,1)} collective-permute-done((bf16[16,128,128]{2,1,0:T(8,128)(2,1)S(1)}, bf16[16,128,128]{2,1,0:T(8,128)(2,1)}, u32[]{:S(2)}, u32[]{:S(2)}) %collective-permute-start.2) | collective-permute-done | bytes 524320 | tf_op jit(solution)/shard_map/ppermute | solution.py:116
  82.2 0.2 fusion.1
  82.6 15.2 %collective-permute-done.7.left_below = bf16[7,8,128,128]{3,2,1,0:T(8,128)(2,1)} collective-permute-done((bf16[7,8,128,128]{3,2,1,0:T(8,128)(2,1)S(1)}, bf16[7,8,128,128]{3,2,1,0:T(8,128)(2,1)}, u32[]{:S(2)}, u32[]{:S(2)}) %collective-permute-start.7) | collective-permute-done | bytes 1835040 | tf_op jit(solution)/shard_map/ppermute | solution.py:116
  97.8 2.0 collective-permute-start.14
  99.8 1.7 collective-permute-done.8.left_above
  101.5 1.3 collective-permute-start.15
  102.8 32.6 %collective-permute-done.12.guest_mine = bf16[7,8,128,128]{3,2,1,0:T(8,128)(2,1)} collective-permute-done((bf16[7,8,128,128]{3,2,1,0:T(8,128)(2,1)}, bf16[7,8,128,128]{3,2,1,0:T(8,128)(2,1)}, u32[]{:S(2)}, u32[]{:S(2)}) %collective-permute-start.12) | collective-permute-done | bytes 1835040 | tf_op jit(solution)/shard_map/ppermute | solution.py:116
  135.4 1.9 collective-permute-start.13
  137.3 1.3 broadcast_select_fusion.3
  138.7 15.3 %shard_map.94 = (f32[32,128,128]{2,1,0:T(8,128)}, bf16[32,128,128]{2,1,0:T(8,128)(2,1)S(1)}) custom-call(s32[64,6]{1,0:T(8,128)S(1)} %bitcast.98, f32[64,896]{1,0:T(8,128)S(1)} %bitcast.95, bf16[32,128,128]{2,1,0:T(8,128)(2,1)S(1)} %copy-done, bf16[32,128,128]{2,1,0:T(8,128)(2,1)S(1)} %pad_maximum_fusion.wave_other.second, ...), custom_call_target="tpu_custom_call" | custom-call | flops 1409286144 | bytes 14680064 | tf_op jit(solution)/shard_map/pallas_call | solution.py:449
  154.0 1.0 slice.169
  154.9 0.3 collective-permute-start.9
  155.4 9.3 %collective-permute-start.10 = (s32[16,6]{0,1:T(8,128)S(1)}, s32[16,6]{0,1:T(8,128)S(1)}, u32[]{:S(2)}, u32[]{:S(2)}) collective-permute-start(s32[16,6]{0,1:T(8,128)S(1)} %broadcast_select_fusion.6), channel_id=1, source_target_pairs={{0,4},{1,5},{2,6},{3,7},{12,8},{13,9},{14,10},{15,11},{16,20},{17,... | collective-permute-start | bytes 1160 | tf_op jit(solution)/shard_map/ppermute | solution.py:116
  165.0 1.1 collective-permute-done.10
  166.1 1.5 shard_map.95
  167.7 5.0 %collective-permute-start.11 = (bf16[16,128,128]{2,1,0:T(8,128)(2,1)}, bf16[16,128,128]{2,1,0:T(8,128)(2,1)}, u32[]{:S(2)}, u32[]{:S(2)}) collective-permute-start(bf16[16,128,128]{2,1,0:T(8,128)(2,1)} %shard_map.95), channel_id=1, source_target_pairs={{0,4},{1,5},{2,6},{3,7},{12,8},{13,9},{14,10},{15,11},{16,20},{17,... | collective-permute-start | bytes 1572872 | tf_op jit(solution)/shard_map/ppermute | solution.py:116
  172.6 2.5 %convert_add_fusion.first_own = f32[24,128,128]{2,1,0:T(8,128)} fusion(bf16[24,128,128]{2,1,0:T(8,128)(2,1)} %collective-permute-done.9, f32[32,128,128]{2,1,0:T(8,128)S(1)} %copy-done.2), kind=kLoop, calls=%fused_computation.3 | loop fusion | flops 786432 | bytes 3932160 | tf_op jit(solution)/shard_map/add | solution.py:470
  175.6 1.1 slice.174.own
  176.7 2.1 collective-permute-done.11.wave_guest
  178.8 9.0 %shard_map.96.carried = bf16[32,128,896]{2,1,0:T(8,128)(2,1)} custom-call(s32[32,6]{1,0:T(8,128)S(1)} %copy.105.table, f32[32,896]{1,0:T(8,128)S(1)} %bitcast.96, bf16[32,128,128]{2,1,0:T(8,128)(2,1)S(1)} %copy-done, bf16[32,128,128]{2,1,0:T(8,128)(2,1)S(1)} %pad_maximum_fusion.wave_other.second, bf16[16,128,128]{2,1,0:T(8,128)(2,1)} %collective-permute-done.11.wave_guest, ...), custom_call_target="tpu_custom_call" | custom-call | flops 469762048 | bytes 18874368 | tf_op jit(solution)/shard_map/pallas_call | solution.py:473
  187.8 4.6 %shard_map.97 = (f32[8,128,128]{2,1,0:T(8,128)S(1)}, bf16[8,128,128]{2,1,0:T(8,128)(2,1)S(1)}, f32[8,128,128]{2,1,0:T(8,128)S(1)}, bf16[8,128,128]{2,1,0:T(8,128)(2,1)S(1)}) custom-call(s32[32,6]{1,0:T(8,128)S(1)} %copy.105.table, s32[1]{0:T(128)} %bitcast.30.low, bf16[32,128,896]{2,1,0:T(8,128)(2,1)} %shard_map.96.carried, ...), custom_call_target="tpu_custom_call" | custom-call | flops 469762048 | bytes 8388608 | tf_op jit(solution)/shard_map/pallas_call | solution.py:493
  192.4 0.7 collective-permute-start.17
  193.2 0.5 collective-permute-start.16
  193.8 1.3 collective-permute-start.18
  195.1 4.5 %collective-permute-done.16 = bf16[8,128,128]{2,1,0:T(8,128)(2,1)S(1)} collective-permute-done((bf16[8,128,128]{2,1,0:T(8,128)(2,1)S(1)}, bf16[8,128,128]{2,1,0:T(8,128)(2,1)S(1)}, u32[]{:S(2)}, u32[]{:S(2)}) %collective-permute-start.16) | collective-permute-done | bytes 262176 | tf_op jit(solution)/shard_map/ppermute | solution.py:116
  199.7 17.9 %collective-permute-done.18.guest_own = bf16[8,128,128]{2,1,0:T(8,128)(2,1)S(1)} collective-permute-done((bf16[8,128,128]{2,1,0:T(8,128)(2,1)S(1)}, bf16[8,128,128]{2,1,0:T(8,128)(2,1)S(1)}, u32[]{:S(2)}, u32[]{:S(2)}) %collective-permute-start.18) | collective-permute-done | bytes 262176 | tf_op jit(solution)/shard_map/ppermute | solution.py:116
  217.9 1.3 collective-permute-done.21.guest_sib
  219.2 6.4 %shard_map.98 = (f32[32,128,128]{2,1,0:T(8,128)}, f32[8,128]{1,0:T(8,128)S(1)}) custom-call(s32[32,2]{1,0:T(8,128)S(1)} %broadcast_select_fusion.4.table, f32[24,128,128]{2,1,0:T(8,128)} %convert_add_fusion.first_own, f32[8,128,128]{2,1,0:T(8,128)S(1)} %convert_add_fusion.1.last_own, bf16[8,128,128]{2,1,0:T(8,128)(2,1)S(1)} %collective-permute-done.18.guest_own, ...), custom_call_target="tpu_custom_call" | custom-call | flops 4194304 | bytes 8388608 | tf_op jit(solution)/shard_map/pallas_call | solution.py:525
  225.6 1.0 collective-permute-start.22
  226.6 2.5 %collective-permute-done.22 = f32[3,128]{1,0:T(4,128)S(1)} collective-permute-done((f32[3,128]{1,0:T(4,128)S(1)}, f32[3,128]{1,0:T(4,128)S(1)}, u32[]{:S(2)}, u32[]{:S(2)}) %collective-permute-start.22) | collective-permute-done | bytes 1568 | tf_op jit(solution)/shard_map/ppermute | solution.py:116
  229.3 3.6 %collective-permute-done.23 = f32[3,128]{1,0:T(4,128)S(1)} collective-permute-done((f32[3,128]{1,0:T(4,128)S(1)}, f32[3,128]{1,0:T(4,128)S(1)}, u32[]{:S(2)}, u32[]{:S(2)}) %collective-permute-start.23) | collective-permute-done | bytes 1568 | tf_op jit(solution)/shard_map/ppermute | solution.py:116
  232.9 9.5 %collective-permute-start.24 = (f32[3,128]{1,0:T(4,128)S(1)}, f32[3,128]{1,0:T(4,128)S(1)}, u32[]{:S(2)}, u32[]{:S(2)}) collective-permute-start(f32[3,128]{1,0:T(4,128)S(1)} %pad_maximum_fusion.2), channel_id=1, source_target_pairs={{0,8},{1,9},{2,10},{3,11},{4,12},{5,13},{6,14},{7,15},{8,0},{9,1},... | collective-permute-start | bytes 4616 | tf_op jit(solution)/shard_map/ppermute | solution.py:116
  242.4 1.6 collective-permute-done.24
  244.1 3.3 %subtract_multiply_fusion = f32[32,128,128]{2,1,0:T(8,128)} fusion(f32[32,128,128]{2,1,0:T(8,128)} %get-tuple-element.9, bf16[32,128,128]{2,1,0:T(8,128)(2,1)S(1)} %copy-done, f32[]{:T(128)} %bitcast.33, f32[]{:T(128)} %bitcast.32), kind=kLoop, calls=%fused_computation | loop fusion | flops 2097152 | bytes 5242888 | tf_op jit(solution)/shard_map/mul | solution.py:544
  (88 shorter events, 3.1 us)
Async XLA Ops:
  0.6 1.9 collective-permute-start.4
  2.5 57.5 %collective-permute-start.5 = (bf16[7,8,128,128]{3,2,1,0:T(8,128)(2,1)}, bf16[7,8,128,128]{3,2,1,0:T(8,128)(2,1)}, u32[]{:S(2)}, u32[]{:S(2)}) collective-permute-start(bf16[7,8,128,128]{3,2,1,0:T(8,128)(2,1)} %param.12), channel_id=1, source_target_pairs={{1,2},{2,1},{5,6},{6,5},{9,10},{10,9},{13,14},{14,13},{17,18},{18,... | collective-permute-start | bytes 5505032 | tf_op jit(solution)/shard_map/ppermute | solution.py:116
  5.8 46.1 %collective-permute-start = (s32[3,32]{1,0:T(4,128)S(1)}, s32[3,32]{1,0:T(4,128)S(1)}, u32[]{:S(2)}, u32[]{:S(2)}) collective-permute-start(s32[3,32]{1,0:T(4,128)S(1)} %get-tuple-element.52), channel_id=1, source_target_pairs={{0,2},{1,3},{2,0},{3,1},{4,6},{5,7},{6,4},{7,5},{8,10},{9,11},{10,... | collective-permute-start | bytes 1160 | tf_op jit(solution)/shard_map/ppermute | solution.py:116
  31.8 35.7 %collective-permute-start.1 = (bf16[7,16]{1,0:T(8,128)(2,1)}, bf16[7,16]{1,0:T(8,128)(2,1)S(1)}, u32[]{:S(2)}, u32[]{:S(2)}) collective-permute-start(bf16[7,16]{1,0:T(8,128)(2,1)} %param.13), channel_id=1, source_target_pairs={{0,1},{1,0},{2,3},{3,2},{4,5},{5,4},{6,7},{7,6},{8,9},{9,8},{10,11... | collective-permute-start | bytes 680 | tf_op jit(solution)/shard_map/ppermute | solution.py:116
  51.9 8.1 %copy-start.3 = (bf16[7,8,128,128]{3,2,1,0:T(8,128)(2,1)S(1)}, bf16[7,8,128,128]{3,2,1,0:T(8,128)(2,1)}, u32[]{:S(2)}) copy-start(bf16[7,8,128,128]{3,2,1,0:T(8,128)(2,1)} %param.12) | copy-start | bytes 5505028
  53.7 7.7 %copy-start.1 = (bf16[7,8,128,128]{3,2,1,0:T(8,128)(2,1)}, bf16[7,8,128,128]{3,2,1,0:T(8,128)(2,1)S(1)}, u32[]{:S(2)}) copy-start(bf16[7,8,128,128]{3,2,1,0:T(8,128)(2,1)S(1)} %broadcast_select_fusion.left_mine) | copy-start | bytes 5505028
  53.7 28.4 %copy-start.4 = (bf16[7,16]{1,0:T(8,128)(2,1)S(1)}, bf16[7,16]{1,0:T(8,128)(2,1)}, u32[]{:S(2)}) copy-start(bf16[7,16]{1,0:T(8,128)(2,1)} %param.13) | copy-start | bytes 676
  53.8 44.1 %collective-permute-start.7 = (bf16[7,8,128,128]{3,2,1,0:T(8,128)(2,1)S(1)}, bf16[7,8,128,128]{3,2,1,0:T(8,128)(2,1)}, u32[]{:S(2)}, u32[]{:S(2)}) collective-permute-start(bf16[7,8,128,128]{3,2,1,0:T(8,128)(2,1)S(1)} %broadcast_select_fusion.left_mine), channel_id=1, source_target_pairs={{0,4},{1,5},{2,6},{3,7},{4,8},{5,9},{6,10},{7,11},{8,12},{9,13},{1... | collective-permute-start | bytes 5505032 | tf_op jit(solution)/shard_map/ppermute | solution.py:116
  58.7 42.8 %collective-permute-start.8 = (bf16[7,8,128,128]{3,2,1,0:T(8,128)(2,1)S(1)}, bf16[7,8,128,128]{3,2,1,0:T(8,128)(2,1)}, u32[]{:S(2)}, u32[]{:S(2)}) collective-permute-start(bf16[7,8,128,128]{3,2,1,0:T(8,128)(2,1)S(1)} %broadcast_select_fusion.left_mine), channel_id=1, source_target_pairs={{4,0},{5,1},{6,2},{7,3},{8,4},{9,5},{10,6},{11,7},{12,8},{13,9},{1... | collective-permute-start | bytes 5505032 | tf_op jit(solution)/shard_map/ppermute | solution.py:116
  61.5 73.9 %collective-permute-start.12 = (bf16[7,8,128,128]{3,2,1,0:T(8,128)(2,1)}, bf16[7,8,128,128]{3,2,1,0:T(8,128)(2,1)}, u32[]{:S(2)}, u32[]{:S(2)}) collective-permute-start(bf16[7,8,128,128]{3,2,1,0:T(8,128)(2,1)} %broadcast_select_fusion.1.right_mine), channel_id=1, source_target_pairs={{0,4},{1,5},{2,6},{3,7},{12,8},{13,9},{14,10},{15,11},{16,20},{17,... | collective-permute-start | bytes 5505032 | tf_op jit(solution)/shard_map/ppermute | solution.py:116
  67.3 71.3 %collective-permute-start.6 = (bf16[7,8,128,128]{3,2,1,0:T(8,128)(2,1)}, bf16[7,8,128,128]{3,2,1,0:T(8,128)(2,1)}, u32[]{:S(2)}, u32[]{:S(2)}) collective-permute-start(bf16[7,8,128,128]{3,2,1,0:T(8,128)(2,1)} %broadcast_select_fusion.1.right_mine), channel_id=1, source_target_pairs={{0,1},{1,0},{2,3},{3,2},{4,5},{5,4},{6,7},{7,6},{8,9},{9,8},{10,11... | collective-permute-start | bytes 5505032 | tf_op jit(solution)/shard_map/ppermute | solution.py:116
  67.5 14.5 %collective-permute-start.2 = (bf16[16,128,128]{2,1,0:T(8,128)(2,1)S(1)}, bf16[16,128,128]{2,1,0:T(8,128)(2,1)}, u32[]{:S(2)}, u32[]{:S(2)}) collective-permute-start(bf16[16,128,128]{2,1,0:T(8,128)(2,1)S(1)} %constant_dynamic-slice_fusion), channel_id=1, source_target_pairs={{0,2},{1,3},{2,0},{3,1},{4,6},{5,7},{6,4},{7,5},{8,10},{9,11},{10,... | collective-permute-start | bytes 1572872 | tf_op jit(solution)/shard_map/ppermute | solution.py:116
  82.0 55.3 %collective-permute-start.3 = (bf16[16,128,128]{2,1,0:T(8,128)(2,1)}, bf16[16,128,128]{2,1,0:T(8,128)(2,1)}, u32[]{:S(2)}, u32[]{:S(2)}) collective-permute-start(bf16[16,128,128]{2,1,0:T(8,128)(2,1)} %collective-permute-done.2), channel_id=1, source_target_pairs={{0,1},{1,0},{2,3},{3,2},{4,5},{5,4},{6,7},{7,6},{8,9},{9,8},{10,11... | collective-permute-start | bytes 1572872 | tf_op jit(solution)/shard_map/ppermute | solution.py:116
  82.6 56.0 %copy-start = (bf16[32,128,128]{2,1,0:T(8,128)(2,1)S(1)}, bf16[32,128,128]{2,1,0:T(8,128)(2,1)}, u32[]{:S(2)}) copy-start(bf16[32,128,128]{2,1,0:T(8,128)(2,1)} %wave.1) | copy-start | bytes 3145732
  97.8 90.0 %collective-permute-start.14 = (bf16[7,8,128,128]{3,2,1,0:T(8,128)(2,1)}, bf16[7,8,128,128]{3,2,1,0:T(8,128)(2,1)}, u32[]{:S(2)}, u32[]{:S(2)}) collective-permute-start(bf16[7,8,128,128]{3,2,1,0:T(8,128)(2,1)} %collective-permute-done.7.left_below), channel_id=1, source_target_pairs={{4,8},{5,9},{6,10},{7,11},{8,12},{9,13},{10,14},{11,15},{20,24},{2... | collective-permute-start | bytes 5505032 | tf_op jit(solution)/shard_map/ppermute | solution.py:116
  101.5 86.3 %collective-permute-start.15 = (bf16[7,8,128,128]{3,2,1,0:T(8,128)(2,1)}, bf16[7,8,128,128]{3,2,1,0:T(8,128)(2,1)}, u32[]{:S(2)}, u32[]{:S(2)}) collective-permute-start(bf16[7,8,128,128]{3,2,1,0:T(8,128)(2,1)} %collective-permute-done.8.left_above), channel_id=1, source_target_pairs={{4,0},{5,1},{6,2},{7,3},{8,4},{9,5},{10,6},{11,7},{20,16},{21,17},... | collective-permute-start | bytes 5505032 | tf_op jit(solution)/shard_map/ppermute | solution.py:116
  135.4 43.4 %collective-permute-start.13 = (bf16[7,8,128,128]{3,2,1,0:T(8,128)(2,1)}, bf16[7,8,128,128]{3,2,1,0:T(8,128)(2,1)}, u32[]{:S(2)}, u32[]{:S(2)}) collective-permute-start(bf16[7,8,128,128]{3,2,1,0:T(8,128)(2,1)} %collective-permute-done.12.guest_mine), channel_id=1, source_target_pairs={{4,5},{5,4},{6,7},{7,6},{8,9},{9,8},{10,11},{11,10},{20,21},{21,20... | collective-permute-start | bytes 5505032 | tf_op jit(solution)/shard_map/ppermute | solution.py:116
  154.9 17.7 %collective-permute-start.9 = (bf16[24,128,128]{2,1,0:T(8,128)(2,1)}, bf16[24,128,128]{2,1,0:T(8,128)(2,1)}, u32[]{:S(2)}, u32[]{:S(2)}) collective-permute-start(bf16[24,128,128]{2,1,0:T(8,128)(2,1)} %slice.169), channel_id=1, source_target_pairs={{0,2},{1,3},{2,0},{3,1},{4,6},{5,7},{6,4},{7,5},{8,10},{9,11},{10,... | collective-permute-start | bytes 2359304 | tf_op jit(solution)/shard_map/ppermute | solution.py:116
  155.4 10.6 %collective-permute-start.10 = (s32[16,6]{0,1:T(8,128)S(1)}, s32[16,6]{0,1:T(8,128)S(1)}, u32[]{:S(2)}, u32[]{:S(2)}) collective-permute-start(s32[16,6]{0,1:T(8,128)S(1)} %broadcast_select_fusion.6), channel_id=1, source_target_pairs={{0,4},{1,5},{2,6},{3,7},{12,8},{13,9},{14,10},{15,11},{16,20},{17,... | collective-permute-start | bytes 1160 | tf_op jit(solution)/shard_map/ppermute | solution.py:116
  165.0 7.7 %copy-start.2 = (f32[32,128,128]{2,1,0:T(8,128)S(1)}, f32[32,128,128]{2,1,0:T(8,128)}, u32[]{:S(2)}) copy-start(f32[32,128,128]{2,1,0:T(8,128)} %get-tuple-element.13) | copy-start | bytes 6291460
  167.7 11.2 %collective-permute-start.11 = (bf16[16,128,128]{2,1,0:T(8,128)(2,1)}, bf16[16,128,128]{2,1,0:T(8,128)(2,1)}, u32[]{:S(2)}, u32[]{:S(2)}) collective-permute-start(bf16[16,128,128]{2,1,0:T(8,128)(2,1)} %shard_map.95), channel_id=1, source_target_pairs={{0,4},{1,5},{2,6},{3,7},{12,8},{13,9},{14,10},{15,11},{16,20},{17,... | collective-permute-start | bytes 1572872 | tf_op jit(solution)/shard_map/ppermute | solution.py:116
  175.2 42.7 %collective-permute-start.19 = (f32[24,128,128]{2,1,0:T(8,128)}, f32[24,128,128]{2,1,0:T(8,128)}, u32[]{:S(2)}, u32[]{:S(2)}) collective-permute-start(f32[24,128,128]{2,1,0:T(8,128)} %convert_add_fusion.first_own), channel_id=1, source_target_pairs={{0,1},{1,0},{2,3},{3,2},{4,5},{5,4},{6,7},{7,6},{8,9},{9,8},{10,11... | collective-permute-start | bytes 4718600 | tf_op jit(solution)/shard_map/ppermute | solution.py:116
  192.4 1.3 collective-permute-start.17
  193.2 6.4 %collective-permute-start.16 = (bf16[8,128,128]{2,1,0:T(8,128)(2,1)S(1)}, bf16[8,128,128]{2,1,0:T(8,128)(2,1)S(1)}, u32[]{:S(2)}, u32[]{:S(2)}) collective-permute-start(bf16[8,128,128]{2,1,0:T(8,128)(2,1)S(1)} %get-tuple-element.16), channel_id=1, source_target_pairs={{0,2},{1,3},{2,0},{3,1},{4,6},{5,7},{6,4},{7,5},{8,10},{9,11},{10,... | collective-permute-start | bytes 786440 | tf_op jit(solution)/shard_map/ppermute | solution.py:116
  193.8 23.8 %collective-permute-start.18 = (bf16[8,128,128]{2,1,0:T(8,128)(2,1)S(1)}, bf16[8,128,128]{2,1,0:T(8,128)(2,1)S(1)}, u32[]{:S(2)}, u32[]{:S(2)}) collective-permute-start(bf16[8,128,128]{2,1,0:T(8,128)(2,1)S(1)} %add_convert_fusion), channel_id=1, source_target_pairs={{4,0},{5,1},{6,2},{7,3},{8,12},{9,13},{10,14},{11,15},{20,16},{21,... | collective-permute-start | bytes 786440 | tf_op jit(solution)/shard_map/ppermute | solution.py:116
  199.6 19.5 %collective-permute-start.20 = (f32[8,128,128]{2,1,0:T(8,128)S(1)}, f32[8,128,128]{2,1,0:T(8,128)S(1)}, u32[]{:S(2)}, u32[]{:S(2)}) collective-permute-start(f32[8,128,128]{2,1,0:T(8,128)S(1)} %convert_add_fusion.1.last_own), channel_id=1, source_target_pairs={{0,1},{1,0},{2,3},{3,2},{4,5},{5,4},{6,7},{7,6},{8,9},{9,8},{10,11... | collective-permute-start | bytes 1572872 | tf_op jit(solution)/shard_map/ppermute | solution.py:116
  217.6 1.5 collective-permute-start.21
  225.6 3.6 %collective-permute-start.22 = (f32[3,128]{1,0:T(4,128)S(1)}, f32[3,128]{1,0:T(4,128)S(1)}, u32[]{:S(2)}, u32[]{:S(2)}) collective-permute-start(f32[3,128]{1,0:T(4,128)S(1)} %slice.177), channel_id=1, source_target_pairs={{0,2},{1,3},{2,0},{3,1},{4,6},{5,7},{6,4},{7,5},{8,10},{9,11},{10,... | collective-permute-start | bytes 4616 | tf_op jit(solution)/shard_map/ppermute | solution.py:116
  229.2 3.7 %collective-permute-start.23 = (f32[3,128]{1,0:T(4,128)S(1)}, f32[3,128]{1,0:T(4,128)S(1)}, u32[]{:S(2)}, u32[]{:S(2)}) collective-permute-start(f32[3,128]{1,0:T(4,128)S(1)} %pad_maximum_fusion.1), channel_id=1, source_target_pairs={{0,4},{1,5},{2,6},{3,7},{4,0},{5,1},{6,2},{7,3},{8,12},{9,13},{10,... | collective-permute-start | bytes 4616 | tf_op jit(solution)/shard_map/ppermute | solution.py:116
  232.9 11.1 %collective-permute-start.24 = (f32[3,128]{1,0:T(4,128)S(1)}, f32[3,128]{1,0:T(4,128)S(1)}, u32[]{:S(2)}, u32[]{:S(2)}) collective-permute-start(f32[3,128]{1,0:T(4,128)S(1)} %pad_maximum_fusion.2), channel_id=1, source_target_pairs={{0,8},{1,9},{2,10},{3,11},{4,12},{5,13},{6,14},{7,15},{8,0},{9,1},... | collective-permute-start | bytes 4616 | tf_op jit(solution)/shard_map/ppermute | solution.py:116

commit v2 on v0

--- a/solution.py
+++ b/solution.py
@@ -1,10 +1,17 @@
+import functools
+
 import jax
 import jax.numpy as jnp
 from jax import lax
+from jax.experimental import pallas as pl
+from jax.experimental.pallas import tpu as pltpu
 from jax.sharding import PartitionSpec as P
 
-
-def on_device(
+BOTH = ("sector", "term")
+VMEM_LIMIT = 48 * 2**20
+
+
+def on_device_any(
     wavefunction,
     left_sector,
     right_sector,
@@ -70,6 +77,665 @@
     return (image, correction, jnp.reshape(rayleigh, (1,)))
 
 
+def pairs_of(target, chosen=lambda z, y, c: True):
+    found = []
+    for z in range(4):
+        for y in range(2):
+            for c in range(2):
+                if chosen(z, y, c):
+                    to = target(z, y, c)
+                    if 0 <= to[0] < 4:
+                        found.append(((z * 2 + y) * 2 + c, (to[0] * 2 + to[1]) * 2 + to[2]))
+    return found
+
+
+def inner(z, y, c):
+    return z in (1, 2)
+
+
+def outer(z, y, c):
+    return z in (0, 3)
+
+
+def straight(z, y, c):
+    return y == c
+
+
+def crossed(z, y, c):
+    return y != c
+
+
+def both(one, two):
+    return lambda z, y, c: one(z, y, c) and two(z, y, c)
+
+
+def up(z, y, c):
+    return z + 1, y, c
+
+
+def down(z, y, c):
+    return z - 1, y, c
+
+
+def other_core(z, y, c):
+    return z, y, 1 - c
+
+
+def other_column(z, y, c):
+    return z, 1 - y, c
+
+
+def inward(z, y, c):
+    return (1 if z == 0 else 2), y, c
+
+
+def outward(z, y, c):
+    return (0 if z == 1 else 3), y, c
+
+
+def outward_crossed(z, y, c):
+    return (0 if z == 1 else 3), 1 - y, c
+
+
+DIAGONAL = pairs_of(lambda z, y, c: (z, 1 - y, 1 - c), crossed)
+CORE = pairs_of(other_core)
+COLUMN = pairs_of(other_column)
+COLUMN_INNER = pairs_of(other_column, inner)
+GUEST = pairs_of(inward, outer)
+GUEST_BACK = pairs_of(outward, inner)
+GUEST_BACK_CROSSED = pairs_of(outward_crossed, inner)
+
+
+def move(array, pairs):
+    return lax.ppermute(array, BOTH, pairs)
+
+
+def carried_of(wave, right, weights):
+    terms, dim, _ = right.shape
+    product = lax.dot_general(
+        wave,
+        right.reshape(terms * dim, dim),
+        (((1,), (1,)), ((), ())),
+        preferred_element_type=jnp.float32,
+    )
+    return (product * weights).astype(jnp.bfloat16)
+
+
+def applied(left, carried):
+    terms, dim, _ = left.shape
+    lefts = jnp.concatenate([left[t] for t in range(terms)], axis=1)
+    stacked = jnp.concatenate(
+        [carried[:, t * dim : (t + 1) * dim] for t in range(terms)], axis=0
+    )
+    return jnp.dot(lefts, stacked, preferred_element_type=jnp.float32)
+
+
+def choose(flag, one, two, target, sem):
+    @pl.when(flag)
+    def _():
+        pltpu.make_async_copy(one, target, sem).start()
+
+    @pl.when(jnp.logical_not(flag))
+    def _():
+        pltpu.make_async_copy(two, target, sem).start()
+
+
+def grouped(low, high, step, body):
+    @pl.loop(0, (high - low + step - 1) // step)
+    def _(group):
+        for n in range(step):
+            body(jnp.minimum(low + group * step + n, high - 1))
+
+
+def count_of(table, base, rows, stage):
+    def add(row, total):
+        return total + (table[base + row, 0] == stage).astype(jnp.int32)
+
+    return lax.fori_loop(0, rows, add, jnp.int32(0))
+
+
+def near_kernel(
+    table, weights, wave_in, right_mine, right_sib, left_mine, below, above,
+    first, last, carried_out,
+    result, carried, wave, right, left, sems, carried_sems,
+):
+    blocks = wave.shape[0]
+    most = last.shape[0]
+    first_slots = blocks - most
+    copies = [
+        pltpu.make_async_copy(source, target, sems.at[n])
+        for n, (source, target) in enumerate(
+            (
+                (wave_in, wave),
+                (right_mine, right.at[0]),
+                (right_sib, right.at[1]),
+                (left_mine, left.at[0]),
+                (below, left.at[1]),
+                (above, left.at[2]),
+            )
+        )
+    ]
+    for copy in copies:
+        copy.start()
+    result[...] = jnp.zeros_like(result)
+    skipped = count_of(table, 0, blocks, -1)
+    end = blocks - count_of(table, 0, blocks, 3)
+    for copy in copies[:3]:
+        copy.wait()
+
+    def carry(slot):
+        return carried_of(
+            wave[table[slot, 1]], right[table[slot, 3], :, table[slot, 4]], weights[pl.ds(table[slot, 5], 1), :]
+        )
+
+    def written(slot):
+        at = slot - first_slots
+        return pltpu.make_async_copy(carried.at[at], carried_out.at[at], carried_sems.at[at])
+
+    def keep(slot):
+        carried[slot - first_slots] = carry(slot)
+
+    grouped(end, blocks, 4, keep)
+
+    @pl.loop(end, blocks)
+    def _(slot):
+        written(slot).start()
+
+    for copy in copies[3:]:
+        copy.wait()
+
+    def apply(slot):
+        found = applied(left[table[slot, 0], :, table[slot, 2]], carry(slot))
+        result[slot] = found.astype(result.dtype)
+
+    grouped(skipped, end, 4, apply)
+    out = pltpu.make_async_copy(result.at[pl.ds(0, first_slots)], first, sems.at[len(copies)])
+    out.start()
+    last[...] = result[first_slots:]
+    out.wait()
+
+    @pl.loop(end, blocks)
+    def _(slot):
+        written(slot).wait()
+
+
+def sum_kernel(one, two, out):
+    out[...] = one[...].astype(out.dtype) + two[...].astype(out.dtype)
+
+
+def far_kernel(
+    flags, table, guest_table, weights, carried_own, carried_other, below, above, own, other,
+    wave_own, wave_other, right_mine, right_sib,
+    own_out, other_out, guest_own_out, guest_other_out,
+    held, held_guest, wave, right, left, sems, guest_sems, wave_sems, left_sem,
+):
+    rows = held.shape[0]
+    half = rows // 2
+    for relation, source in enumerate((wave_own, wave_other)):
+        pltpu.make_async_copy(
+            source.at[pl.ds(0, half)], wave.at[pl.ds(relation * half, half)], wave_sems.at[relation]
+        ).start()
+
+    @pl.loop(0, rows)
+    def _(row):
+        @pl.when(guest_table[row, 0] == 3)
+        def _():
+            sector = guest_table[row, 4]
+            choose(
+                flags[1 + row // half] == 0, right_mine.at[:, sector], right_sib.at[:, sector],
+                right.at[row], guest_sems.at[row],
+            )
+
+    choose(flags[0] == 1, above, below, left, left_sem.at[0])
+
+    @pl.loop(0, half)
+    def _(slot):
+        for part, carried in enumerate((carried_own, carried_other)):
+            row = part * half + slot
+
+            @pl.when(table[row, 0] == 3)
+            def _():
+                pltpu.make_async_copy(carried.at[slot], held.at[row], sems.at[row]).start()
+
+    own_out[...] = own[...]
+    other_out[...] = other[...]
+    guest_own_out[...] = jnp.zeros_like(guest_own_out)
+    guest_other_out[...] = jnp.zeros_like(guest_other_out)
+    for relation, source in enumerate((wave_own, wave_other)):
+        pltpu.make_async_copy(
+            source.at[pl.ds(0, half)], wave.at[pl.ds(relation * half, half)], wave_sems.at[relation]
+        ).wait()
+
+    @pl.loop(0, rows)
+    def _(row):
+        @pl.when(guest_table[row, 0] == 3)
+        def _():
+            pltpu.make_async_copy(right_mine.at[:, 0], right.at[row], guest_sems.at[row]).wait()
+
+    def carry(row):
+        held_guest[row] = carried_of(
+            wave[row], right[row], weights[pl.ds(guest_table[row, 5], 1), :]
+        )
+
+    counts = [count_of(guest_table, part * half, half, 3) for part in range(2)]
+    for part in range(2):
+        grouped(part * half, part * half + counts[part], 4, carry)
+    pltpu.make_async_copy(above, left, left_sem.at[0]).wait()
+    for part, target in enumerate((guest_own_out, guest_other_out)):
+
+        def apply_guest(row):
+            result = applied(left[:, guest_table[row, 2]], held_guest[row])
+            target[row - part * half] = result.astype(target.dtype)
+
+        grouped(part * half, part * half + counts[part], 4, apply_guest)
+
+    @pl.loop(0, rows)
+    def _(row):
+        @pl.when(table[row, 0] == 3)
+        def _():
+            pltpu.make_async_copy(carried_own.at[0], held.at[row], sems.at[row]).wait()
+
+    for part, target in enumerate((own_out, other_out)):
+
+        def apply_own(row):
+            result = applied(left[:, table[row, 2]], held[row])
+            target[row - part * half] = result.astype(target.dtype)
+
+        high = (part + 1) * half
+        grouped(high - count_of(table, part * half, half, 3), high, 4, apply_own)
+
+
+def pick_kernel(table, own, facts, out):
+    slots = out.shape[0] - 1
+    out[slots] = facts[0]
+
+    @pl.loop(0, slots)
+    def _(slot):
+        out[slot] = own[table[slot, 1]]
+
+
+def folded(value):
+    return jnp.sum(value.reshape(-1, 8, 128), axis=0)
+
+
+def first_kernel(table, first_own, first_sib, wave, image, sums):
+    blocks = image.shape[0]
+    zero = jnp.zeros((8, 128), jnp.float32)
+    image[...] = jnp.zeros_like(image)
+
+    def place(k, totals):
+        for code, source in ((0, first_own), (3, first_sib)):
+
+            @pl.when(table[k, 0] == code)
+            def _():
+                image[k] = source[table[k, 1]]
+
+        kept = ((table[k, 0] == 0) | (table[k, 0] == 3)).astype(jnp.float32)
+        value = wave[k].astype(jnp.float32) * kept
+        return totals[0] + folded(value * value), totals[1] + folded(value * image[k])
+
+    norm_map, correlation_map = lax.fori_loop(0, blocks, place, (zero, zero), unroll=2)
+    norm = jnp.sum(norm_map, keepdims=True)
+    correlation = jnp.sum(correlation_map, keepdims=True)
+    ratio = ratio_of(norm, correlation)
+
+    def rest(k, total):
+        kept = ((table[k, 0] == 0) | (table[k, 0] == 3)).astype(jnp.float32)
+        residual = image[k] - ratio * (wave[k].astype(jnp.float32) * kept)
+        return total + folded(residual * residual)
+
+    resid = jnp.sum(lax.fori_loop(0, blocks, rest, zero, unroll=2), keepdims=True)
+    sums[...] = lined(norm, correlation, resid)
+
+
+def lined(*values):
+    line = lax.broadcasted_iota(jnp.int32, (8, 128), 0)
+    result = jnp.zeros((8, 128), jnp.float32)
+    for n, value in enumerate(values):
+        result = jnp.where(line == n, value, result)
+    return result
+
+
+def last_kernel(
+    table, sums_first, last_own, guest_own, last_sib, guest_sib, wave, held,
+    image, sums, late, out_sems,
+):
+    blocks = wave.shape[0]
+    most = last_own.shape[0]
+    zero = jnp.zeros((8, 128), jnp.float32)
+    for n, source in enumerate((last_own, guest_own, last_sib, guest_sib)):
+        late[pl.ds(n * most, most)] = source[...]
+    count = count_of(table, 0, blocks, 1)
+
+    def write(n):
+        return pltpu.make_async_copy(late.at[table[n, 2]], image.at[table[n, 1]], out_sems.at[n])
+
+    def add(n, totals):
+        write(n).start()
+        value, found = wave[table[n, 1]].astype(jnp.float32), late[table[n, 2]]
+        return totals[0] + folded(value * value), totals[1] + folded(value * found)
+
+    norm_map, correlation_map = lax.fori_loop(0, count, add, (zero, zero))
+    norm = jnp.sum(norm_map, keepdims=True)
+    correlation = jnp.sum(correlation_map, keepdims=True)
+    ratio = ratio_of(norm, correlation)
+
+    def rest(n, total):
+        residual = late[table[n, 2]] - ratio * wave[table[n, 1]].astype(jnp.float32)
+        return total + folded(residual * residual)
+
+    resid = jnp.sum(lax.fori_loop(0, count, rest, zero), keepdims=True)
+    first = [sums_first[n : n + 1, 0:1] for n in range(3)]
+    sums[...] = lined(*merged(first, (norm, correlation, resid)))
+
+    @pl.loop(0, count)
+    def _(n):
+        write(n).wait()
+
+
+def correction_kernel(
+    entries, sums, near, far, across, image_in, wave_in, out, ratio, image, wave, result, sems
+):
+    chunks = sems.shape[1]
+    size = image.shape[0] // chunks
+
+    def copy(kind, source, target, n):
+        part = pl.ds(n * size, size)
+        return pltpu.make_async_copy(source.at[part], target.at[part], sems.at[kind, n])
+
+    images = [copy(0, image_in, image, n) for n in range(chunks)]
+    waves = [copy(1, wave_in, wave, n) for n in range(chunks)]
+    results = [copy(2, result, out, n) for n in range(chunks)]
+    for n in range(chunks):
+        images[n].start()
+        waves[n].start()
+
+    def total(ref):
+        return merged(*([ref[base + n : base + n + 1, 0:1] for n in range(3)] for base in (0, 8)))
+
+    whole = merged(merged(total(sums), total(near)), merged(total(far), total(across)))
+    rayleigh = whole[1] / whole[0]
+    scale = lax.rsqrt(whole[2] / entries + 1e-06)
+    ratio[...] = jnp.broadcast_to(rayleigh, (8, 128))
+    for n in range(chunks):
+        images[n].wait()
+        waves[n].wait()
+        part = pl.ds(n * size, size)
+        result[part] = (image[part] - rayleigh * wave[part].astype(jnp.float32)) * scale
+        results[n].start()
+    for n in range(chunks):
+        results[n].wait()
+
+
+def ratio_of(norm, correlation):
+    return jnp.where(norm > 0, correlation / jnp.where(norm > 0, norm, 1.0), 0.0)
+
+
+def merged(one, two):
+    low, high = jnp.minimum(one[0], two[0]), jnp.maximum(one[0], two[0])
+    norm = one[0] + two[0]
+    gap = ratio_of(one[0], one[1]) - ratio_of(two[0], two[1])
+    shared = low * jnp.where(norm > 0, high / jnp.where(norm > 0, norm, 1.0), 0.0)
+    return norm, one[1] + two[1], one[2] + two[2] + gap * gap * shared
+
+
+def ranks(key):
+    at = jnp.arange(key.shape[-1])
+    mine, others = key[..., :, None], key[..., None, :]
+    before = (others < mine) | ((others == mine) & (at[None, :] < at[:, None]))
+    return jnp.sum(before.astype(jnp.int32), axis=-1)
+
+
+def call(kernel, out_shape, in_spaces, out_spaces, scratch, flops=1, aliases={}):
+    return pl.pallas_call(
+        kernel,
+        out_shape=out_shape,
+        in_specs=[pl.BlockSpec(memory_space=space) for space in in_spaces],
+        out_specs=jax.tree.map(lambda space: pl.BlockSpec(memory_space=space), out_spaces),
+        scratch_shapes=scratch,
+        input_output_aliases=aliases,
+        compiler_params=pltpu.CompilerParams(vmem_limit_bytes=VMEM_LIMIT),
+        cost_estimate=pl.CostEstimate(
+            flops=flops, bytes_accessed=1, transcendentals=0
+        ),
+    )
+
+
+def after(array, *others):
+    return lax.optimization_barrier((array, *others))[0]
+
+
+def on_device(
+    wavefunction,
+    left_sector,
+    right_sector,
+    phys_index,
+    left_environment,
+    right_environment,
+    term_weights,
+):
+    blocks, dim, _ = wavefunction.shape
+    terms, per_device = left_environment.shape[:2]
+    most = 2 * max(1, blocks // 8)
+    first_slots = blocks - most
+    index = lax.axis_index("sector")
+    z, y, c = index // 2, index % 2, lax.axis_index("term")
+    flags = jnp.stack([z < 2, y != c, y == c]).astype(jnp.int32)
+
+    def hop(array, step, where=lambda z, y, c: True):
+        return move(array, pairs_of(step, where))
+
+    def mine_of(own, swapped):
+        return jnp.where(y == c, own, swapped)
+
+    def tiled(facts):
+        rows, columns = facts.shape
+        return jnp.pad(facts.astype(bf16), ((0, dim - rows), (0, dim - columns)))[None]
+
+    HBM, VMEM, SMEM = pltpu.HBM, pltpu.VMEM, pltpu.SMEM
+    bf16, f32 = jnp.bfloat16, jnp.float32
+    square = (dim, dim)
+    env = (terms, per_device) + square
+    info = jnp.stack([left_sector, right_sector - index * per_device, phys_index])
+    parity = jnp.stack([c, c, 1 - c])[:, None]
+    side = jnp.where(jnp.arange(2) == 0, y, 1 - y)
+
+    def sorted_out(infos, count):
+        left_device = infos[:, 0] // per_device
+        step = left_device // 2 - z
+        stage = jnp.where(step == 0, 0, jnp.where(step == -1, 1, jnp.where(step == 1, 2, 3)))
+        here = left_device % 2 == parity[:count]
+        guest = here & (jnp.abs(step) == 3)
+        stage = jnp.where(here & ~guest, stage, -1)
+        place = ranks(jnp.where(stage < 0, 0, jnp.where(stage == 3, 2, 1)))
+        return here, guest, stage, place
+
+    def ordered(places, rows, fields):
+        chosen = (jnp.arange(rows)[None, :, None] == places[:, None, :]).astype(f32)
+        values = jnp.stack(fields, axis=-1).astype(f32)
+        return jnp.einsum("rsk,rkf->rsf", chosen, values, precision=lax.Precision.HIGHEST).astype(
+            jnp.int32
+        )
+
+    weights_sib = move(term_weights, CORE)
+    left_n = move(left_environment, DIAGONAL)
+    left_n, weights_sib = lax.optimization_barrier((left_n, weights_sib))
+    weights = mine_of(term_weights, weights_sib).astype(f32).T
+    weights = jnp.broadcast_to(weights[:, :, None], weights.shape + (dim,)).reshape(-1, terms * dim)
+    left_mine = mine_of(left_environment, left_n)
+    below = hop(left_mine, up)
+    above = hop(left_mine, down)
+
+    right_n = move(after(right_environment, left_mine), DIAGONAL)
+    right_mine = mine_of(right_environment, right_n)
+    info_other = move(after(info, left_mine), COLUMN)
+
+    block = jnp.arange(blocks)
+    _, guest, _, _ = sorted_out(info[None], 1)
+    guest_place = ranks(jnp.where(guest, 0, 1))
+    guest_fields = [jnp.where(guest, 3, -1), block[None], info[None, 0] % per_device]
+    guest_fields += [jnp.broadcast_to(side[:1, None] != c, (1, blocks)), info[None, 1], info[None, 2]]
+    guest_table = ordered(guest_place, most, guest_fields)[0]
+    picked = call(
+        pick_kernel,
+        jax.ShapeDtypeStruct((most + 1,) + square, bf16),
+        [SMEM, VMEM, VMEM],
+        VMEM,
+        [],
+    )(guest_table, wavefunction, tiled(guest_table))
+    wave_guest = move(after(picked, left_mine), GUEST)
+
+    infos = jnp.stack([info, info_other, info])
+    here, guest, stage, place = sorted_out(infos, 3)
+    guest_place = ranks(jnp.where(guest, 0, 1))
+    table = ordered(
+        place[:2],
+        blocks,
+        [
+            stage[:2],
+            jnp.broadcast_to(block, (2, blocks)),
+            infos[:2, 0] % per_device,
+            jnp.broadcast_to(side[:, None] != c, (2, blocks)),
+            infos[:2, 1],
+            infos[:2, 2],
+        ],
+    )
+    far_table = table[:, first_slots:].reshape(2 * most, -1)
+    table = table.reshape(2 * blocks, -1)
+    table = table.reshape(2, blocks, -1)
+
+    def source_of(which, of):
+        code = jnp.where(guest[of], 2, jnp.where(place[of] < first_slots, 0, 1))
+        slot = jnp.where(
+            guest[of], guest_place[of], jnp.where(place[of] < first_slots, place[of], place[of] - first_slots)
+        )
+        return jnp.stack([code + 3 * which, slot], axis=-1)
+
+    sources = jnp.where(here[0][:, None], source_of(0, 0), source_of(1, 2))
+    is_late = sources[:, 0] % 3 != 0
+    late_order = ranks(jnp.where(is_late, 0, 1)[None])
+    source_row = (sources[:, 0] - sources[:, 0] // 3 - 1) * most + sources[:, 1]
+    late_table = ordered(late_order, blocks, [is_late[None], block[None], source_row[None]])[0]
+
+    held = (below, above, right_mine, wave_guest)
+    held += (table, far_table, weights, sources, late_table)
+    held = lax.optimization_barrier(held)
+    below, above, right_mine, wave_guest = held[:4]
+    table, far_table, weights, sources, late_table = held[4:]
+    below_two = hop(below, up, inner)
+    above_two = hop(above, down, inner)
+    right_guest = hop(right_mine, inward, outer)
+    wave_other = move(after(wavefunction, right_mine), COLUMN)
+    right_sib = move(right_mine, CORE)
+    def near(relation, blocks_of, kind):
+        return call(
+            near_kernel,
+            (
+                jax.ShapeDtypeStruct((first_slots,) + square, kind),
+                jax.ShapeDtypeStruct((most,) + square, kind),
+                jax.ShapeDtypeStruct((most, dim, terms * dim), bf16),
+            ),
+            [SMEM, VMEM] + [HBM] * 6,
+            (HBM, VMEM, HBM),
+            [
+                pltpu.VMEM((blocks,) + square, kind),
+                pltpu.VMEM((most, dim, terms * dim), bf16),
+                pltpu.VMEM((blocks,) + square, bf16),
+                pltpu.VMEM((2,) + env, bf16),
+                pltpu.VMEM((3,) + env, bf16),
+                pltpu.SemaphoreType.DMA((7,)),
+                pltpu.SemaphoreType.DMA((most,)),
+            ],
+        )(
+            table[relation], weights, blocks_of, right_mine, right_sib,
+            left_mine, below, above,
+        )
+
+    own, own_last, carried_own = near(0, wavefunction, f32)
+    other, other_last, carried_other = near(1, wave_other, bf16)
+    wave_guest_other = move(after(wave_guest, own), COLUMN_INNER)
+    held = (below_two, above_two, right_guest, wave_guest_other)
+    held += (own, own_last, carried_own, other, other_last, carried_other)
+    held = lax.optimization_barrier(held)
+    below_two, above_two, right_guest, wave_guest_other = held[:4]
+    own, own_last, carried_own, other, other_last, carried_other = held[4:]
+    first_got = move(other, COLUMN)
+    right_guest_sib = hop(right_guest, other_core, inner)
+    guest_got = jnp.concatenate(
+        [guests[most, :most, :6] for guests in (wave_guest, wave_guest_other)]
+    ).astype(jnp.int32)
+
+    last = jax.ShapeDtypeStruct((most,) + square, f32)
+    last_sent = jax.ShapeDtypeStruct((most,) + square, bf16)
+    last_own, last_other, guest_own, guest_other = call(
+        far_kernel,
+        (last, last_sent, last_sent, last_sent),
+        [SMEM] * 3 + [VMEM] + [HBM] * 4 + [VMEM] * 2 + [HBM] * 4,
+        (VMEM,) * 4,
+        [
+            pltpu.VMEM((2 * most, dim, terms * dim), bf16),
+            pltpu.VMEM((2 * most, dim, terms * dim), bf16),
+            pltpu.VMEM((2 * most,) + square, bf16),
+            pltpu.VMEM((2 * most, terms) + square, bf16),
+            pltpu.VMEM(env, bf16),
+            pltpu.SemaphoreType.DMA((2 * most,)),
+            pltpu.SemaphoreType.DMA((2 * most,)),
+            pltpu.SemaphoreType.DMA((2,)),
+            pltpu.SemaphoreType.DMA((1,)),
+        ],
+    )(
+        flags, far_table, guest_got, weights, carried_own, carried_other,
+        below_two, above_two, own_last, other_last,
+        wave_guest, wave_guest_other, right_guest, right_guest_sib,
+    )
+    guest_straight = move(guest_own, GUEST_BACK)
+    guest_crossed = move(guest_other, GUEST_BACK_CROSSED)
+    last_got = move(last_other, COLUMN)
+    last_full = last_own + last_got.astype(f32)
+    first_own = own + after(first_got, last_own).astype(f32)
+    first_sib = move(first_own, CORE)
+    last_sib = move(last_full, CORE)
+    image_shape = jax.ShapeDtypeStruct((blocks,) + square, f32)
+    image, sums_first = call(
+        first_kernel,
+        (image_shape, jax.ShapeDtypeStruct((8, 128), f32)),
+        [SMEM] + [VMEM] * 3,
+        (VMEM, VMEM),
+        [],
+    )(after(sources, last_own), first_own, first_sib, wavefunction)
+    guest_full = call(sum_kernel, last, [VMEM] * 2, VMEM, [], 2**37)(
+        after(guest_straight, sums_first), guest_crossed
+    )
+    guest_sib = move(guest_full, CORE)
+
+    image, sums = call(
+        last_kernel,
+        (image_shape, jax.ShapeDtypeStruct((8, 128), f32)),
+        [SMEM] + [VMEM] * 6 + [HBM],
+        (HBM, VMEM),
+        [
+            pltpu.VMEM((4 * most,) + square, f32),
+            pltpu.SemaphoreType.DMA((blocks,)),
+        ],
+        aliases={7: 0},
+    )(late_table, sums_first, last_full, guest_full, last_sib, guest_sib, wavefunction, image)
+    sums = jnp.concatenate([sums, move(sums, COLUMN)])
+    sums = [sums] + [move(sums, pairs_of(lambda z, y, c: (z ^ n, y, c))) for n in (1, 2, 3)]
+    correction, rayleigh = call(
+        functools.partial(correction_kernel, blocks * 8 * dim * dim),
+        (image_shape, jax.ShapeDtypeStruct((8, 128), f32)),
+        [VMEM] * 4 + [HBM] * 2,
+        (HBM, VMEM),
+        [
+            pltpu.VMEM((blocks,) + square, f32),
+            pltpu.VMEM((blocks,) + square, bf16),
+            pltpu.VMEM((blocks,) + square, f32),
+            pltpu.SemaphoreType.DMA((3, 4)),
+        ],
+    )(*sums, image, wavefunction)
+    return image, correction, rayleigh[0, :1]
+
+
 def solution(mesh):
     placed = (
         P(("parts", "sector"), None, None),
@@ -80,8 +746,9 @@
         P(("parts", "term"), "sector", None, None),
         P(("parts", "term"), None),
     )
+    paired = mesh.shape["sector"] == 8 and mesh.shape["term"] == 2
     return jax.shard_map(
-        on_device,
+        on_device if paired else on_device_any,
         mesh=mesh,
         in_specs=placed,
         out_specs=(

time: 470 us -> 181 us (0.39)
  waiting for transfers between devices: 332 us -> 45.4 us
  starting transfers between devices: 5.72 us -> 75.9 us
  blocking collectives: 53.6 us -> 0 us
  Pallas kernels: 0 us -> 33.7 us
  between operations: 17.3 us -> 1.21 us
  other arithmetic: 24.7 us -> 9.08 us
  local copies, waits for them, and re-layouts: 25.9 us -> 14.5 us
  matrix products: 9.72 us -> 0.41 us
    all_to_all x1 -> x0, waiting for transfers between devices: 312 us -> none  [on_device(): lax.all_to_all(picked, 'sector', split_axis=0, concat_axis=0, tiled=True)]
    ppermute x0 -> x25, starting transfers between devices: none -> 75.9 us  [move(): return lax.ppermute(array, BOTH, pairs)]
    ppermute x0 -> x25, waiting for transfers between devices: none -> 45.4 us  [move(): return lax.ppermute(array, BOTH, pairs)]
    psum x2 -> x0, blocking collectives: 40 us -> none  [the longest x1 22.2 us: on_device(): norm_all, correlation_all = lax.psum((norm_wave, correlation), 'sector')]
    pallas_call x0 -> x8, Pallas kernels: none -> 33.7 us  [the longest x2 18.7 us: near(): call(near_kernel, (jax.ShapeDtypeStruct((first_slots,) + square, kind), j...]
    gather x3 -> x0, local copies, waits for them, and re-layouts: 22 us -> none  [the longest x1 9.69 us: on_device(): jnp.take(fetched.reshape(slot_count, left_environment.shape[0], sector_di...]
    psum x1 -> x0, waiting for transfers between devices: 20.3 us -> none  [on_device(): image = lax.psum(image_partial_result, 'term')]
    all_to_all x1 -> x0, blocking collectives: 13.6 us -> none  [on_device(): lax.all_to_all(wanted.reshape(sector_count, capacity), 'sector', split_ax...]
  transfers between devices with their start and end apart: 2 -> 25, of which waited for: 2 -> 11; matrix products, arithmetic and copies ran while one was open for 1% -> 5% of each run, Pallas kernels for 0% -> 16%
where the time goes in v2:
time: 181 us; the launch traced here: 180 us
  starting transfers between devices  75.9 us (42%)
  waiting for transfers between devices  45.4 us (25%)
  Pallas kernels  33.7 us (19%)
  local copies, waits for them, and re-layouts  14.5 us (8%)
  other arithmetic  9.08 us (5%)
    ppermute x25, starting transfers between devices, move(): return lax.ppermute(array, BOTH, pairs)  75.9 us
    ppermute x25, waiting for transfers between devices, move(): return lax.ppermute(array, BOTH, pairs)  45.4 us
    pallas_call x2, Pallas kernels, near(): call(near_kernel, (jax.ShapeDtypeStruct((first_slots,) + square, kind), j...  18.7 us
    unnamed x36, local copies, waits for them, and re-layouts  10.7 us
    pallas_call x1, Pallas kernels, on_device(): call(far_kernel, (last, last_sent, last_sent, last_sent), [SMEM] * 3 + [V...  5.24 us
    select_n x2, other arithmetic, mine_of(): return jnp.where(y == c, own, swapped)  4.91 us
    pallas_call x1, Pallas kernels, on_device(): call(first_kernel, (image_shape, jax.ShapeDtypeStruct((8, 128), f32)), [S...  4.27 us
  transfers between devices with their start and end apart: 25, of which 11 were waited for; matrix products, arithmetic and copies ran while one was open for 5% of the time, Pallas kernels for 16%

profile of v2, /device:TPU:0, one launch (start us, length us, event | category | flops | bytes accessed | tf_op | source)
XLA Modules:
  0.0 180.3 jit_solution(7705923887014197101)
XLA Ops:
  0.6 0.8 collective-permute-start
  1.4 4.3 %collective-permute-start.1 = (bf16[7,16]{1,0:T(8,128)(2,1)}, bf16[7,16]{1,0:T(8,128)(2,1)S(1)}, u32[]{:S(2)}, u32[]{:S(2)}) collective-permute-start(bf16[7,16]{1,0:T(8,128)(2,1)} %param.13), channel_id=1, source_target_pairs={{0,1},{1,0},{2,3},{3,2},{4,5},{5,4},{6,7},{7,6},{8,9},{9,8},{10,11... | collective-permute-start | bytes 680 | tf_op jit(solution)/shard_map/ppermute | solution.py:150
  5.7 0.7 subtract_bitcast_fusion
  6.4 0.7 pad_add_fusion
  7.4 0.7 stack.96
  8.5 1.2 copy-done
  10.4 3.1 %broadcast_select_fusion.1.left_mine = bf16[7,8,128,128]{3,2,1,0:T(8,128)(2,1)} fusion(bf16[7,8,128,128]{3,2,1,0:T(8,128)(2,1)} %param.11, bf16[7,8,128,128]{3,2,1,0:T(8,128)(2,1)S(1)} %collective-permute-done, pred[]{:T(512)} %eq.254), kind=kLoop, calls=%fused_computation.1 | loop fusion | flops 917504 | bytes 5505025 | tf_op jit(solution)/shard_map/jit(_where)/select_n | solution.py:529
  13.6 4.7 %collective-permute-start.2 = (bf16[7,8,128,128]{3,2,1,0:T(8,128)(2,1)}, bf16[7,8,128,128]{3,2,1,0:T(8,128)(2,1)}, u32[]{:S(2)}, u32[]{:S(2)}) collective-permute-start(bf16[7,8,128,128]{3,2,1,0:T(8,128)(2,1)} %broadcast_select_fusion.1.left_mine), channel_id=1, source_target_pairs={{0,4},{1,5},{2,6},{3,7},{4,8},{5,9},{6,10},{7,11},{8,12},{9,13},{1... | collective-permute-start | bytes 5505032 | tf_op jit(solution)/shard_map/ppermute | solution.py:150
  18.3 1.3 collective-permute-start.3
  19.6 16.5 %collective-permute-start.6 = (s32[3,32]{1,0:T(4,128)S(1)}, s32[3,32]{1,0:T(4,128)S(1)}, u32[]{:S(2)}, u32[]{:S(2)}) collective-permute-start(s32[3,32]{1,0:T(4,128)S(1)} %get-tuple-element.51), channel_id=1, source_target_pairs={{0,2},{1,3},{2,0},{3,1},{4,6},{5,7},{6,4},{7,5},{8,10},{9,11},{10,... | collective-permute-start | bytes 1160 | tf_op jit(solution)/shard_map/ppermute | solution.py:150
  36.1 1.9 %collective-permute-start.4 = (bf16[7,8,128,128]{3,2,1,0:T(8,128)(2,1)}, bf16[7,8,128,128]{3,2,1,0:T(8,128)(2,1)}, u32[]{:S(2)}, u32[]{:S(2)}) collective-permute-start(bf16[7,8,128,128]{3,2,1,0:T(8,128)(2,1)} %param.12), channel_id=1, source_target_pairs={{1,2},{2,1},{5,6},{6,5},{9,10},{10,9},{13,14},{14,13},{17,18},{18,... | collective-permute-start | bytes 5505032 | tf_op jit(solution)/shard_map/ppermute | solution.py:150
  38.0 4.6 %collective-permute-start.5 = (bf16[9,128,128]{2,1,0:T(8,128)(2,1)S(1)}, bf16[9,128,128]{2,1,0:T(8,128)(2,1)S(1)}, u32[]{:S(2)}, u32[]{:S(2)}) collective-permute-start(bf16[9,128,128]{2,1,0:T(8,128)(2,1)S(1)} %shard_map.94), channel_id=1, source_target_pairs={{0,4},{1,5},{2,6},{3,7},{12,8},{13,9},{14,10},{15,11},{16,20},{17,... | collective-permute-start | bytes 884744 | tf_op jit(solution)/shard_map/ppermute | solution.py:150
  45.1 1.8 broadcast_select_fusion.right_mine
  46.9 3.1 %collective-permute-done.5.wave_own = bf16[9,128,128]{2,1,0:T(8,128)(2,1)S(1)} collective-permute-done((bf16[9,128,128]{2,1,0:T(8,128)(2,1)S(1)}, bf16[9,128,128]{2,1,0:T(8,128)(2,1)S(1)}, u32[]{:S(2)}, u32[]{:S(2)}) %collective-permute-start.5) | collective-permute-done | bytes 294944 | tf_op jit(solution)/shard_map/ppermute | solution.py:150
  50.0 14.2 %collective-permute-start.10 = (bf16[7,8,128,128]{3,2,1,0:T(8,128)(2,1)S(1)}, bf16[7,8,128,128]{3,2,1,0:T(8,128)(2,1)S(1)}, u32[]{:S(2)}, u32[]{:S(2)}) collective-permute-start(bf16[7,8,128,128]{3,2,1,0:T(8,128)(2,1)S(1)} %broadcast_select_fusion.right_mine), channel_id=1, source_target_pairs={{0,1},{1,0},{2,3},{3,2},{4,5},{5,4},{6,7},{7,6},{8,9},{9,8},{10,11... | collective-permute-start | bytes 5505032 | tf_op jit(solution)/shard_map/ppermute | solution.py:150
  64.1 0.8 collective-permute-start.7
  64.9 1.3 collective-permute-start.8
  66.2 12.3 %collective-permute-start.9 = (bf16[7,8,128,128]{3,2,1,0:T(8,128)(2,1)S(1)}, bf16[7,8,128,128]{3,2,1,0:T(8,128)(2,1)}, u32[]{:S(2)}, u32[]{:S(2)}) collective-permute-start(bf16[7,8,128,128]{3,2,1,0:T(8,128)(2,1)S(1)} %broadcast_select_fusion.right_mine), channel_id=1, source_target_pairs={{0,4},{1,5},{2,6},{3,7},{12,8},{13,9},{14,10},{15,11},{16,20},{17,... | collective-permute-start | bytes 5505032 | tf_op jit(solution)/shard_map/ppermute | solution.py:150
  78.5 1.2 copy-done.13
  79.8 10.1 %shard_map.95 = (f32[24,128,128]{2,1,0:T(8,128)S(1)}, f32[8,128,128]{2,1,0:T(8,128)S(1)}, bf16[8,128,896]{2,1,0:T(8,128)(2,1)S(1)}) custom-call(s32[32,6]{1,0:T(8,128)S(1)} %get-tuple-element.112.table, f32[16,896]{1,0:T(8,128)S(1)} %bitcast.110, bf16[32,128,128]{2,1,0:T(8,128)(2,1)S(1)} %copy-done.1, bf16[7,8,128,128]{3,2,1,0:T(8,128)(2,1)} %copy-done.2, ...), custom_call_target="tpu_custom_call" | custom-call | flops 1 | bytes 1 | tf_op jit(solution)/shard_map/pallas_call | solution.py:631
  89.9 1.1 copy-done.6
  91.0 1.4 collective-permute-start.11
  92.4 10.6 %collective-permute-done.12.wave_in = bf16[32,128,128]{2,1,0:T(8,128)(2,1)S(1)} collective-permute-done((bf16[32,128,128]{2,1,0:T(8,128)(2,1)S(1)}, bf16[32,128,128]{2,1,0:T(8,128)(2,1)S(1)}, u32[]{:S(2)}, u32[]{:S(2)}) %collective-permute-start.12) | collective-permute-done | bytes 1048608 | tf_op jit(solution)/shard_map/ppermute | solution.py:150
  103.0 1.5 copy-done.3
  104.5 8.6 %shard_map.96 = (bf16[24,128,128]{2,1,0:T(8,128)(2,1)}, bf16[8,128,128]{2,1,0:T(8,128)(2,1)S(1)}, bf16[8,128,896]{2,1,0:T(8,128)(2,1)S(1)}) custom-call(s32[32,6]{1,0:T(8,128)S(1)} %get-tuple-element.111.table, f32[16,896]{1,0:T(8,128)S(1)} %bitcast.111, bf16[32,128,128]{2,1,0:T(8,128)(2,1)S(1)} %collective-permute-done.12.wave_in, ...), custom_call_target="tpu_custom_call" | custom-call | flops 1 | bytes 1 | tf_op jit(solution)/shard_map/pallas_call | solution.py:631
  113.1 1.2 copy-done.5
  114.3 0.7 copy-done.11
  115.6 0.9 collective-permute-done.9.right_mine
  116.4 1.9 %collective-permute-start.13 = (bf16[7,8,128,128]{3,2,1,0:T(8,128)(2,1)}, bf16[7,8,128,128]{3,2,1,0:T(8,128)(2,1)}, u32[]{:S(2)}, u32[]{:S(2)}) collective-permute-start(bf16[7,8,128,128]{3,2,1,0:T(8,128)(2,1)} %collective-permute-done.9.right_mine), channel_id=1, source_target_pairs={{4,5},{5,4},{6,7},{7,6},{8,9},{9,8},{10,11},{11,10},{20,21},{21,20... | collective-permute-start | bytes 5505032 | tf_op jit(solution)/shard_map/ppermute | solution.py:150
  118.3 2.0 %collective-permute-start.14 = (bf16[24,128,128]{2,1,0:T(8,128)(2,1)}, bf16[24,128,128]{2,1,0:T(8,128)(2,1)}, u32[]{:S(2)}, u32[]{:S(2)}) collective-permute-start(bf16[24,128,128]{2,1,0:T(8,128)(2,1)} %get-tuple-element.81), channel_id=1, source_target_pairs={{0,2},{1,3},{2,0},{3,1},{4,6},{5,7},{6,4},{7,5},{8,10},{9,11},{10,... | collective-permute-start | bytes 2359304 | tf_op jit(solution)/shard_map/ppermute | solution.py:150
  121.8 1.1 copy-done.10
  122.9 0.9 copy-done.12
  123.8 5.2 %shard_map.97 = (f32[8,128,128]{2,1,0:T(8,128)S(1)}, bf16[8,128,128]{2,1,0:T(8,128)(2,1)S(1)}, bf16[8,128,128]{2,1,0:T(8,128)(2,1)S(1)}, bf16[8,128,128]{2,1,0:T(8,128)(2,1)S(1)}) custom-call(s32[3]{0:T(128)S(1)} %add_convert_fusion.2.flags, s32[16,6]{1,0:T(8,128)S(1)} %copy.166.table, s32[16,6]{1,0:T(8,128)S(1)} %maximum_convert_fusion.guest_table, ...), custom_call_target="tpu_custom_call" | custom-call | flops 1 | bytes 1 | tf_op jit(solution)/shard_map/pallas_call | solution.py:670
  129.1 7.9 %collective-permute-done.14 = bf16[24,128,128]{2,1,0:T(8,128)(2,1)} collective-permute-done((bf16[24,128,128]{2,1,0:T(8,128)(2,1)}, bf16[24,128,128]{2,1,0:T(8,128)(2,1)}, u32[]{:S(2)}, u32[]{:S(2)}) %collective-permute-start.14) | collective-permute-done | bytes 786464 | tf_op jit(solution)/shard_map/ppermute | solution.py:150
  137.0 1.4 convert_add_fusion.first_own
  138.8 1.3 collective-permute-start.17
  140.1 1.3 collective-permute-start.18
  141.4 5.7 %collective-permute-done.16 = bf16[8,128,128]{2,1,0:T(8,128)(2,1)S(1)} collective-permute-done((bf16[8,128,128]{2,1,0:T(8,128)(2,1)S(1)}, bf16[8,128,128]{2,1,0:T(8,128)(2,1)S(1)}, u32[]{:S(2)}, u32[]{:S(2)}) %collective-permute-start.16) | collective-permute-done | bytes 262176 | tf_op jit(solution)/shard_map/ppermute | solution.py:150
  147.3 4.3 %shard_map.98 = (f32[32,128,128]{2,1,0:T(8,128)}, f32[8,128]{1,0:T(8,128)S(1)}) custom-call(s32[32,2]{1,0:T(8,128)S(1)} %add_select_fusion.7.table, f32[24,128,128]{2,1,0:T(8,128)S(1)} %convert_add_fusion.first_own, f32[24,128,128]{2,1,0:T(8,128)S(1)} %collective-permute-done.15.first_sib, bf16[32,128,128]{2,1,0:T(8,128)(2,1)S(1)} %copy-done.1), custom_call_target="tpu_custom_call" | custom-call | flops 1 | bytes 1 | tf_op jit(solution)/shard_map/pallas_call | solution.py:699
  151.5 6.2 %collective-permute-done.18.two = bf16[8,128,128]{2,1,0:T(8,128)(2,1)S(1)} collective-permute-done((bf16[8,128,128]{2,1,0:T(8,128)(2,1)S(1)}, bf16[8,128,128]{2,1,0:T(8,128)(2,1)S(1)}, u32[]{:S(2)}, u32[]{:S(2)}) %collective-permute-start.18) | collective-permute-done | bytes 262176 | tf_op jit(solution)/shard_map/ppermute | solution.py:150
  157.9 1.9 %collective-permute-done.20.guest_sib = f32[8,128,128]{2,1,0:T(8,128)S(1)} collective-permute-done((f32[8,128,128]{2,1,0:T(8,128)S(1)}, f32[8,128,128]{2,1,0:T(8,128)S(1)}, u32[]{:S(2)}, u32[]{:S(2)}) %collective-permute-start.20) | collective-permute-done | bytes 524320 | tf_op jit(solution)/shard_map/ppermute | solution.py:150
  159.8 2.9 %shard_map.100 = (f32[32,128,128]{2,1,0:T(8,128)}, f32[8,128]{1,0:T(8,128)S(1)}) custom-call(s32[32,3]{1,0:T(8,128)S(1)} %convolution_convert_fusion.1.table, f32[8,128]{1,0:T(8,128)S(1)} %get-tuple-element.83.sums_first, f32[8,128,128]{2,1,0:T(8,128)S(1)} %convert_add_fusion.1.last_own, ...), custom_call_target="tpu_custom_call", output_to_operand_aliasing={{0}: (7, {})} | custom-call | flops 1 | bytes 1 | tf_op jit(solution)/shard_map/pallas_call | solution.py:711
  163.2 3.2 %collective-permute-done.21 = f32[8,128]{1,0:T(8,128)S(1)} collective-permute-done((f32[8,128]{1,0:T(8,128)S(1)}, f32[8,128]{1,0:T(8,128)S(1)}, u32[]{:S(2)}, u32[]{:S(2)}) %collective-permute-start.21) | collective-permute-done | bytes 4128 | tf_op jit(solution)/shard_map/ppermute | solution.py:150
  166.4 4.4 %collective-permute-start.23 = (f32[16,128]{1,0:T(8,128)S(1)}, f32[16,128]{1,0:T(8,128)S(1)}, u32[]{:S(2)}, u32[]{:S(2)}) collective-permute-start(f32[16,128]{1,0:T(8,128)S(1)} %constant_dynamic-update-slice_fusion.sums), channel_id=1, source_target_pairs={{0,8},{1,9},{2,10},{3,11},{4,12},{5,13},{6,14},{7,15},{8,0},{9,1},... | collective-permute-start | bytes 24584 | tf_op jit(solution)/shard_map/ppermute | solution.py:150
  170.9 1.6 collective-permute-done.23.far
  172.5 3.8 %collective-permute-done.24.across = f32[16,128]{1,0:T(8,128)S(1)} collective-permute-done((f32[16,128]{1,0:T(8,128)S(1)}, f32[16,128]{1,0:T(8,128)S(1)}, u32[]{:S(2)}, u32[]{:S(2)}) %collective-permute-start.24) | collective-permute-done | bytes 8224 | tf_op jit(solution)/shard_map/ppermute | solution.py:150
  176.3 1.6 copy-done.4
  177.9 1.8 %shard_map.101 = (f32[32,128,128]{2,1,0:T(8,128)}, f32[8,128]{1,0:T(8,128)S(1)}) custom-call(f32[16,128]{1,0:T(8,128)S(1)} %constant_dynamic-update-slice_fusion.sums, f32[16,128]{1,0:T(8,128)S(1)} %collective-permute-done.22.near, f32[16,128]{1,0:T(8,128)S(1)} %collective-permute-done.23.far, f32[16,128]{1,0:T(8,128)S(1)} %collective-permute-done.24.across, ...), custom_call_target="tpu_custom_call" | custom-call | flops 1 | bytes 1 | tf_op jit(solution)/shard_map/pallas_call | solution.py:724
  (116 shorter events, 7.4 us)
Async XLA Ops:
  0.6 9.8 %collective-permute-start = (bf16[7,8,128,128]{3,2,1,0:T(8,128)(2,1)}, bf16[7,8,128,128]{3,2,1,0:T(8,128)(2,1)S(1)}, u32[]{:S(2)}, u32[]{:S(2)}) collective-permute-start(bf16[7,8,128,128]{3,2,1,0:T(8,128)(2,1)} %param.11), channel_id=1, source_target_pairs={{1,2},{2,1},{5,6},{6,5},{9,10},{10,9},{13,14},{14,13},{17,18},{18,... | collective-permute-start | bytes 5505032 | tf_op jit(solution)/shard_map/ppermute | solution.py:150
  1.4 9.0 %collective-permute-start.1 = (bf16[7,16]{1,0:T(8,128)(2,1)}, bf16[7,16]{1,0:T(8,128)(2,1)S(1)}, u32[]{:S(2)}, u32[]{:S(2)}) collective-permute-start(bf16[7,16]{1,0:T(8,128)(2,1)} %param.13), channel_id=1, source_target_pairs={{0,1},{1,0},{2,3},{3,2},{4,5},{5,4},{6,7},{7,6},{8,9},{9,8},{10,11... | collective-permute-start | bytes 680 | tf_op jit(solution)/shard_map/ppermute | solution.py:150
  8.5 1.2 copy-start
  10.4 32.2 %copy-start.15 = (bf16[7,16]{1,0:T(8,128)(2,1)S(1)}, bf16[7,16]{1,0:T(8,128)(2,1)}, u32[]{:S(2)}) copy-start(bf16[7,16]{1,0:T(8,128)(2,1)} %param.13) | copy-start | bytes 676
  13.6 36.4 %collective-permute-start.2 = (bf16[7,8,128,128]{3,2,1,0:T(8,128)(2,1)}, bf16[7,8,128,128]{3,2,1,0:T(8,128)(2,1)}, u32[]{:S(2)}, u32[]{:S(2)}) collective-permute-start(bf16[7,8,128,128]{3,2,1,0:T(8,128)(2,1)} %broadcast_select_fusion.1.left_mine), channel_id=1, source_target_pairs={{0,4},{1,5},{2,6},{3,7},{4,8},{5,9},{6,10},{7,11},{8,12},{9,13},{1... | collective-permute-start | bytes 5505032 | tf_op jit(solution)/shard_map/ppermute | solution.py:150
  18.3 31.7 %collective-permute-start.3 = (bf16[7,8,128,128]{3,2,1,0:T(8,128)(2,1)}, bf16[7,8,128,128]{3,2,1,0:T(8,128)(2,1)}, u32[]{:S(2)}, u32[]{:S(2)}) collective-permute-start(bf16[7,8,128,128]{3,2,1,0:T(8,128)(2,1)} %broadcast_select_fusion.1.left_mine), channel_id=1, source_target_pairs={{4,0},{5,1},{6,2},{7,3},{8,4},{9,5},{10,6},{11,7},{12,8},{13,9},{1... | collective-permute-start | bytes 5505032 | tf_op jit(solution)/shard_map/ppermute | solution.py:150
  19.6 23.2 %collective-permute-start.6 = (s32[3,32]{1,0:T(4,128)S(1)}, s32[3,32]{1,0:T(4,128)S(1)}, u32[]{:S(2)}, u32[]{:S(2)}) collective-permute-start(s32[3,32]{1,0:T(4,128)S(1)} %get-tuple-element.51), channel_id=1, source_target_pairs={{0,2},{1,3},{2,0},{3,1},{4,6},{5,7},{6,4},{7,5},{8,10},{9,11},{10,... | collective-permute-start | bytes 1160 | tf_op jit(solution)/shard_map/ppermute | solution.py:150
  36.1 9.0 %collective-permute-start.4 = (bf16[7,8,128,128]{3,2,1,0:T(8,128)(2,1)}, bf16[7,8,128,128]{3,2,1,0:T(8,128)(2,1)}, u32[]{:S(2)}, u32[]{:S(2)}) collective-permute-start(bf16[7,8,128,128]{3,2,1,0:T(8,128)(2,1)} %param.12), channel_id=1, source_target_pairs={{1,2},{2,1},{5,6},{6,5},{9,10},{10,9},{13,14},{14,13},{17,18},{18,... | collective-permute-start | bytes 5505032 | tf_op jit(solution)/shard_map/ppermute | solution.py:150
  38.0 12.0 %collective-permute-start.5 = (bf16[9,128,128]{2,1,0:T(8,128)(2,1)S(1)}, bf16[9,128,128]{2,1,0:T(8,128)(2,1)S(1)}, u32[]{:S(2)}, u32[]{:S(2)}) collective-permute-start(bf16[9,128,128]{2,1,0:T(8,128)(2,1)S(1)} %shard_map.94), channel_id=1, source_target_pairs={{0,4},{1,5},{2,6},{3,7},{12,8},{13,9},{14,10},{15,11},{16,20},{17,... | collective-permute-start | bytes 884744 | tf_op jit(solution)/shard_map/ppermute | solution.py:150
  45.1 33.4 %copy-start.1 = (bf16[32,128,128]{2,1,0:T(8,128)(2,1)S(1)}, bf16[32,128,128]{2,1,0:T(8,128)(2,1)}, u32[]{:S(2)}) copy-start(bf16[32,128,128]{2,1,0:T(8,128)(2,1)} %wave_in.3) | copy-start | bytes 3145732
  46.9 31.7 %copy-start.2 = (bf16[7,8,128,128]{3,2,1,0:T(8,128)(2,1)}, bf16[7,8,128,128]{3,2,1,0:T(8,128)(2,1)S(1)}, u32[]{:S(2)}) copy-start(bf16[7,8,128,128]{3,2,1,0:T(8,128)(2,1)S(1)} %broadcast_select_fusion.right_mine) | copy-start | bytes 5505028
  50.0 28.5 %copy-start.8 = (bf16[9,128,128]{2,1,0:T(8,128)(2,1)}, bf16[9,128,128]{2,1,0:T(8,128)(2,1)S(1)}, u32[]{:S(2)}) copy-start(bf16[9,128,128]{2,1,0:T(8,128)(2,1)S(1)} %collective-permute-done.5.wave_own) | copy-start | bytes 884740
  50.0 28.5 %collective-permute-start.10 = (bf16[7,8,128,128]{3,2,1,0:T(8,128)(2,1)S(1)}, bf16[7,8,128,128]{3,2,1,0:T(8,128)(2,1)S(1)}, u32[]{:S(2)}, u32[]{:S(2)}) collective-permute-start(bf16[7,8,128,128]{3,2,1,0:T(8,128)(2,1)S(1)} %broadcast_select_fusion.right_mine), channel_id=1, source_target_pairs={{0,1},{1,0},{2,3},{3,2},{4,5},{5,4},{6,7},{7,6},{8,9},{9,8},{10,11... | collective-permute-start | bytes 5505032 | tf_op jit(solution)/shard_map/ppermute | solution.py:150
  64.1 50.9 %collective-permute-start.7 = (bf16[7,8,128,128]{3,2,1,0:T(8,128)(2,1)}, bf16[7,8,128,128]{3,2,1,0:T(8,128)(2,1)S(1)}, u32[]{:S(2)}, u32[]{:S(2)}) collective-permute-start(bf16[7,8,128,128]{3,2,1,0:T(8,128)(2,1)} %collective-permute-done.2.below), channel_id=1, source_target_pairs={{4,8},{5,9},{6,10},{7,11},{8,12},{9,13},{10,14},{11,15},{20,24},{2... | collective-permute-start | bytes 5505032 | tf_op jit(solution)/shard_map/ppermute | solution.py:150
  64.9 50.6 %collective-permute-start.8 = (bf16[7,8,128,128]{3,2,1,0:T(8,128)(2,1)}, bf16[7,8,128,128]{3,2,1,0:T(8,128)(2,1)}, u32[]{:S(2)}, u32[]{:S(2)}) collective-permute-start(bf16[7,8,128,128]{3,2,1,0:T(8,128)(2,1)} %collective-permute-done.3.above), channel_id=1, source_target_pairs={{4,0},{5,1},{6,2},{7,3},{8,4},{9,5},{10,6},{11,7},{20,16},{21,17},... | collective-permute-start | bytes 5505032 | tf_op jit(solution)/shard_map/ppermute | solution.py:150
  66.2 50.2 %collective-permute-start.9 = (bf16[7,8,128,128]{3,2,1,0:T(8,128)(2,1)S(1)}, bf16[7,8,128,128]{3,2,1,0:T(8,128)(2,1)}, u32[]{:S(2)}, u32[]{:S(2)}) collective-permute-start(bf16[7,8,128,128]{3,2,1,0:T(8,128)(2,1)S(1)} %broadcast_select_fusion.right_mine), channel_id=1, source_target_pairs={{0,4},{1,5},{2,6},{3,7},{12,8},{13,9},{14,10},{15,11},{16,20},{17,... | collective-permute-start | bytes 5505032 | tf_op jit(solution)/shard_map/ppermute | solution.py:150
  78.5 24.5 %collective-permute-start.12 = (bf16[32,128,128]{2,1,0:T(8,128)(2,1)S(1)}, bf16[32,128,128]{2,1,0:T(8,128)(2,1)S(1)}, u32[]{:S(2)}, u32[]{:S(2)}) collective-permute-start(bf16[32,128,128]{2,1,0:T(8,128)(2,1)S(1)} %copy-done.1), channel_id=1, source_target_pairs={{0,2},{1,3},{2,0},{3,1},{4,6},{5,7},{6,4},{7,5},{8,10},{9,11},{10,... | collective-permute-start | bytes 3145736 | tf_op jit(solution)/shard_map/ppermute | solution.py:150
  78.5 1.2 copy-start.13
  79.8 11.3 %copy-start.9 = (bf16[9,128,128]{2,1,0:T(8,128)(2,1)S(1)}, bf16[9,128,128]{2,1,0:T(8,128)(2,1)}, u32[]{:S(2)}) copy-start(bf16[9,128,128]{2,1,0:T(8,128)(2,1)} %copy-done.8) | copy-start | bytes 884740
  89.9 1.1 copy-start.6
  91.0 25.4 %collective-permute-start.11 = (bf16[9,128,128]{2,1,0:T(8,128)(2,1)S(1)}, bf16[9,128,128]{2,1,0:T(8,128)(2,1)}, u32[]{:S(2)}, u32[]{:S(2)}) collective-permute-start(bf16[9,128,128]{2,1,0:T(8,128)(2,1)S(1)} %copy-done.9), channel_id=1, source_target_pairs={{4,6},{5,7},{6,4},{7,5},{8,10},{9,11},{10,8},{11,9},{20,22},{21,23... | collective-permute-start | bytes 884744 | tf_op jit(solution)/shard_map/ppermute | solution.py:150
  103.0 1.5 copy-start.3
  113.1 1.2 copy-start.5
  114.3 0.7 copy-start.11
  115.1 1.4 copy-start.14
  116.4 5.4 %collective-permute-start.13 = (bf16[7,8,128,128]{3,2,1,0:T(8,128)(2,1)}, bf16[7,8,128,128]{3,2,1,0:T(8,128)(2,1)}, u32[]{:S(2)}, u32[]{:S(2)}) collective-permute-start(bf16[7,8,128,128]{3,2,1,0:T(8,128)(2,1)} %collective-permute-done.9.right_mine), channel_id=1, source_target_pairs={{4,5},{5,4},{6,7},{7,6},{8,9},{9,8},{10,11},{11,10},{20,21},{21,20... | collective-permute-start | bytes 5505032 | tf_op jit(solution)/shard_map/ppermute | solution.py:150
  118.3 18.6 %collective-permute-start.14 = (bf16[24,128,128]{2,1,0:T(8,128)(2,1)}, bf16[24,128,128]{2,1,0:T(8,128)(2,1)}, u32[]{:S(2)}, u32[]{:S(2)}) collective-permute-start(bf16[24,128,128]{2,1,0:T(8,128)(2,1)} %get-tuple-element.81), channel_id=1, source_target_pairs={{0,2},{1,3},{2,0},{3,1},{4,6},{5,7},{6,4},{7,5},{8,10},{9,11},{10,... | collective-permute-start | bytes 2359304 | tf_op jit(solution)/shard_map/ppermute | solution.py:150
  121.8 15.2 %copy-start.7 = (f32[24,128,128]{2,1,0:T(8,128)S(1)}, f32[24,128,128]{2,1,0:T(8,128)}, u32[]{:S(2)}) copy-start(f32[24,128,128]{2,1,0:T(8,128)} %copy-done.6) | copy-start | bytes 4718596
  121.8 1.1 copy-start.10
  122.9 0.9 copy-start.12
  138.3 8.9 %collective-permute-start.15 = (f32[24,128,128]{2,1,0:T(8,128)S(1)}, f32[24,128,128]{2,1,0:T(8,128)S(1)}, u32[]{:S(2)}, u32[]{:S(2)}) collective-permute-start(f32[24,128,128]{2,1,0:T(8,128)S(1)} %convert_add_fusion.first_own), channel_id=1, source_target_pairs={{0,1},{1,0},{2,3},{3,2},{4,5},{5,4},{6,7},{7,6},{8,9},{9,8},{10,11... | collective-permute-start | bytes 4718600 | tf_op jit(solution)/shard_map/ppermute | solution.py:150
  138.4 8.7 %collective-permute-start.16 = (bf16[8,128,128]{2,1,0:T(8,128)(2,1)S(1)}, bf16[8,128,128]{2,1,0:T(8,128)(2,1)S(1)}, u32[]{:S(2)}, u32[]{:S(2)}) collective-permute-start(bf16[8,128,128]{2,1,0:T(8,128)(2,1)S(1)} %get-tuple-element.84), channel_id=1, source_target_pairs={{0,2},{1,3},{2,0},{3,1},{4,6},{5,7},{6,4},{7,5},{8,10},{9,11},{10,... | collective-permute-start | bytes 786440 | tf_op jit(solution)/shard_map/ppermute | solution.py:150
  138.8 12.7 %collective-permute-start.17 = (bf16[8,128,128]{2,1,0:T(8,128)(2,1)S(1)}, bf16[8,128,128]{2,1,0:T(8,128)(2,1)S(1)}, u32[]{:S(2)}, u32[]{:S(2)}) collective-permute-start(bf16[8,128,128]{2,1,0:T(8,128)(2,1)S(1)} %get-tuple-element.85), channel_id=1, source_target_pairs={{4,0},{5,1},{6,2},{7,3},{8,12},{9,13},{10,14},{11,15},{20,16},{21,... | collective-permute-start | bytes 786440 | tf_op jit(solution)/shard_map/ppermute | solution.py:150
  140.1 17.7 %collective-permute-start.18 = (bf16[8,128,128]{2,1,0:T(8,128)(2,1)S(1)}, bf16[8,128,128]{2,1,0:T(8,128)(2,1)S(1)}, u32[]{:S(2)}, u32[]{:S(2)}) collective-permute-start(bf16[8,128,128]{2,1,0:T(8,128)(2,1)S(1)} %get-tuple-element.87), channel_id=1, source_target_pairs={{4,2},{5,3},{6,0},{7,1},{8,14},{9,15},{10,12},{11,13},{20,18},{21,... | collective-permute-start | bytes 786440 | tf_op jit(solution)/shard_map/ppermute | solution.py:150
  147.2 10.7 %collective-permute-start.19 = (f32[8,128,128]{2,1,0:T(8,128)S(1)}, f32[8,128,128]{2,1,0:T(8,128)S(1)}, u32[]{:S(2)}, u32[]{:S(2)}) collective-permute-start(f32[8,128,128]{2,1,0:T(8,128)S(1)} %convert_add_fusion.1.last_own), channel_id=1, source_target_pairs={{0,1},{1,0},{2,3},{3,2},{4,5},{5,4},{6,7},{7,6},{8,9},{9,8},{10,11... | collective-permute-start | bytes 1572872 | tf_op jit(solution)/shard_map/ppermute | solution.py:150
  157.8 2.0 %collective-permute-start.20 = (f32[8,128,128]{2,1,0:T(8,128)S(1)}, f32[8,128,128]{2,1,0:T(8,128)S(1)}, u32[]{:S(2)}, u32[]{:S(2)}) collective-permute-start(f32[8,128,128]{2,1,0:T(8,128)S(1)} %shard_map.99.guest_own), channel_id=1, source_target_pairs={{0,1},{1,0},{2,3},{3,2},{4,5},{5,4},{6,7},{7,6},{8,9},{9,8},{10,11... | collective-permute-start | bytes 1572872 | tf_op jit(solution)/shard_map/ppermute | solution.py:150
  162.7 3.7 %collective-permute-start.21 = (f32[8,128]{1,0:T(8,128)S(1)}, f32[8,128]{1,0:T(8,128)S(1)}, u32[]{:S(2)}, u32[]{:S(2)}) collective-permute-start(f32[8,128]{1,0:T(8,128)S(1)} %get-tuple-element.90), channel_id=1, source_target_pairs={{0,2},{1,3},{2,0},{3,1},{4,6},{5,7},{6,4},{7,5},{8,10},{9,11},{10,... | collective-permute-start | bytes 12296 | tf_op jit(solution)/shard_map/ppermute | solution.py:150
  166.4 4.5 %collective-permute-start.22 = (f32[16,128]{1,0:T(8,128)S(1)}, f32[16,128]{1,0:T(8,128)S(1)}, u32[]{:S(2)}, u32[]{:S(2)}) collective-permute-start(f32[16,128]{1,0:T(8,128)S(1)} %constant_dynamic-update-slice_fusion.sums), channel_id=1, source_target_pairs={{0,4},{1,5},{2,6},{3,7},{4,0},{5,1},{6,2},{7,3},{8,12},{9,13},{10,... | collective-permute-start | bytes 24584 | tf_op jit(solution)/shard_map/ppermute | solution.py:150
  166.4 6.1 %collective-permute-start.23 = (f32[16,128]{1,0:T(8,128)S(1)}, f32[16,128]{1,0:T(8,128)S(1)}, u32[]{:S(2)}, u32[]{:S(2)}) collective-permute-start(f32[16,128]{1,0:T(8,128)S(1)} %constant_dynamic-update-slice_fusion.sums), channel_id=1, source_target_pairs={{0,8},{1,9},{2,10},{3,11},{4,12},{5,13},{6,14},{7,15},{8,0},{9,1},... | collective-permute-start | bytes 24584 | tf_op jit(solution)/shard_map/ppermute | solution.py:150
  170.9 5.4 %collective-permute-start.24 = (f32[16,128]{1,0:T(8,128)S(1)}, f32[16,128]{1,0:T(8,128)S(1)}, u32[]{:S(2)}, u32[]{:S(2)}) collective-permute-start(f32[16,128]{1,0:T(8,128)S(1)} %constant_dynamic-update-slice_fusion.sums), channel_id=1, source_target_pairs={{0,12},{1,13},{2,14},{3,15},{4,8},{5,9},{6,10},{7,11},{8,4},{9,5},... | collective-permute-start | bytes 24584 | tf_op jit(solution)/shard_map/ppermute | solution.py:150
  176.3 1.6 copy-start.4

commit v3 on v2

--- a/solution.py
+++ b/solution.py
@@ -8,7 +8,8 @@
 from jax.sharding import PartitionSpec as P
 
 BOTH = ("sector", "term")
-VMEM_LIMIT = 48 * 2**20
+VMEM_LIMIT = 60 * 2**20
+VMEM_SMALL = 32 * 2**20
 
 
 def on_device_any(
@@ -249,100 +250,107 @@
         result[slot] = found.astype(result.dtype)
 
     grouped(skipped, end, 4, apply)
-    out = pltpu.make_async_copy(result.at[pl.ds(0, first_slots)], first, sems.at[len(copies)])
-    out.start()
-    last[...] = result[first_slots:]
-    out.wait()
+    outs = [
+        pltpu.make_async_copy(result.at[part], target, sems.at[len(copies) + n])
+        for n, (part, target) in enumerate(
+            ((pl.ds(0, first_slots), first), (pl.ds(first_slots, most), last))
+        )
+    ]
+    for out in outs:
+        out.start()
+    for out in outs:
+        out.wait()
 
     @pl.loop(end, blocks)
     def _(slot):
         written(slot).wait()
 
 
-def sum_kernel(one, two, out):
-    out[...] = one[...].astype(out.dtype) + two[...].astype(out.dtype)
+def guest_kernel(
+    flags, table, weights, below, above, wave_own, wave_other, right_mine, right_sib,
+    own_out, other_out,
+    wave, right, left, sems,
+):
+    half = own_out.shape[0]
+    counts = [count_of(table, part * half, half, 3) for part in range(2)]
+    copies = [
+        pltpu.make_async_copy(source, target, sems.at[n])
+        for n, (source, target) in enumerate(
+            (
+                (right_mine, right.at[0]),
+                (right_sib, right.at[1]),
+                (wave_own.at[pl.ds(0, half)], wave.at[pl.ds(0, half)]),
+                (wave_other.at[pl.ds(0, half)], wave.at[pl.ds(half, half)]),
+            )
+        )
+    ]
+
+    @pl.when(counts[0] + counts[1] > 0)
+    def _():
+        for copy in copies:
+            copy.start()
+        choose(flags[0] == 1, above, below, left, sems.at[len(copies)])
+
+    own_out[...] = jnp.zeros_like(own_out)
+    other_out[...] = jnp.zeros_like(other_out)
+
+    @pl.when(counts[0] + counts[1] > 0)
+    def _():
+        for copy in copies:
+            copy.wait()
+        pltpu.make_async_copy(above, left, sems.at[len(copies)]).wait()
+
+    for part, target in enumerate((own_out, other_out)):
+
+        def apply(row):
+            carried = carried_of(
+                wave[row],
+                right[flags[1 + part], :, table[row, 4]],
+                weights[pl.ds(table[row, 5], 1), :],
+            )
+            result = applied(left[:, table[row, 2]], carried)
+            target[row - part * half] = result.astype(target.dtype)
+
+        grouped(part * half, part * half + counts[part], 4, apply)
 
 
 def far_kernel(
-    flags, table, guest_table, weights, carried_own, carried_other, below, above, own, other,
-    wave_own, wave_other, right_mine, right_sib,
-    own_out, other_out, guest_own_out, guest_other_out,
-    held, held_guest, wave, right, left, sems, guest_sems, wave_sems, left_sem,
+    flags, table, carried_own, carried_other, below, above, own, other,
+    own_out, other_out,
+    held, left, sems, more_sems,
 ):
-    rows = held.shape[0]
-    half = rows // 2
-    for relation, source in enumerate((wave_own, wave_other)):
-        pltpu.make_async_copy(
-            source.at[pl.ds(0, half)], wave.at[pl.ds(relation * half, half)], wave_sems.at[relation]
-        ).start()
-
-    @pl.loop(0, rows)
-    def _(row):
-        @pl.when(guest_table[row, 0] == 3)
-        def _():
-            sector = guest_table[row, 4]
-            choose(
-                flags[1 + row // half] == 0, right_mine.at[:, sector], right_sib.at[:, sector],
-                right.at[row], guest_sems.at[row],
-            )
-
-    choose(flags[0] == 1, above, below, left, left_sem.at[0])
-
-    @pl.loop(0, half)
-    def _(slot):
-        for part, carried in enumerate((carried_own, carried_other)):
+    half = own_out.shape[0]
+    lows = [half - count_of(table, part * half, half, 3) for part in range(2)]
+    choose(flags[0] == 1, above, below, left, more_sems.at[0])
+    kept = [
+        pltpu.make_async_copy(source, target, more_sems.at[1 + n])
+        for n, (source, target) in enumerate(((own, own_out), (other, other_out)))
+    ]
+    for copy in kept:
+        copy.start()
+    for part, carried in enumerate((carried_own, carried_other)):
+
+        @pl.loop(lows[part], half)
+        def _(slot):
             row = part * half + slot
-
-            @pl.when(table[row, 0] == 3)
-            def _():
-                pltpu.make_async_copy(carried.at[slot], held.at[row], sems.at[row]).start()
-
-    own_out[...] = own[...]
-    other_out[...] = other[...]
-    guest_own_out[...] = jnp.zeros_like(guest_own_out)
-    guest_other_out[...] = jnp.zeros_like(guest_other_out)
-    for relation, source in enumerate((wave_own, wave_other)):
-        pltpu.make_async_copy(
-            source.at[pl.ds(0, half)], wave.at[pl.ds(relation * half, half)], wave_sems.at[relation]
-        ).wait()
-
-    @pl.loop(0, rows)
-    def _(row):
-        @pl.when(guest_table[row, 0] == 3)
-        def _():
-            pltpu.make_async_copy(right_mine.at[:, 0], right.at[row], guest_sems.at[row]).wait()
-
-    def carry(row):
-        held_guest[row] = carried_of(
-            wave[row], right[row], weights[pl.ds(guest_table[row, 5], 1), :]
-        )
-
-    counts = [count_of(guest_table, part * half, half, 3) for part in range(2)]
-    for part in range(2):
-        grouped(part * half, part * half + counts[part], 4, carry)
-    pltpu.make_async_copy(above, left, left_sem.at[0]).wait()
-    for part, target in enumerate((guest_own_out, guest_other_out)):
-
-        def apply_guest(row):
-            result = applied(left[:, guest_table[row, 2]], held_guest[row])
-            target[row - part * half] = result.astype(target.dtype)
-
-        grouped(part * half, part * half + counts[part], 4, apply_guest)
-
-    @pl.loop(0, rows)
-    def _(row):
-        @pl.when(table[row, 0] == 3)
-        def _():
-            pltpu.make_async_copy(carried_own.at[0], held.at[row], sems.at[row]).wait()
-
-    for part, target in enumerate((own_out, other_out)):
-
-        def apply_own(row):
-            result = applied(left[:, table[row, 2]], held[row])
-            target[row - part * half] = result.astype(target.dtype)
-
-        high = (part + 1) * half
-        grouped(high - count_of(table, part * half, half, 3), high, 4, apply_own)
+            pltpu.make_async_copy(carried.at[slot], held.at[row], sems.at[row]).start()
+
+    for copy in kept:
+        copy.wait()
+    pltpu.make_async_copy(above, left, more_sems.at[0]).wait()
+    for part, (carried, target) in enumerate(((carried_other, other_out), (carried_own, own_out))):
+        part = 1 - part
+
+        @pl.loop(lows[part], half)
+        def _(slot):
+            row = part * half + slot
+            pltpu.make_async_copy(carried.at[slot], held.at[row], sems.at[row]).wait()
+
+        def apply(slot):
+            row = part * half + slot
+            target[slot] = applied(left[:, table[row, 2]], held[row]).astype(target.dtype)
+
+        grouped(lows[part], half, 4, apply)
 
 
 def pick_kernel(table, own, facts, out):
@@ -358,33 +366,26 @@
     return jnp.sum(value.reshape(-1, 8, 128), axis=0)
 
 
-def first_kernel(table, first_own, first_sib, wave, image, sums):
-    blocks = image.shape[0]
+def first_kernel(table, own, got, wave, whole, sums):
+    blocks = wave.shape[0]
     zero = jnp.zeros((8, 128), jnp.float32)
-    image[...] = jnp.zeros_like(image)
-
-    def place(k, totals):
-        for code, source in ((0, first_own), (3, first_sib)):
-
-            @pl.when(table[k, 0] == code)
-            def _():
-                image[k] = source[table[k, 1]]
-
-        kept = ((table[k, 0] == 0) | (table[k, 0] == 3)).astype(jnp.float32)
-        value = wave[k].astype(jnp.float32) * kept
-        return totals[0] + folded(value * value), totals[1] + folded(value * image[k])
-
-    norm_map, correlation_map = lax.fori_loop(0, blocks, place, (zero, zero), unroll=2)
+    whole[...] = own[...] + got[...].astype(jnp.float32)
+    count = count_of(table, 0, blocks, 1)
+
+    def add(n, totals):
+        value, found = wave[table[n, 1]].astype(jnp.float32), whole[table[n, 2]]
+        return totals[0] + folded(value * value), totals[1] + folded(value * found)
+
+    norm_map, correlation_map = lax.fori_loop(0, count, add, (zero, zero))
     norm = jnp.sum(norm_map, keepdims=True)
     correlation = jnp.sum(correlation_map, keepdims=True)
     ratio = ratio_of(norm, correlation)
 
-    def rest(k, total):
-        kept = ((table[k, 0] == 0) | (table[k, 0] == 3)).astype(jnp.float32)
-        residual = image[k] - ratio * (wave[k].astype(jnp.float32) * kept)
+    def rest(n, total):
+        residual = whole[table[n, 2]] - ratio * wave[table[n, 1]].astype(jnp.float32)
         return total + folded(residual * residual)
 
-    resid = jnp.sum(lax.fori_loop(0, blocks, rest, zero, unroll=2), keepdims=True)
+    resid = jnp.sum(lax.fori_loop(0, count, rest, zero), keepdims=True)
     sums[...] = lined(norm, correlation, resid)
 
 
@@ -396,22 +397,19 @@
     return result
 
 
-def last_kernel(
-    table, sums_first, last_own, guest_own, last_sib, guest_sib, wave, held,
-    image, sums, late, out_sems,
-):
+def sum_kernel(one, two, out):
+    out[...] = one[...].astype(out.dtype) + two[...].astype(out.dtype)
+
+
+def late_kernel(table, sums_first, last_own, last_got, guest_full, wave, late, sums):
     blocks = wave.shape[0]
     most = last_own.shape[0]
     zero = jnp.zeros((8, 128), jnp.float32)
-    for n, source in enumerate((last_own, guest_own, last_sib, guest_sib)):
-        late[pl.ds(n * most, most)] = source[...]
+    late[pl.ds(0, most)] = last_own[...] + last_got[...].astype(jnp.float32)
+    late[pl.ds(most, most)] = guest_full[...]
     count = count_of(table, 0, blocks, 1)
 
-    def write(n):
-        return pltpu.make_async_copy(late.at[table[n, 2]], image.at[table[n, 1]], out_sems.at[n])
-
     def add(n, totals):
-        write(n).start()
         value, found = wave[table[n, 1]].astype(jnp.float32), late[table[n, 2]]
         return totals[0] + folded(value * value), totals[1] + folded(value * found)
 
@@ -428,43 +426,41 @@
     first = [sums_first[n : n + 1, 0:1] for n in range(3)]
     sums[...] = lined(*merged(first, (norm, correlation, resid)))
 
-    @pl.loop(0, count)
-    def _(n):
-        write(n).wait()
-
-
-def correction_kernel(
-    entries, sums, near, far, across, image_in, wave_in, out, ratio, image, wave, result, sems
-):
-    chunks = sems.shape[1]
+
+def place_kernel(table, first_own, late_own, first_sib, late_sib, image, kept, sem):
+    @pl.loop(0, kept.shape[0])
+    def _(k):
+        for code, source in enumerate((first_own, late_own, first_sib, late_sib)):
+
+            @pl.when(table[k, 0] == code)
+            def _():
+                kept[k] = source[table[k, 1]]
+
+    copy = pltpu.make_async_copy(kept, image, sem.at[0])
+    copy.start()
+    copy.wait()
+
+
+def correction_kernel(entries, sums, near, far, across, image, wave, out, ratio, result, sems):
+    chunks = sems.shape[0]
     size = image.shape[0] // chunks
 
-    def copy(kind, source, target, n):
-        part = pl.ds(n * size, size)
-        return pltpu.make_async_copy(source.at[part], target.at[part], sems.at[kind, n])
-
-    images = [copy(0, image_in, image, n) for n in range(chunks)]
-    waves = [copy(1, wave_in, wave, n) for n in range(chunks)]
-    results = [copy(2, result, out, n) for n in range(chunks)]
-    for n in range(chunks):
-        images[n].start()
-        waves[n].start()
-
     def total(ref):
-        return merged(*([ref[base + n : base + n + 1, 0:1] for n in range(3)] for base in (0, 8)))
+        parts = [[ref[base + n : base + n + 1, 0:1] for n in range(3)] for base in (0, 8, 16, 24)]
+        return merged(merged(*parts[:2]), merged(*parts[2:]))
 
     whole = merged(merged(total(sums), total(near)), merged(total(far), total(across)))
     rayleigh = whole[1] / whole[0]
     scale = lax.rsqrt(whole[2] / entries + 1e-06)
-    ratio[...] = jnp.broadcast_to(rayleigh, (8, 128))
+    ratio[0] = rayleigh[0, 0]
+    copies = []
     for n in range(chunks):
-        images[n].wait()
-        waves[n].wait()
         part = pl.ds(n * size, size)
         result[part] = (image[part] - rayleigh * wave[part].astype(jnp.float32)) * scale
-        results[n].start()
-    for n in range(chunks):
-        results[n].wait()
+        copies.append(pltpu.make_async_copy(result.at[part], out.at[part], sems.at[n]))
+        copies[n].start()
+    for copy in copies:
+        copy.wait()
 
 
 def ratio_of(norm, correlation):
@@ -486,7 +482,7 @@
     return jnp.sum(before.astype(jnp.int32), axis=-1)
 
 
-def call(kernel, out_shape, in_spaces, out_spaces, scratch, flops=1, aliases={}):
+def call(kernel, out_shape, in_spaces, out_spaces, scratch, flops=1, aliases={}, vmem=VMEM_LIMIT):
     return pl.pallas_call(
         kernel,
         out_shape=out_shape,
@@ -494,7 +490,7 @@
         out_specs=jax.tree.map(lambda space: pl.BlockSpec(memory_space=space), out_spaces),
         scratch_shapes=scratch,
         input_output_aliases=aliases,
-        compiler_params=pltpu.CompilerParams(vmem_limit_bytes=VMEM_LIMIT),
+        compiler_params=pltpu.CompilerParams(vmem_limit_bytes=vmem),
         cost_estimate=pl.CostEstimate(
             flops=flops, bytes_accessed=1, transcendentals=0
         ),
@@ -605,23 +601,29 @@
     table = table.reshape(2, blocks, -1)
 
     def source_of(which, of):
-        code = jnp.where(guest[of], 2, jnp.where(place[of] < first_slots, 0, 1))
-        slot = jnp.where(
-            guest[of], guest_place[of], jnp.where(place[of] < first_slots, place[of], place[of] - first_slots)
+        late_place = jnp.where(guest[of], most + guest_place[of], place[of] - first_slots)
+        late = guest[of] | (place[of] >= first_slots)
+        return jnp.stack(
+            [2 * which + late.astype(jnp.int32), jnp.where(late, late_place, place[of])], axis=-1
         )
-        return jnp.stack([code + 3 * which, slot], axis=-1)
 
     sources = jnp.where(here[0][:, None], source_of(0, 0), source_of(1, 2))
-    is_late = sources[:, 0] % 3 != 0
-    late_order = ranks(jnp.where(is_late, 0, 1)[None])
-    source_row = (sources[:, 0] - sources[:, 0] // 3 - 1) * most + sources[:, 1]
-    late_table = ordered(late_order, blocks, [is_late[None], block[None], source_row[None]])[0]
+    picked_out = jnp.stack([sources[:, 0] == 0, sources[:, 0] == 1]).astype(jnp.int32)
+    first_table, late_table = ordered(
+        ranks(1 - picked_out),
+        blocks,
+        [
+            picked_out,
+            jnp.broadcast_to(block, (2, blocks)),
+            jnp.broadcast_to(sources[:, 1], (2, blocks)),
+        ],
+    )
 
     held = (below, above, right_mine, wave_guest)
-    held += (table, far_table, weights, sources, late_table)
+    held += (table, far_table, weights, sources, first_table, late_table)
     held = lax.optimization_barrier(held)
     below, above, right_mine, wave_guest = held[:4]
-    table, far_table, weights, sources, late_table = held[4:]
+    table, far_table, weights, sources, first_table, late_table = held[4:]
     below_two = hop(below, up, inner)
     above_two = hop(above, down, inner)
     right_guest = hop(right_mine, inward, outer)
@@ -636,14 +638,14 @@
                 jax.ShapeDtypeStruct((most, dim, terms * dim), bf16),
             ),
             [SMEM, VMEM] + [HBM] * 6,
-            (HBM, VMEM, HBM),
+            (HBM, HBM, HBM),
             [
                 pltpu.VMEM((blocks,) + square, kind),
                 pltpu.VMEM((most, dim, terms * dim), bf16),
                 pltpu.VMEM((blocks,) + square, bf16),
                 pltpu.VMEM((2,) + env, bf16),
                 pltpu.VMEM((3,) + env, bf16),
-                pltpu.SemaphoreType.DMA((7,)),
+                pltpu.SemaphoreType.DMA((8,)),
                 pltpu.SemaphoreType.DMA((most,)),
             ],
         )(
@@ -667,73 +669,82 @@
 
     last = jax.ShapeDtypeStruct((most,) + square, f32)
     last_sent = jax.ShapeDtypeStruct((most,) + square, bf16)
-    last_own, last_other, guest_own, guest_other = call(
+    guest_own, guest_other = call(
+        guest_kernel,
+        (last_sent, last_sent),
+        [SMEM] * 2 + [VMEM] + [HBM] * 6,
+        (VMEM,) * 2,
+        [
+            pltpu.VMEM((2 * most,) + square, bf16),
+            pltpu.VMEM((2,) + env, bf16),
+            pltpu.VMEM(env, bf16),
+            pltpu.SemaphoreType.DMA((5,)),
+        ],
+    )(
+        flags, guest_got, weights, below_two, above_two,
+        wave_guest, wave_guest_other, right_guest, right_guest_sib,
+    )
+    guest_straight = move(guest_own, GUEST_BACK)
+    guest_crossed = move(guest_other, GUEST_BACK_CROSSED)
+    last_own, last_other = call(
         far_kernel,
-        (last, last_sent, last_sent, last_sent),
-        [SMEM] * 3 + [VMEM] + [HBM] * 4 + [VMEM] * 2 + [HBM] * 4,
-        (VMEM,) * 4,
+        (last, last_sent),
+        [SMEM] * 2 + [HBM] * 6,
+        (VMEM,) * 2,
         [
             pltpu.VMEM((2 * most, dim, terms * dim), bf16),
-            pltpu.VMEM((2 * most, dim, terms * dim), bf16),
-            pltpu.VMEM((2 * most,) + square, bf16),
-            pltpu.VMEM((2 * most, terms) + square, bf16),
             pltpu.VMEM(env, bf16),
             pltpu.SemaphoreType.DMA((2 * most,)),
-            pltpu.SemaphoreType.DMA((2 * most,)),
-            pltpu.SemaphoreType.DMA((2,)),
-            pltpu.SemaphoreType.DMA((1,)),
+            pltpu.SemaphoreType.DMA((3,)),
         ],
+        2**37,
     )(
-        flags, far_table, guest_got, weights, carried_own, carried_other,
-        below_two, above_two, own_last, other_last,
-        wave_guest, wave_guest_other, right_guest, right_guest_sib,
-    )
-    guest_straight = move(guest_own, GUEST_BACK)
-    guest_crossed = move(guest_other, GUEST_BACK_CROSSED)
+        flags, after(far_table, guest_own), carried_own, carried_other, below_two, above_two,
+        own_last, other_last,
+    )
     last_got = move(last_other, COLUMN)
-    last_full = last_own + last_got.astype(f32)
-    first_own = own + after(first_got, last_own).astype(f32)
-    first_sib = move(first_own, CORE)
-    last_sib = move(last_full, CORE)
-    image_shape = jax.ShapeDtypeStruct((blocks,) + square, f32)
-    image, sums_first = call(
+    first_own, sums_first = call(
         first_kernel,
-        (image_shape, jax.ShapeDtypeStruct((8, 128), f32)),
+        (jax.ShapeDtypeStruct((first_slots,) + square, f32), jax.ShapeDtypeStruct((8, 128), f32)),
         [SMEM] + [VMEM] * 3,
         (VMEM, VMEM),
         [],
-    )(after(sources, last_own), first_own, first_sib, wavefunction)
-    guest_full = call(sum_kernel, last, [VMEM] * 2, VMEM, [], 2**37)(
+        vmem=VMEM_SMALL,
+    )(first_table, own, after(first_got, last_own), wavefunction)
+    first_sib = move(first_own, CORE)
+    guest_full = call(sum_kernel, last, [VMEM] * 2, VMEM, [], 2**37, vmem=VMEM_SMALL)(
         after(guest_straight, sums_first), guest_crossed
     )
-    guest_sib = move(guest_full, CORE)
-
-    image, sums = call(
-        last_kernel,
-        (image_shape, jax.ShapeDtypeStruct((8, 128), f32)),
-        [SMEM] + [VMEM] * 6 + [HBM],
+    late, sums = call(
+        late_kernel,
+        (jax.ShapeDtypeStruct((2 * most,) + square, f32), jax.ShapeDtypeStruct((8, 128), f32)),
+        [SMEM] + [VMEM] * 5,
+        (VMEM, VMEM),
+        [],
+        vmem=VMEM_SMALL,
+    )(late_table, sums_first, last_own, last_got, guest_full, wavefunction)
+    late_sib = move(late, CORE)
+    image_shape = jax.ShapeDtypeStruct((blocks,) + square, f32)
+    image, kept = call(
+        place_kernel,
+        (image_shape, image_shape),
+        [SMEM] + [VMEM] * 4,
         (HBM, VMEM),
-        [
-            pltpu.VMEM((4 * most,) + square, f32),
-            pltpu.SemaphoreType.DMA((blocks,)),
-        ],
-        aliases={7: 0},
-    )(late_table, sums_first, last_full, guest_full, last_sib, guest_sib, wavefunction, image)
-    sums = jnp.concatenate([sums, move(sums, COLUMN)])
+        [pltpu.SemaphoreType.DMA((1,))],
+        vmem=VMEM_SMALL,
+    )(sources, first_own, late, first_sib, late_sib)
+    for pairs in (CORE, COLUMN):
+        sums = jnp.concatenate([sums, move(sums, pairs)])
     sums = [sums] + [move(sums, pairs_of(lambda z, y, c: (z ^ n, y, c))) for n in (1, 2, 3)]
     correction, rayleigh = call(
         functools.partial(correction_kernel, blocks * 8 * dim * dim),
-        (image_shape, jax.ShapeDtypeStruct((8, 128), f32)),
-        [VMEM] * 4 + [HBM] * 2,
-        (HBM, VMEM),
-        [
-            pltpu.VMEM((blocks,) + square, f32),
-            pltpu.VMEM((blocks,) + square, bf16),
-            pltpu.VMEM((blocks,) + square, f32),
-            pltpu.SemaphoreType.DMA((3, 4)),
-        ],
-    )(*sums, image, wavefunction)
-    return image, correction, rayleigh[0, :1]
+        (image_shape, jax.ShapeDtypeStruct((1,), f32)),
+        [VMEM] * 6,
+        (HBM, SMEM),
+        [pltpu.VMEM((blocks,) + square, f32), pltpu.SemaphoreType.DMA((8,))],
+        vmem=VMEM_SMALL,
+    )(*sums, kept, wavefunction)
+    return image, correction, rayleigh
 
 
 def solution(mesh):

time: 181 us -> 171 us (0.945)
  local copies, waits for them, and re-layouts: 14.5 us -> 5.99 us
  waiting for transfers between devices: 45.4 us -> 41.1 us
  Pallas kernels: 33.7 us -> 37.1 us
    unnamed x36 -> x27, local copies, waits for them, and re-layouts: 10.7 us -> 1.93 us
    ppermute x25, waiting for transfers between devices: 45.4 us -> 41.1 us  [move(): return lax.ppermute(array, BOTH, pairs)]
    pallas_call x4 -> x6, Pallas kernels: 12.5 us -> 14.7 us  [the longest x1 5.55 us: on_device(): call(far_kernel, (last, last_sent), [SMEM] * 2 + [HBM] * 6, (VMEM,) * 2,...]
  transfers between devices with their start and end apart: 25 -> 25, of which waited for: 11 -> 11; matrix products, arithmetic and copies ran while one was open for 5% -> 7% of each run, Pallas kernels for 16% -> 21%
where the time goes in v3:
time: 171 us; the launch traced here: 170 us
  starting transfers between devices  75 us (44%)
  waiting for transfers between devices  41.1 us (24%)
  Pallas kernels  37.1 us (22%)
  other arithmetic  8.56 us (5%)
  local copies, waits for them, and re-layouts  5.99 us (4%)
    ppermute x25, starting transfers between devices, move(): return lax.ppermute(array, BOTH, pairs)  75 us
    ppermute x25, waiting for transfers between devices, move(): return lax.ppermute(array, BOTH, pairs)  41.1 us
    pallas_call x2, Pallas kernels, near(): call(near_kernel, (jax.ShapeDtypeStruct((first_slots,) + square, kind), j...  18.4 us
    pallas_call x1, Pallas kernels, on_device(): call(far_kernel, (last, last_sent), [SMEM] * 2 + [HBM] * 6, (VMEM,) * 2,...  5.55 us
    select_n x2, other arithmetic, mine_of(): return jnp.where(y == c, own, swapped)  4.71 us
    pallas_call x1, Pallas kernels, on_device(): call(place_kernel, (image_shape, image_shape), [SMEM] + [VMEM] * 4, (HBM,...  3.58 us
  transfers between devices with their start and end apart: 25, of which 11 were waited for; matrix products, arithmetic and copies ran while one was open for 7% of the time, Pallas kernels for 21%

profile of v3, /device:TPU:0, one launch (start us, length us, event | category | flops | bytes accessed | tf_op | source)
XLA Modules:
  0.0 169.9 jit_solution(17255527879091232826)
XLA Ops:
  0.6 1.9 %collective-permute-start = (bf16[7,8,128,128]{3,2,1,0:T(8,128)(2,1)}, bf16[7,8,128,128]{3,2,1,0:T(8,128)(2,1)}, u32[]{:S(2)}, u32[]{:S(2)}) collective-permute-start(bf16[7,8,128,128]{3,2,1,0:T(8,128)(2,1)} %param.11), channel_id=1, source_target_pairs={{1,2},{2,1},{5,6},{6,5},{9,10},{10,9},{13,14},{14,13},{17,18},{18,... | collective-permute-start | bytes 5505032 | tf_op jit(solution)/shard_map/ppermute | solution.py:151
  2.5 3.1 %collective-permute-start.1 = (bf16[7,16]{1,0:T(8,128)(2,1)}, bf16[7,16]{1,0:T(8,128)(2,1)S(1)}, u32[]{:S(2)}, u32[]{:S(2)}) collective-permute-start(bf16[7,16]{1,0:T(8,128)(2,1)} %param.13), channel_id=1, source_target_pairs={{0,1},{1,0},{2,3},{3,2},{4,5},{5,4},{6,7},{7,6},{8,9},{9,8},{10,11... | collective-permute-start | bytes 680 | tf_op jit(solution)/shard_map/ppermute | solution.py:151
  5.7 0.7 subtract_bitcast_fusion
  6.4 0.7 pad_add_fusion
  7.4 0.7 stack.107
  8.3 0.7 fusion.39
  9.7 2.0 %shard_map.94 = bf16[9,128,128]{2,1,0:T(8,128)(2,1)} custom-call(s32[8,6]{1,0:T(8,128)} %get-tuple-element.138.table, bf16[32,128,128]{2,1,0:T(8,128)(2,1)} %wave.5, bf16[1,128,128]{2,1,0:T(8,128)(2,1)} %pad_bitcast_fusion.facts), custom_call_target="tpu_custom_call" | custom-call | flops 1 | bytes 1 | tf_op jit(solution)/shard_map/pallas_call | solution.py:575
  11.7 1.7 %broadcast_select_fusion.1.left_mine = bf16[7,8,128,128]{3,2,1,0:T(8,128)(2,1)S(1)} fusion(bf16[7,8,128,128]{3,2,1,0:T(8,128)(2,1)} %param.11, bf16[7,8,128,128]{3,2,1,0:T(8,128)(2,1)} %collective-permute-done, pred[]{:T(512)} %eq.285), kind=kLoop, calls=%fused_computation.1 | loop fusion | flops 917504 | bytes 5505025 | tf_op jit(solution)/shard_map/jit(_where)/select_n | solution.py:525
  13.4 4.8 %collective-permute-start.2 = (bf16[7,8,128,128]{3,2,1,0:T(8,128)(2,1)S(1)}, bf16[7,8,128,128]{3,2,1,0:T(8,128)(2,1)}, u32[]{:S(2)}, u32[]{:S(2)}) collective-permute-start(bf16[7,8,128,128]{3,2,1,0:T(8,128)(2,1)S(1)} %broadcast_select_fusion.1.left_mine), channel_id=1, source_target_pairs={{0,4},{1,5},{2,6},{3,7},{4,8},{5,9},{6,10},{7,11},{8,12},{9,13},{1... | collective-permute-start | bytes 5505032 | tf_op jit(solution)/shard_map/ppermute | solution.py:151
  18.2 1.3 collective-permute-start.3
  19.5 16.8 %collective-permute-start.6 = (s32[3,32]{1,0:T(4,128)S(1)}, s32[3,32]{1,0:T(4,128)S(1)}, u32[]{:S(2)}, u32[]{:S(2)}) collective-permute-start(s32[3,32]{1,0:T(4,128)S(1)} %get-tuple-element.54), channel_id=1, source_target_pairs={{0,2},{1,3},{2,0},{3,1},{4,6},{5,7},{6,4},{7,5},{8,10},{9,11},{10,... | collective-permute-start | bytes 1160 | tf_op jit(solution)/shard_map/ppermute | solution.py:151
  36.3 1.9 %collective-permute-start.4 = (bf16[7,8,128,128]{3,2,1,0:T(8,128)(2,1)}, bf16[7,8,128,128]{3,2,1,0:T(8,128)(2,1)}, u32[]{:S(2)}, u32[]{:S(2)}) collective-permute-start(bf16[7,8,128,128]{3,2,1,0:T(8,128)(2,1)} %param.12), channel_id=1, source_target_pairs={{1,2},{2,1},{5,6},{6,5},{9,10},{10,9},{13,14},{14,13},{17,18},{18,... | collective-permute-start | bytes 5505032 | tf_op jit(solution)/shard_map/ppermute | solution.py:151
  38.2 4.6 %collective-permute-start.5 = (bf16[9,128,128]{2,1,0:T(8,128)(2,1)}, bf16[9,128,128]{2,1,0:T(8,128)(2,1)S(1)}, u32[]{:S(2)}, u32[]{:S(2)}) collective-permute-start(bf16[9,128,128]{2,1,0:T(8,128)(2,1)} %shard_map.94), channel_id=1, source_target_pairs={{0,4},{1,5},{2,6},{3,7},{12,8},{13,9},{14,10},{15,11},{16,20},{17,... | collective-permute-start | bytes 884744 | tf_op jit(solution)/shard_map/ppermute | solution.py:151
  42.9 0.7 copy.161
  46.0 3.0 %broadcast_select_fusion.right_mine = bf16[7,8,128,128]{3,2,1,0:T(8,128)(2,1)} fusion(bf16[7,8,128,128]{3,2,1,0:T(8,128)(2,1)} %param.12, bf16[7,8,128,128]{3,2,1,0:T(8,128)(2,1)} %collective-permute-done.4, pred[]{:T(512)} %eq.285), kind=kLoop, calls=%fused_computation | loop fusion | flops 917504 | bytes 5505025 | tf_op jit(solution)/shard_map/jit(_where)/select_n | solution.py:525
  49.0 1.5 collective-permute-done.5.wave_own
  50.5 13.4 %collective-permute-start.10 = (bf16[7,8,128,128]{3,2,1,0:T(8,128)(2,1)}, bf16[7,8,128,128]{3,2,1,0:T(8,128)(2,1)}, u32[]{:S(2)}, u32[]{:S(2)}) collective-permute-start(bf16[7,8,128,128]{3,2,1,0:T(8,128)(2,1)} %broadcast_select_fusion.right_mine), channel_id=1, source_target_pairs={{0,1},{1,0},{2,3},{3,2},{4,5},{5,4},{6,7},{7,6},{8,9},{9,8},{10,11... | collective-permute-start | bytes 5505032 | tf_op jit(solution)/shard_map/ppermute | solution.py:151
  63.9 1.9 %collective-permute-start.7 = (bf16[7,8,128,128]{3,2,1,0:T(8,128)(2,1)}, bf16[7,8,128,128]{3,2,1,0:T(8,128)(2,1)}, u32[]{:S(2)}, u32[]{:S(2)}) collective-permute-start(bf16[7,8,128,128]{3,2,1,0:T(8,128)(2,1)} %collective-permute-done.2.below), channel_id=1, source_target_pairs={{4,8},{5,9},{6,10},{7,11},{8,12},{9,13},{10,14},{11,15},{20,24},{2... | collective-permute-start | bytes 5505032 | tf_op jit(solution)/shard_map/ppermute | solution.py:151
  65.8 1.3 collective-permute-start.8
  67.1 12.2 %collective-permute-start.9 = (bf16[7,8,128,128]{3,2,1,0:T(8,128)(2,1)}, bf16[7,8,128,128]{3,2,1,0:T(8,128)(2,1)}, u32[]{:S(2)}, u32[]{:S(2)}) collective-permute-start(bf16[7,8,128,128]{3,2,1,0:T(8,128)(2,1)} %broadcast_select_fusion.right_mine), channel_id=1, source_target_pairs={{0,4},{1,5},{2,6},{3,7},{12,8},{13,9},{14,10},{15,11},{16,20},{17,... | collective-permute-start | bytes 5505032 | tf_op jit(solution)/shard_map/ppermute | solution.py:151
  79.3 0.6 slice_bitcast_fusion
  79.9 8.6 %shard_map.95 = (f32[24,128,128]{2,1,0:T(8,128)}, f32[8,128,128]{2,1,0:T(8,128)}, bf16[8,128,896]{2,1,0:T(8,128)(2,1)}) custom-call(s32[32,6]{1,0:T(8,128)} %get-tuple-element.118.table, f32[16,896]{1,0:T(8,128)} %bitcast.117, bf16[32,128,128]{2,1,0:T(8,128)(2,1)} %wave.5, bf16[7,8,128,128]{3,2,1,0:T(8,128)(2,1)} %broadcast_select_fusion.right_mine, ...), custom_call_target="tpu_custom_call" | custom-call | flops 1 | bytes 1 | tf_op jit(solution)/shard_map/pallas_call | solution.py:633
  88.5 0.7 collective-permute-start.11
  89.2 14.7 %collective-permute-done.12.wave_in = bf16[32,128,128]{2,1,0:T(8,128)(2,1)} collective-permute-done((bf16[32,128,128]{2,1,0:T(8,128)(2,1)S(1)}, bf16[32,128,128]{2,1,0:T(8,128)(2,1)}, u32[]{:S(2)}, u32[]{:S(2)}) %collective-permute-start.12) | collective-permute-done | bytes 1048608 | tf_op jit(solution)/shard_map/ppermute | solution.py:151
  103.9 9.8 %shard_map.96 = (bf16[24,128,128]{2,1,0:T(8,128)(2,1)}, bf16[8,128,128]{2,1,0:T(8,128)(2,1)}, bf16[8,128,896]{2,1,0:T(8,128)(2,1)}) custom-call(s32[32,6]{1,0:T(8,128)} %get-tuple-element.117.table, f32[16,896]{1,0:T(8,128)} %bitcast.118, bf16[32,128,128]{2,1,0:T(8,128)(2,1)} %collective-permute-done.12.wave_in, ...), custom_call_target="tpu_custom_call" | custom-call | flops 1 | bytes 1 | tf_op jit(solution)/shard_map/pallas_call | solution.py:633
  113.7 2.6 %collective-permute-done.8.above = bf16[7,8,128,128]{3,2,1,0:T(8,128)(2,1)} collective-permute-done((bf16[7,8,128,128]{3,2,1,0:T(8,128)(2,1)}, bf16[7,8,128,128]{3,2,1,0:T(8,128)(2,1)}, u32[]{:S(2)}, u32[]{:S(2)}) %collective-permute-start.8) | collective-permute-done | bytes 1835040 | tf_op jit(solution)/shard_map/ppermute | solution.py:151
  116.4 1.2 collective-permute-done.9.right_mine
  117.5 0.8 collective-permute-start.14
  119.8 1.2 copy-done.7
  121.0 1.9 %shard_map.97 = (bf16[8,128,128]{2,1,0:T(8,128)(2,1)}, bf16[8,128,128]{2,1,0:T(8,128)(2,1)}) custom-call(s32[3]{0:T(128)} %add_convert_fusion.4.flags, s32[16,6]{1,0:T(8,128)} %maximum_convert_fusion.table, f32[16,896]{1,0:T(8,128)} %bitcast.119, bf16[7,8,128,128]{3,2,1,0:T(8,128)(2,1)} %collective-permute-done.7.below, ...), custom_call_target="tpu_custom_call" | custom-call | flops 1 | bytes 1 | tf_op jit(solution)/shard_map/pallas_call | solution.py:672
  122.9 1.3 collective-permute-start.16
  124.2 0.7 copy.133.table
  124.9 1.5 collective-permute-start.17
  126.4 5.5 %shard_map.98 = (f32[8,128,128]{2,1,0:T(8,128)}, bf16[8,128,128]{2,1,0:T(8,128)(2,1)}) custom-call(s32[3]{0:T(128)} %add_convert_fusion.4.flags, s32[16,6]{1,0:T(8,128)} %copy.133.table, bf16[8,128,896]{2,1,0:T(8,128)(2,1)} %get-tuple-element.81.carried_own, bf16[8,128,896]{2,1,0:T(8,128)(2,1)} %get-tuple-element.82.carried_other, ...), custom_call_target="tpu_custom_call" | custom-call | flops 137438953472 | bytes 1 | tf_op jit(solution)/shard_map/pallas_call | solution.py:689
  132.0 5.7 %collective-permute-done.13.got = bf16[24,128,128]{2,1,0:T(8,128)(2,1)S(1)} collective-permute-done((bf16[24,128,128]{2,1,0:T(8,128)(2,1)}, bf16[24,128,128]{2,1,0:T(8,128)(2,1)S(1)}, u32[]{:S(2)}, u32[]{:S(2)}) %collective-permute-start.13) | collective-permute-done | bytes 786464 | tf_op jit(solution)/shard_map/ppermute | solution.py:151
  138.0 1.7 %shard_map.99 = (f32[24,128,128]{2,1,0:T(8,128)S(1)}, f32[8,128]{1,0:T(8,128)S(1)}) custom-call(s32[32,3]{1,0:T(8,128)S(1)} %copy.134.table, f32[24,128,128]{2,1,0:T(8,128)S(1)} %copy-done.2, bf16[24,128,128]{2,1,0:T(8,128)(2,1)S(1)} %collective-permute-done.13.got, bf16[32,128,128]{2,1,0:T(8,128)(2,1)S(1)} %copy-done.1), custom_call_target="tpu_custom_call" | custom-call | flops 1 | bytes 1 | tf_op jit(solution)/shard_map/pallas_call | solution.py:706
  139.8 2.9 %collective-permute-done.16.one = bf16[8,128,128]{2,1,0:T(8,128)(2,1)S(1)} collective-permute-done((bf16[8,128,128]{2,1,0:T(8,128)(2,1)}, bf16[8,128,128]{2,1,0:T(8,128)(2,1)S(1)}, u32[]{:S(2)}, u32[]{:S(2)}) %collective-permute-start.16) | collective-permute-done | bytes 262176 | tf_op jit(solution)/shard_map/ppermute | solution.py:151
  142.7 3.2 %collective-permute-done.17.two = bf16[8,128,128]{2,1,0:T(8,128)(2,1)S(1)} collective-permute-done((bf16[8,128,128]{2,1,0:T(8,128)(2,1)}, bf16[8,128,128]{2,1,0:T(8,128)(2,1)S(1)}, u32[]{:S(2)}, u32[]{:S(2)}) %collective-permute-start.17) | collective-permute-done | bytes 262176 | tf_op jit(solution)/shard_map/ppermute | solution.py:151
  146.0 3.7 %collective-permute-done.15.last_got = bf16[8,128,128]{2,1,0:T(8,128)(2,1)S(1)} collective-permute-done((bf16[8,128,128]{2,1,0:T(8,128)(2,1)}, bf16[8,128,128]{2,1,0:T(8,128)(2,1)S(1)}, u32[]{:S(2)}, u32[]{:S(2)}) %collective-permute-start.15) | collective-permute-done | bytes 262176 | tf_op jit(solution)/shard_map/ppermute | solution.py:151
  149.7 2.0 %shard_map.101 = (f32[16,128,128]{2,1,0:T(8,128)S(1)}, f32[8,128]{1,0:T(8,128)S(1)}) custom-call(s32[32,3]{1,0:T(8,128)S(1)} %copy.135.table, f32[8,128]{1,0:T(8,128)S(1)} %get-tuple-element.89.sums_first, f32[8,128,128]{2,1,0:T(8,128)S(1)} %copy-done.3, bf16[8,128,128]{2,1,0:T(8,128)(2,1)S(1)} %collective-permute-done.15.last_got, ...), custom_call_target="tpu_custom_call" | custom-call | flops 1 | bytes 1 | tf_op jit(solution)/shard_map/pallas_call | solution.py:718
  152.2 2.2 %collective-permute-done.20 = f32[8,128]{1,0:T(8,128)S(1)} collective-permute-done((f32[8,128]{1,0:T(8,128)S(1)}, f32[8,128]{1,0:T(8,128)S(1)}, u32[]{:S(2)}, u32[]{:S(2)}) %collective-permute-start.20) | collective-permute-done | bytes 4128 | tf_op jit(solution)/shard_map/ppermute | solution.py:151
  154.3 0.7 collective-permute-start.21
  155.1 2.9 %collective-permute-done.21 = f32[16,128]{1,0:T(8,128)S(1)} collective-permute-done((f32[16,128]{1,0:T(8,128)S(1)}, f32[16,128]{1,0:T(8,128)S(1)}, u32[]{:S(2)}, u32[]{:S(2)}) %collective-permute-start.21) | collective-permute-done | bytes 8224 | tf_op jit(solution)/shard_map/ppermute | solution.py:151
  158.0 1.3 collective-permute-start.22
  159.3 3.1 %collective-permute-start.23 = (f32[32,128]{1,0:T(8,128)S(1)}, f32[32,128]{1,0:T(8,128)S(1)}, u32[]{:S(2)}, u32[]{:S(2)}) collective-permute-start(f32[32,128]{1,0:T(8,128)S(1)} %constant_dynamic-update-slice_fusion.sums), channel_id=1, source_target_pairs={{0,8},{1,9},{2,10},{3,11},{4,12},{5,13},{6,14},{7,15},{8,0},{9,1},... | collective-permute-start | bytes 49160 | tf_op jit(solution)/shard_map/ppermute | solution.py:151
  162.4 1.5 collective-permute-start.24
  163.9 3.6 %shard_map.102 = (f32[32,128,128]{2,1,0:T(8,128)}, f32[32,128,128]{2,1,0:T(8,128)S(1)}) custom-call(s32[32,2]{1,0:T(8,128)S(1)} %copy-done.5, f32[24,128,128]{2,1,0:T(8,128)S(1)} %get-tuple-element.87.first_own, f32[16,128,128]{2,1,0:T(8,128)S(1)} %get-tuple-element.93.late_own, f32[24,128,128]{2,1,0:T(8,128)S(1)} %collective-permute-done.18.first_sib, ...), custom_call_target="tpu_custom_call" | custom-call | flops 1 | bytes 1 | tf_op jit(solution)/shard_map/pallas_call | solution.py:728
  167.9 2.0 %shard_map.103 = (f32[32,128,128]{2,1,0:T(8,128)}, f32[1]{0:T(128)}) custom-call(f32[32,128]{1,0:T(8,128)S(1)} %constant_dynamic-update-slice_fusion.sums, f32[32,128]{1,0:T(8,128)S(1)} %collective-permute-done.22.near, f32[32,128]{1,0:T(8,128)S(1)} %collective-permute-done.23.far, f32[32,128]{1,0:T(8,128)S(1)} %collective-permute-done.24.across, ...), custom_call_target="tpu_custom_call" | custom-call | flops 1 | bytes 1 | tf_op jit(solution)/shard_map/pallas_call | solution.py:739
  (111 shorter events, 6.5 us)
Async XLA Ops:
  0.6 11.1 %collective-permute-start = (bf16[7,8,128,128]{3,2,1,0:T(8,128)(2,1)}, bf16[7,8,128,128]{3,2,1,0:T(8,128)(2,1)}, u32[]{:S(2)}, u32[]{:S(2)}) collective-permute-start(bf16[7,8,128,128]{3,2,1,0:T(8,128)(2,1)} %param.11), channel_id=1, source_target_pairs={{1,2},{2,1},{5,6},{6,5},{9,10},{10,9},{13,14},{14,13},{17,18},{18,... | collective-permute-start | bytes 5505032 | tf_op jit(solution)/shard_map/ppermute | solution.py:151
  2.5 9.2 %collective-permute-start.1 = (bf16[7,16]{1,0:T(8,128)(2,1)}, bf16[7,16]{1,0:T(8,128)(2,1)S(1)}, u32[]{:S(2)}, u32[]{:S(2)}) collective-permute-start(bf16[7,16]{1,0:T(8,128)(2,1)} %param.13), channel_id=1, source_target_pairs={{0,1},{1,0},{2,3},{3,2},{4,5},{5,4},{6,7},{7,6},{8,9},{9,8},{10,11... | collective-permute-start | bytes 680 | tf_op jit(solution)/shard_map/ppermute | solution.py:151
  11.7 31.0 %copy-start.10 = (bf16[7,16]{1,0:T(8,128)(2,1)S(1)}, bf16[7,16]{1,0:T(8,128)(2,1)}, u32[]{:S(2)}) copy-start(bf16[7,16]{1,0:T(8,128)(2,1)} %param.13) | copy-start | bytes 676
  13.4 66.5 %copy-start.6 = (bf16[7,8,128,128]{3,2,1,0:T(8,128)(2,1)}, bf16[7,8,128,128]{3,2,1,0:T(8,128)(2,1)S(1)}, u32[]{:S(2)}) copy-start(bf16[7,8,128,128]{3,2,1,0:T(8,128)(2,1)S(1)} %broadcast_select_fusion.1.left_mine) | copy-start | bytes 5505028
  13.4 37.1 %collective-permute-start.2 = (bf16[7,8,128,128]{3,2,1,0:T(8,128)(2,1)S(1)}, bf16[7,8,128,128]{3,2,1,0:T(8,128)(2,1)}, u32[]{:S(2)}, u32[]{:S(2)}) collective-permute-start(bf16[7,8,128,128]{3,2,1,0:T(8,128)(2,1)S(1)} %broadcast_select_fusion.1.left_mine), channel_id=1, source_target_pairs={{0,4},{1,5},{2,6},{3,7},{4,8},{5,9},{6,10},{7,11},{8,12},{9,13},{1... | collective-permute-start | bytes 5505032 | tf_op jit(solution)/shard_map/ppermute | solution.py:151
  18.2 32.3 %collective-permute-start.3 = (bf16[7,8,128,128]{3,2,1,0:T(8,128)(2,1)S(1)}, bf16[7,8,128,128]{3,2,1,0:T(8,128)(2,1)}, u32[]{:S(2)}, u32[]{:S(2)}) collective-permute-start(bf16[7,8,128,128]{3,2,1,0:T(8,128)(2,1)S(1)} %broadcast_select_fusion.1.left_mine), channel_id=1, source_target_pairs={{4,0},{5,1},{6,2},{7,3},{8,4},{9,5},{10,6},{11,7},{12,8},{13,9},{1... | collective-permute-start | bytes 5505032 | tf_op jit(solution)/shard_map/ppermute | solution.py:151
  19.5 24.1 %collective-permute-start.6 = (s32[3,32]{1,0:T(4,128)S(1)}, s32[3,32]{1,0:T(4,128)S(1)}, u32[]{:S(2)}, u32[]{:S(2)}) collective-permute-start(s32[3,32]{1,0:T(4,128)S(1)} %get-tuple-element.54), channel_id=1, source_target_pairs={{0,2},{1,3},{2,0},{3,1},{4,6},{5,7},{6,4},{7,5},{8,10},{9,11},{10,... | collective-permute-start | bytes 1160 | tf_op jit(solution)/shard_map/ppermute | solution.py:151
  36.3 9.7 %collective-permute-start.4 = (bf16[7,8,128,128]{3,2,1,0:T(8,128)(2,1)}, bf16[7,8,128,128]{3,2,1,0:T(8,128)(2,1)}, u32[]{:S(2)}, u32[]{:S(2)}) collective-permute-start(bf16[7,8,128,128]{3,2,1,0:T(8,128)(2,1)} %param.12), channel_id=1, source_target_pairs={{1,2},{2,1},{5,6},{6,5},{9,10},{10,9},{13,14},{14,13},{17,18},{18,... | collective-permute-start | bytes 5505032 | tf_op jit(solution)/shard_map/ppermute | solution.py:151
  38.2 12.3 %collective-permute-start.5 = (bf16[9,128,128]{2,1,0:T(8,128)(2,1)}, bf16[9,128,128]{2,1,0:T(8,128)(2,1)S(1)}, u32[]{:S(2)}, u32[]{:S(2)}) collective-permute-start(bf16[9,128,128]{2,1,0:T(8,128)(2,1)} %shard_map.94), channel_id=1, source_target_pairs={{0,4},{1,5},{2,6},{3,7},{12,8},{13,9},{14,10},{15,11},{16,20},{17,... | collective-permute-start | bytes 884744 | tf_op jit(solution)/shard_map/ppermute | solution.py:151
  45.2 0.7 copy-start.4
  45.9 33.4 %copy-start = (bf16[32,128,128]{2,1,0:T(8,128)(2,1)S(1)}, bf16[32,128,128]{2,1,0:T(8,128)(2,1)}, u32[]{:S(2)}) copy-start(bf16[32,128,128]{2,1,0:T(8,128)(2,1)} %wave.5) | copy-start | bytes 3145732
  50.5 68.6 %copy-start.8 = (bf16[9,128,128]{2,1,0:T(8,128)(2,1)}, bf16[9,128,128]{2,1,0:T(8,128)(2,1)S(1)}, u32[]{:S(2)}) copy-start(bf16[9,128,128]{2,1,0:T(8,128)(2,1)S(1)} %collective-permute-done.5.wave_own) | copy-start | bytes 884740
  50.5 29.4 %collective-permute-start.10 = (bf16[7,8,128,128]{3,2,1,0:T(8,128)(2,1)}, bf16[7,8,128,128]{3,2,1,0:T(8,128)(2,1)}, u32[]{:S(2)}, u32[]{:S(2)}) collective-permute-start(bf16[7,8,128,128]{3,2,1,0:T(8,128)(2,1)} %broadcast_select_fusion.right_mine), channel_id=1, source_target_pairs={{0,1},{1,0},{2,3},{3,2},{4,5},{5,4},{6,7},{7,6},{8,9},{9,8},{10,11... | collective-permute-start | bytes 5505032 | tf_op jit(solution)/shard_map/ppermute | solution.py:151
  63.9 49.8 %collective-permute-start.7 = (bf16[7,8,128,128]{3,2,1,0:T(8,128)(2,1)}, bf16[7,8,128,128]{3,2,1,0:T(8,128)(2,1)}, u32[]{:S(2)}, u32[]{:S(2)}) collective-permute-start(bf16[7,8,128,128]{3,2,1,0:T(8,128)(2,1)} %collective-permute-done.2.below), channel_id=1, source_target_pairs={{4,8},{5,9},{6,10},{7,11},{8,12},{9,13},{10,14},{11,15},{20,24},{2... | collective-permute-start | bytes 5505032 | tf_op jit(solution)/shard_map/ppermute | solution.py:151
  65.8 50.5 %collective-permute-start.8 = (bf16[7,8,128,128]{3,2,1,0:T(8,128)(2,1)}, bf16[7,8,128,128]{3,2,1,0:T(8,128)(2,1)}, u32[]{:S(2)}, u32[]{:S(2)}) collective-permute-start(bf16[7,8,128,128]{3,2,1,0:T(8,128)(2,1)} %collective-permute-done.3.above), channel_id=1, source_target_pairs={{4,0},{5,1},{6,2},{7,3},{8,4},{9,5},{10,6},{11,7},{20,16},{21,17},... | collective-permute-start | bytes 5505032 | tf_op jit(solution)/shard_map/ppermute | solution.py:151
  67.1 50.4 %collective-permute-start.9 = (bf16[7,8,128,128]{3,2,1,0:T(8,128)(2,1)}, bf16[7,8,128,128]{3,2,1,0:T(8,128)(2,1)}, u32[]{:S(2)}, u32[]{:S(2)}) collective-permute-start(bf16[7,8,128,128]{3,2,1,0:T(8,128)(2,1)} %broadcast_select_fusion.right_mine), channel_id=1, source_target_pairs={{0,4},{1,5},{2,6},{3,7},{12,8},{13,9},{14,10},{15,11},{16,20},{17,... | collective-permute-start | bytes 5505032 | tf_op jit(solution)/shard_map/ppermute | solution.py:151
  79.3 24.6 %collective-permute-start.12 = (bf16[32,128,128]{2,1,0:T(8,128)(2,1)S(1)}, bf16[32,128,128]{2,1,0:T(8,128)(2,1)}, u32[]{:S(2)}, u32[]{:S(2)}) collective-permute-start(bf16[32,128,128]{2,1,0:T(8,128)(2,1)S(1)} %copy-done), channel_id=1, source_target_pairs={{0,2},{1,3},{2,0},{3,1},{4,6},{5,7},{6,4},{7,5},{8,10},{9,11},{10,... | collective-permute-start | bytes 3145736 | tf_op jit(solution)/shard_map/ppermute | solution.py:151
  88.5 29.0 %collective-permute-start.11 = (bf16[9,128,128]{2,1,0:T(8,128)(2,1)S(1)}, bf16[9,128,128]{2,1,0:T(8,128)(2,1)S(1)}, u32[]{:S(2)}, u32[]{:S(2)}) collective-permute-start(bf16[9,128,128]{2,1,0:T(8,128)(2,1)S(1)} %collective-permute-done.5.wave_own), channel_id=1, source_target_pairs={{4,6},{5,7},{6,4},{7,5},{8,10},{9,11},{10,8},{11,9},{20,22},{21,23... | collective-permute-start | bytes 884744 | tf_op jit(solution)/shard_map/ppermute | solution.py:151
  117.5 2.2 %copy-start.9 = (bf16[9,128,128]{2,1,0:T(8,128)(2,1)}, bf16[9,128,128]{2,1,0:T(8,128)(2,1)S(1)}, u32[]{:S(2)}) copy-start(bf16[9,128,128]{2,1,0:T(8,128)(2,1)S(1)} %collective-permute-done.11.wave_other) | copy-start | bytes 884740
  117.5 2.2 %collective-permute-start.14 = (bf16[7,8,128,128]{3,2,1,0:T(8,128)(2,1)}, bf16[7,8,128,128]{3,2,1,0:T(8,128)(2,1)S(1)}, u32[]{:S(2)}, u32[]{:S(2)}) collective-permute-start(bf16[7,8,128,128]{3,2,1,0:T(8,128)(2,1)} %collective-permute-done.9.right_mine), channel_id=1, source_target_pairs={{4,5},{5,4},{6,7},{7,6},{8,9},{9,8},{10,11},{11,10},{20,21},{21,20... | collective-permute-start | bytes 5505032 | tf_op jit(solution)/shard_map/ppermute | solution.py:151
  119.1 18.6 %collective-permute-start.13 = (bf16[24,128,128]{2,1,0:T(8,128)(2,1)}, bf16[24,128,128]{2,1,0:T(8,128)(2,1)S(1)}, u32[]{:S(2)}, u32[]{:S(2)}) collective-permute-start(bf16[24,128,128]{2,1,0:T(8,128)(2,1)} %get-tuple-element.73), channel_id=1, source_target_pairs={{0,2},{1,3},{2,0},{3,1},{4,6},{5,7},{6,4},{7,5},{8,10},{9,11},{10,... | collective-permute-start | bytes 2359304 | tf_op jit(solution)/shard_map/ppermute | solution.py:151
  119.8 1.2 copy-start.7
  122.9 19.8 %collective-permute-start.16 = (bf16[8,128,128]{2,1,0:T(8,128)(2,1)}, bf16[8,128,128]{2,1,0:T(8,128)(2,1)S(1)}, u32[]{:S(2)}, u32[]{:S(2)}) collective-permute-start(bf16[8,128,128]{2,1,0:T(8,128)(2,1)} %get-tuple-element.79), channel_id=1, source_target_pairs={{4,0},{5,1},{6,2},{7,3},{8,12},{9,13},{10,14},{11,15},{20,16},{21,... | collective-permute-start | bytes 786440 | tf_op jit(solution)/shard_map/ppermute | solution.py:151
  124.9 13.1 %copy-start.1 = (bf16[32,128,128]{2,1,0:T(8,128)(2,1)S(1)}, bf16[32,128,128]{2,1,0:T(8,128)(2,1)}, u32[]{:S(2)}) copy-start(bf16[32,128,128]{2,1,0:T(8,128)(2,1)} %wave.5) | copy-start | bytes 3145732
  124.9 13.1 %copy-start.2 = (f32[24,128,128]{2,1,0:T(8,128)S(1)}, f32[24,128,128]{2,1,0:T(8,128)}, u32[]{:S(2)}) copy-start(f32[24,128,128]{2,1,0:T(8,128)} %get-tuple-element.72.own) | copy-start | bytes 4718596
  124.9 21.0 %collective-permute-start.17 = (bf16[8,128,128]{2,1,0:T(8,128)(2,1)}, bf16[8,128,128]{2,1,0:T(8,128)(2,1)S(1)}, u32[]{:S(2)}, u32[]{:S(2)}) collective-permute-start(bf16[8,128,128]{2,1,0:T(8,128)(2,1)} %get-tuple-element.92), channel_id=1, source_target_pairs={{4,2},{5,3},{6,0},{7,1},{8,14},{9,15},{10,12},{11,13},{20,18},{21,... | collective-permute-start | bytes 786440 | tf_op jit(solution)/shard_map/ppermute | solution.py:151
  137.7 12.0 %collective-permute-start.15 = (bf16[8,128,128]{2,1,0:T(8,128)(2,1)}, bf16[8,128,128]{2,1,0:T(8,128)(2,1)S(1)}, u32[]{:S(2)}, u32[]{:S(2)}) collective-permute-start(bf16[8,128,128]{2,1,0:T(8,128)(2,1)} %get-tuple-element.90), channel_id=1, source_target_pairs={{0,2},{1,3},{2,0},{3,1},{4,6},{5,7},{6,4},{7,5},{8,10},{9,11},{10,... | collective-permute-start | bytes 786440 | tf_op jit(solution)/shard_map/ppermute | solution.py:151
  139.7 24.1 %collective-permute-start.18 = (f32[24,128,128]{2,1,0:T(8,128)S(1)}, f32[24,128,128]{2,1,0:T(8,128)S(1)}, u32[]{:S(2)}, u32[]{:S(2)}) collective-permute-start(f32[24,128,128]{2,1,0:T(8,128)S(1)} %get-tuple-element.87.first_own), channel_id=1, source_target_pairs={{0,1},{1,0},{2,3},{3,2},{4,5},{5,4},{6,7},{7,6},{8,9},{9,8},{10,11... | collective-permute-start | bytes 4718600 | tf_op jit(solution)/shard_map/ppermute | solution.py:151
  142.7 7.0 %copy-start.3 = (f32[8,128,128]{2,1,0:T(8,128)S(1)}, f32[8,128,128]{2,1,0:T(8,128)}, u32[]{:S(2)}) copy-start(f32[8,128,128]{2,1,0:T(8,128)} %get-tuple-element.85.last_own) | copy-start | bytes 1572868
  146.0 17.9 %copy-start.5 = (s32[32,2]{1,0:T(8,128)S(1)}, s32[32,2]{1,0:T(8,128)}, u32[]{:S(2)}) copy-start(s32[32,2]{1,0:T(8,128)} %copy-done.4) | copy-start | bytes 772
  151.6 12.2 %collective-permute-start.19 = (f32[16,128,128]{2,1,0:T(8,128)S(1)}, f32[16,128,128]{2,1,0:T(8,128)S(1)}, u32[]{:S(2)}, u32[]{:S(2)}) collective-permute-start(f32[16,128,128]{2,1,0:T(8,128)S(1)} %get-tuple-element.93.late_own), channel_id=1, source_target_pairs={{0,1},{1,0},{2,3},{3,2},{4,5},{5,4},{6,7},{7,6},{8,9},{9,8},{10,11... | collective-permute-start | bytes 3145736 | tf_op jit(solution)/shard_map/ppermute | solution.py:151
  151.7 2.7 %collective-permute-start.20 = (f32[8,128]{1,0:T(8,128)S(1)}, f32[8,128]{1,0:T(8,128)S(1)}, u32[]{:S(2)}, u32[]{:S(2)}) collective-permute-start(f32[8,128]{1,0:T(8,128)S(1)} %get-tuple-element.95), channel_id=1, source_target_pairs={{0,1},{1,0},{2,3},{3,2},{4,5},{5,4},{6,7},{7,6},{8,9},{9,8},{10,11... | collective-permute-start | bytes 12296 | tf_op jit(solution)/shard_map/ppermute | solution.py:151
  154.3 3.7 %collective-permute-start.21 = (f32[16,128]{1,0:T(8,128)S(1)}, f32[16,128]{1,0:T(8,128)S(1)}, u32[]{:S(2)}, u32[]{:S(2)}) collective-permute-start(f32[16,128]{1,0:T(8,128)S(1)} %pad_maximum_fusion), channel_id=1, source_target_pairs={{0,2},{1,3},{2,0},{3,1},{4,6},{5,7},{6,4},{7,5},{8,10},{9,11},{10,... | collective-permute-start | bytes 24584 | tf_op jit(solution)/shard_map/ppermute | solution.py:151
  158.0 9.4 %collective-permute-start.22 = (f32[32,128]{1,0:T(8,128)S(1)}, f32[32,128]{1,0:T(8,128)S(1)}, u32[]{:S(2)}, u32[]{:S(2)}) collective-permute-start(f32[32,128]{1,0:T(8,128)S(1)} %constant_dynamic-update-slice_fusion.sums), channel_id=1, source_target_pairs={{0,4},{1,5},{2,6},{3,7},{4,0},{5,1},{6,2},{7,3},{8,12},{9,13},{10,... | collective-permute-start | bytes 49160 | tf_op jit(solution)/shard_map/ppermute | solution.py:151
  159.3 8.2 %collective-permute-start.23 = (f32[32,128]{1,0:T(8,128)S(1)}, f32[32,128]{1,0:T(8,128)S(1)}, u32[]{:S(2)}, u32[]{:S(2)}) collective-permute-start(f32[32,128]{1,0:T(8,128)S(1)} %constant_dynamic-update-slice_fusion.sums), channel_id=1, source_target_pairs={{0,8},{1,9},{2,10},{3,11},{4,12},{5,13},{6,14},{7,15},{8,0},{9,1},... | collective-permute-start | bytes 49160 | tf_op jit(solution)/shard_map/ppermute | solution.py:151
  162.4 5.5 %collective-permute-start.24 = (f32[32,128]{1,0:T(8,128)S(1)}, f32[32,128]{1,0:T(8,128)S(1)}, u32[]{:S(2)}, u32[]{:S(2)}) collective-permute-start(f32[32,128]{1,0:T(8,128)S(1)} %constant_dynamic-update-slice_fusion.sums), channel_id=1, source_target_pairs={{0,12},{1,13},{2,14},{3,15},{4,8},{5,9},{6,10},{7,11},{8,4},{9,5},... | collective-permute-start | bytes 49160 | tf_op jit(solution)/shard_map/ppermute | solution.py:151

commit v4 on v3

--- a/solution.py
+++ b/solution.py
@@ -141,6 +141,7 @@
 DIAGONAL = pairs_of(lambda z, y, c: (z, 1 - y, 1 - c), crossed)
 CORE = pairs_of(other_core)
 COLUMN = pairs_of(other_column)
+ACROSS = pairs_of(lambda z, y, c: (z, 1 - y, 1 - c))
 COLUMN_INNER = pairs_of(other_column, inner)
 GUEST = pairs_of(inward, outer)
 GUEST_BACK = pairs_of(outward, inner)
@@ -185,7 +186,16 @@
     @pl.loop(0, (high - low + step - 1) // step)
     def _(group):
         for n in range(step):
-            body(jnp.minimum(low + group * step + n, high - 1))
+            row = low + group * step + n
+            body(jnp.minimum(row, high - 1), (row < high).astype(jnp.float32))
+
+
+def folded(value):
+    return jnp.sum(value.reshape(-1, 8, 128), axis=0)
+
+
+def paired(found, wave, counted):
+    return folded(found * wave.astype(jnp.float32)) * counted
 
 
 def count_of(table, base, rows, stage):
@@ -196,9 +206,9 @@
 
 
 def near_kernel(
-    table, weights, wave_in, right_mine, right_sib, left_mine, below, above,
-    first, last, carried_out,
-    result, carried, wave, right, left, sems, carried_sems,
+    table, weights_in, wave_in, right_mine, right_sib, left_mine, below, above,
+    first, last, carried_out, correlation,
+    weights, result, carried, wave, right, left, sems, carried_sems,
 ):
     blocks = wave.shape[0]
     most = last.shape[0]
@@ -210,6 +220,7 @@
                 (wave_in, wave),
                 (right_mine, right.at[0]),
                 (right_sib, right.at[1]),
+                (weights_in, weights),
                 (left_mine, left.at[0]),
                 (below, left.at[1]),
                 (above, left.at[2]),
@@ -219,9 +230,10 @@
     for copy in copies:
         copy.start()
     result[...] = jnp.zeros_like(result)
+    correlation[...] = jnp.zeros_like(correlation)
     skipped = count_of(table, 0, blocks, -1)
     end = blocks - count_of(table, 0, blocks, 3)
-    for copy in copies[:3]:
+    for copy in copies[:4]:
         copy.wait()
 
     def carry(slot):
@@ -233,7 +245,7 @@
         at = slot - first_slots
         return pltpu.make_async_copy(carried.at[at], carried_out.at[at], carried_sems.at[at])
 
-    def keep(slot):
+    def keep(slot, _):
         carried[slot - first_slots] = carry(slot)
 
     grouped(end, blocks, 4, keep)
@@ -242,12 +254,13 @@
     def _(slot):
         written(slot).start()
 
-    for copy in copies[3:]:
+    for copy in copies[4:]:
         copy.wait()
 
-    def apply(slot):
+    def apply(slot, counted):
         found = applied(left[table[slot, 0], :, table[slot, 2]], carry(slot))
         result[slot] = found.astype(result.dtype)
+        correlation[...] += paired(found, wave[table[slot, 1]], counted)
 
     grouped(skipped, end, 4, apply)
     outs = [
@@ -267,9 +280,9 @@
 
 
 def guest_kernel(
-    flags, table, weights, below, above, wave_own, wave_other, right_mine, right_sib,
-    own_out, other_out,
-    wave, right, left, sems,
+    flags, table, weights_in, below, above, wave_own, wave_other, right_mine, right_sib,
+    own_out, other_out, correlation,
+    weights, wave, right, left, sems,
 ):
     half = own_out.shape[0]
     counts = [count_of(table, part * half, half, 3) for part in range(2)]
@@ -281,6 +294,7 @@
                 (right_sib, right.at[1]),
                 (wave_own.at[pl.ds(0, half)], wave.at[pl.ds(0, half)]),
                 (wave_other.at[pl.ds(0, half)], wave.at[pl.ds(half, half)]),
+                (weights_in, weights),
             )
         )
     ]
@@ -293,6 +307,7 @@
 
     own_out[...] = jnp.zeros_like(own_out)
     other_out[...] = jnp.zeros_like(other_out)
+    correlation[...] = jnp.zeros_like(correlation)
 
     @pl.when(counts[0] + counts[1] > 0)
     def _():
@@ -302,7 +317,7 @@
 
     for part, target in enumerate((own_out, other_out)):
 
-        def apply(row):
+        def apply(row, counted):
             carried = carried_of(
                 wave[row],
                 right[flags[1 + part], :, table[row, 4]],
@@ -310,14 +325,15 @@
             )
             result = applied(left[:, table[row, 2]], carried)
             target[row - part * half] = result.astype(target.dtype)
+            correlation[...] += paired(result, wave[row], counted)
 
         grouped(part * half, part * half + counts[part], 4, apply)
 
 
 def far_kernel(
-    flags, table, carried_own, carried_other, below, above, own, other,
-    own_out, other_out,
-    held, left, sems, more_sems,
+    flags, table, carried_own, carried_other, below, above, own, other, wave_own, wave_other,
+    own_out, other_out, correlation,
+    held, wave, left, sems, wave_sems, more_sems,
 ):
     half = own_out.shape[0]
     lows = [half - count_of(table, part * half, half, 3) for part in range(2)]
@@ -328,13 +344,15 @@
     ]
     for copy in kept:
         copy.start()
-    for part, carried in enumerate((carried_own, carried_other)):
+    for part, (carried, waves) in enumerate(((carried_own, wave_own), (carried_other, wave_other))):
 
         @pl.loop(lows[part], half)
         def _(slot):
             row = part * half + slot
             pltpu.make_async_copy(carried.at[slot], held.at[row], sems.at[row]).start()
-
+            pltpu.make_async_copy(waves.at[table[row, 1]], wave.at[row], wave_sems.at[row]).start()
+
+    correlation[...] = jnp.zeros_like(correlation)
     for copy in kept:
         copy.wait()
     pltpu.make_async_copy(above, left, more_sems.at[0]).wait()
@@ -345,10 +363,13 @@
         def _(slot):
             row = part * half + slot
             pltpu.make_async_copy(carried.at[slot], held.at[row], sems.at[row]).wait()
-
-        def apply(slot):
+            pltpu.make_async_copy(wave_own.at[0], wave.at[row], wave_sems.at[row]).wait()
+
+        def apply(slot, counted):
             row = part * half + slot
-            target[slot] = applied(left[:, table[row, 2]], held[row]).astype(target.dtype)
+            result = applied(left[:, table[row, 2]], held[row])
+            target[slot] = result.astype(target.dtype)
+            correlation[...] += paired(result, wave[row], counted)
 
         grouped(lows[part], half, 4, apply)
 
@@ -360,10 +381,6 @@
     @pl.loop(0, slots)
     def _(slot):
         out[slot] = own[table[slot, 1]]
-
-
-def folded(value):
-    return jnp.sum(value.reshape(-1, 8, 128), axis=0)
 
 
 def first_kernel(table, own, got, wave, whole, sums):
@@ -401,7 +418,9 @@
     out[...] = one[...].astype(out.dtype) + two[...].astype(out.dtype)
 
 
-def late_kernel(table, sums_first, last_own, last_got, guest_full, wave, late, sums):
+def late_kernel(
+    table, sums_first, last_own, last_got, guest_full, wave, map_a, map_b, map_c, map_d, late, sums
+):
     blocks = wave.shape[0]
     most = last_own.shape[0]
     zero = jnp.zeros((8, 128), jnp.float32)
@@ -423,11 +442,12 @@
         return total + folded(residual * residual)
 
     resid = jnp.sum(lax.fori_loop(0, count, rest, zero), keepdims=True)
-    first = [sums_first[n : n + 1, 0:1] for n in range(3)]
-    sums[...] = lined(*merged(first, (norm, correlation, resid)))
-
-
-def place_kernel(table, first_own, late_own, first_sib, late_sib, image, kept, sem):
+    first = [sums_first[n : n + 1, 0:1] for n in range(4)]
+    exact = jnp.sum(map_a[...] + map_b[...] + map_c[...] + map_d[...], keepdims=True)
+    sums[...] = lined(*merged(first, (norm, correlation, resid, exact)))
+
+
+def place_kernel(table, first_own, late_own, first_sib, late_sib, kept):
     @pl.loop(0, kept.shape[0])
     def _(k):
         for code, source in enumerate((first_own, late_own, first_sib, late_sib)):
@@ -436,29 +456,29 @@
             def _():
                 kept[k] = source[table[k, 1]]
 
-    copy = pltpu.make_async_copy(kept, image, sem.at[0])
-    copy.start()
-    copy.wait()
-
-
-def correction_kernel(entries, sums, near, far, across, image, wave, out, ratio, result, sems):
-    chunks = sems.shape[0]
+
+def correction_kernel(
+    entries, sums, near, far, across, image, wave, image_out, out, ratio, result, sems
+):
+    chunks = sems.shape[0] - 1
     size = image.shape[0] // chunks
 
     def total(ref):
-        parts = [[ref[base + n : base + n + 1, 0:1] for n in range(3)] for base in (0, 8, 16, 24)]
+        parts = [[ref[base + n : base + n + 1, 0:1] for n in range(4)] for base in (0, 8, 16, 24)]
         return merged(merged(*parts[:2]), merged(*parts[2:]))
 
     whole = merged(merged(total(sums), total(near)), merged(total(far), total(across)))
-    rayleigh = whole[1] / whole[0]
-    scale = lax.rsqrt(whole[2] / entries + 1e-06)
+    rayleigh = whole[3] / whole[0]
+    gap = ratio_of(whole[0], whole[1]) - rayleigh
+    scale = lax.rsqrt((whole[2] + gap * gap * whole[0]) / entries + 1e-06)
     ratio[0] = rayleigh[0, 0]
-    copies = []
+    copies = [pltpu.make_async_copy(image, image_out, sems.at[chunks])]
+    copies[0].start()
     for n in range(chunks):
         part = pl.ds(n * size, size)
         result[part] = (image[part] - rayleigh * wave[part].astype(jnp.float32)) * scale
         copies.append(pltpu.make_async_copy(result.at[part], out.at[part], sems.at[n]))
-        copies[n].start()
+        copies[-1].start()
     for copy in copies:
         copy.wait()
 
@@ -472,7 +492,7 @@
     norm = one[0] + two[0]
     gap = ratio_of(one[0], one[1]) - ratio_of(two[0], two[1])
     shared = low * jnp.where(norm > 0, high / jnp.where(norm > 0, norm, 1.0), 0.0)
-    return norm, one[1] + two[1], one[2] + two[2] + gap * gap * shared
+    return norm, one[1] + two[1], one[2] + two[2] + gap * gap * shared, one[3] + two[3]
 
 
 def ranks(key):
@@ -578,7 +598,7 @@
         [SMEM, VMEM, VMEM],
         VMEM,
         [],
-    )(guest_table, wavefunction, tiled(guest_table))
+    )(guest_table, after(wavefunction, info_other), tiled(guest_table))
     wave_guest = move(after(picked, left_mine), GUEST)
 
     infos = jnp.stack([info, info_other, info])
@@ -629,6 +649,8 @@
     right_guest = hop(right_mine, inward, outer)
     wave_other = move(after(wavefunction, right_mine), COLUMN)
     right_sib = move(right_mine, CORE)
+    map_shape = jax.ShapeDtypeStruct((8, 128), f32)
+
     def near(relation, blocks_of, kind):
         return call(
             near_kernel,
@@ -636,16 +658,18 @@
                 jax.ShapeDtypeStruct((first_slots,) + square, kind),
                 jax.ShapeDtypeStruct((most,) + square, kind),
                 jax.ShapeDtypeStruct((most, dim, terms * dim), bf16),
+                map_shape,
             ),
-            [SMEM, VMEM] + [HBM] * 6,
-            (HBM, HBM, HBM),
+            [SMEM] + [HBM] * 7,
+            (HBM, HBM, HBM, VMEM),
             [
+                pltpu.VMEM(weights.shape, f32),
                 pltpu.VMEM((blocks,) + square, kind),
                 pltpu.VMEM((most, dim, terms * dim), bf16),
                 pltpu.VMEM((blocks,) + square, bf16),
                 pltpu.VMEM((2,) + env, bf16),
                 pltpu.VMEM((3,) + env, bf16),
-                pltpu.SemaphoreType.DMA((8,)),
+                pltpu.SemaphoreType.DMA((9,)),
                 pltpu.SemaphoreType.DMA((most,)),
             ],
         )(
@@ -653,8 +677,8 @@
             left_mine, below, above,
         )
 
-    own, own_last, carried_own = near(0, wavefunction, f32)
-    other, other_last, carried_other = near(1, wave_other, bf16)
+    own, own_last, carried_own, map_own = near(0, wavefunction, f32)
+    other, other_last, carried_other, map_other = near(1, wave_other, bf16)
     wave_guest_other = move(after(wave_guest, own), COLUMN_INNER)
     held = (below_two, above_two, right_guest, wave_guest_other)
     held += (own, own_last, carried_own, other, other_last, carried_other)
@@ -669,38 +693,42 @@
 
     last = jax.ShapeDtypeStruct((most,) + square, f32)
     last_sent = jax.ShapeDtypeStruct((most,) + square, bf16)
-    guest_own, guest_other = call(
+    guest_own, guest_other, map_guest = call(
         guest_kernel,
-        (last_sent, last_sent),
-        [SMEM] * 2 + [VMEM] + [HBM] * 6,
-        (VMEM,) * 2,
+        (last_sent, last_sent, map_shape),
+        [SMEM] * 2 + [HBM] * 7,
+        (VMEM,) * 3,
         [
+            pltpu.VMEM(weights.shape, f32),
             pltpu.VMEM((2 * most,) + square, bf16),
             pltpu.VMEM((2,) + env, bf16),
             pltpu.VMEM(env, bf16),
-            pltpu.SemaphoreType.DMA((5,)),
+            pltpu.SemaphoreType.DMA((6,)),
         ],
+        vmem=VMEM_SMALL,
     )(
         flags, guest_got, weights, below_two, above_two,
         wave_guest, wave_guest_other, right_guest, right_guest_sib,
     )
     guest_straight = move(guest_own, GUEST_BACK)
     guest_crossed = move(guest_other, GUEST_BACK_CROSSED)
-    last_own, last_other = call(
+    last_own, last_other, map_far = call(
         far_kernel,
-        (last, last_sent),
-        [SMEM] * 2 + [HBM] * 6,
-        (VMEM,) * 2,
+        (last, last_sent, map_shape),
+        [SMEM] * 2 + [HBM] * 8,
+        (VMEM,) * 3,
         [
             pltpu.VMEM((2 * most, dim, terms * dim), bf16),
+            pltpu.VMEM((2 * most,) + square, bf16),
             pltpu.VMEM(env, bf16),
+            pltpu.SemaphoreType.DMA((2 * most,)),
             pltpu.SemaphoreType.DMA((2 * most,)),
             pltpu.SemaphoreType.DMA((3,)),
         ],
         2**37,
     )(
         flags, after(far_table, guest_own), carried_own, carried_other, below_two, above_two,
-        own_last, other_last,
+        own_last, other_last, wavefunction, wave_other,
     )
     last_got = move(last_other, COLUMN)
     first_own, sums_first = call(
@@ -718,30 +746,32 @@
     late, sums = call(
         late_kernel,
         (jax.ShapeDtypeStruct((2 * most,) + square, f32), jax.ShapeDtypeStruct((8, 128), f32)),
-        [SMEM] + [VMEM] * 5,
+        [SMEM] + [VMEM] * 9,
         (VMEM, VMEM),
         [],
         vmem=VMEM_SMALL,
-    )(late_table, sums_first, last_own, last_got, guest_full, wavefunction)
+    )(
+        late_table, sums_first, last_own, last_got, guest_full, wavefunction,
+        map_own, map_other, map_guest, map_far,
+    )
     late_sib = move(late, CORE)
     image_shape = jax.ShapeDtypeStruct((blocks,) + square, f32)
-    image, kept = call(
+    kept = call(
         place_kernel,
-        (image_shape, image_shape),
+        image_shape,
         [SMEM] + [VMEM] * 4,
-        (HBM, VMEM),
-        [pltpu.SemaphoreType.DMA((1,))],
+        VMEM,
+        [],
         vmem=VMEM_SMALL,
     )(sources, first_own, late, first_sib, late_sib)
-    for pairs in (CORE, COLUMN):
-        sums = jnp.concatenate([sums, move(sums, pairs)])
+    sums = jnp.concatenate([sums] + [move(sums, pairs) for pairs in (CORE, COLUMN, ACROSS)])
     sums = [sums] + [move(sums, pairs_of(lambda z, y, c: (z ^ n, y, c))) for n in (1, 2, 3)]
-    correction, rayleigh = call(
+    image, correction, rayleigh = call(
         functools.partial(correction_kernel, blocks * 8 * dim * dim),
-        (image_shape, jax.ShapeDtypeStruct((1,), f32)),
+        (image_shape, image_shape, jax.ShapeDtypeStruct((1,), f32)),
         [VMEM] * 6,
-        (HBM, SMEM),
-        [pltpu.VMEM((blocks,) + square, f32), pltpu.SemaphoreType.DMA((8,))],
+        (HBM, HBM, SMEM),
+        [pltpu.VMEM((blocks,) + square, f32), pltpu.SemaphoreType.DMA((9,))],
         vmem=VMEM_SMALL,
     )(*sums, kept, wavefunction)
     return image, correction, rayleigh

time: 171 us -> 166 us (0.971)
  starting transfers between devices: 75 us -> 70 us
  waiting for transfers between devices: 41.1 us -> 43.7 us
    ppermute x25 -> x26, starting transfers between devices: 75 us -> 70 us  [move(): return lax.ppermute(array, BOTH, pairs)]
    ppermute x25 -> x26, waiting for transfers between devices: 41.1 us -> 43.7 us  [move(): return lax.ppermute(array, BOTH, pairs)]
    pallas_call x3, Pallas kernels: 11 us -> 9.05 us  [the longest x1 5.16 us: on_device(): call(far_kernel, (last, last_sent, map_shape), [SMEM] * 2 + [HBM] * 8, (V...]
  transfers between devices with their start and end apart: 25 -> 26, of which waited for: 11 -> 12; matrix products, arithmetic and copies ran while one was open for 7% -> 7% of each run, Pallas kernels for 21% -> 20%
where the time goes in v4:
time: 166 us; the launch traced here: 165 us
  starting transfers between devices  70 us (42%)
  waiting for transfers between devices  43.7 us (26%)
  Pallas kernels  36.5 us (22%)
  other arithmetic  7.45 us (4%)
  local copies, waits for them, and re-layouts  5.46 us (3%)
    ppermute x26, starting transfers between devices, move(): return lax.ppermute(array, BOTH, pairs)  70 us
    ppermute x26, waiting for transfers between devices, move(): return lax.ppermute(array, BOTH, pairs)  43.7 us
    pallas_call x2, Pallas kernels, near(): call(near_kernel, (jax.ShapeDtypeStruct((first_slots,) + square, kind), j...  18.8 us
    pallas_call x1, Pallas kernels, on_device(): call(far_kernel, (last, last_sent, map_shape), [SMEM] * 2 + [HBM] * 8, (V...  5.16 us
    select_n x2, other arithmetic, mine_of(): return jnp.where(y == c, own, swapped)  4.71 us
  transfers between devices with their start and end apart: 26, of which 12 were waited for; matrix products, arithmetic and copies ran while one was open for 7% of the time, Pallas kernels for 20%

profile of v4, /device:TPU:0, one launch (start us, length us, event | category | flops | bytes accessed | tf_op | source)
XLA Modules:
  0.0 165.3 jit_solution(12765507318518282613)
XLA Ops:
  0.6 1.9 %collective-permute-start = (bf16[7,8,128,128]{3,2,1,0:T(8,128)(2,1)}, bf16[7,8,128,128]{3,2,1,0:T(8,128)(2,1)}, u32[]{:S(2)}, u32[]{:S(2)}) collective-permute-start(bf16[7,8,128,128]{3,2,1,0:T(8,128)(2,1)} %param.11), channel_id=1, source_target_pairs={{1,2},{2,1},{5,6},{6,5},{9,10},{10,9},{13,14},{14,13},{17,18},{18,... | collective-permute-start | bytes 5505032 | tf_op jit(solution)/shard_map/ppermute | solution.py:152
  2.6 3.1 %collective-permute-start.1 = (bf16[7,16]{1,0:T(8,128)(2,1)}, bf16[7,16]{1,0:T(8,128)(2,1)S(1)}, u32[]{:S(2)}, u32[]{:S(2)}) collective-permute-start(bf16[7,16]{1,0:T(8,128)(2,1)} %param.13), channel_id=1, source_target_pairs={{0,1},{1,0},{2,3},{3,2},{4,5},{5,4},{6,7},{7,6},{8,9},{9,8},{10,11... | collective-permute-start | bytes 680 | tf_op jit(solution)/shard_map/ppermute | solution.py:152
  5.7 0.7 subtract_bitcast_fusion
  6.4 0.7 pad_add_fusion
  7.4 0.7 stack.107
  8.3 0.7 fusion.39
  9.7 1.7 %broadcast_select_fusion.1.left_mine = bf16[7,8,128,128]{3,2,1,0:T(8,128)(2,1)S(1)} fusion(bf16[7,8,128,128]{3,2,1,0:T(8,128)(2,1)} %param.11, bf16[7,8,128,128]{3,2,1,0:T(8,128)(2,1)} %collective-permute-done, pred[]{:T(512)} %eq.285), kind=kLoop, calls=%fused_computation.1 | loop fusion | flops 917504 | bytes 5505025 | tf_op jit(solution)/shard_map/jit(_where)/select_n | solution.py:545
  11.4 4.7 %collective-permute-start.2 = (bf16[7,8,128,128]{3,2,1,0:T(8,128)(2,1)S(1)}, bf16[7,8,128,128]{3,2,1,0:T(8,128)(2,1)}, u32[]{:S(2)}, u32[]{:S(2)}) collective-permute-start(bf16[7,8,128,128]{3,2,1,0:T(8,128)(2,1)S(1)} %broadcast_select_fusion.1.left_mine), channel_id=1, source_target_pairs={{0,4},{1,5},{2,6},{3,7},{4,8},{5,9},{6,10},{7,11},{8,12},{9,13},{1... | collective-permute-start | bytes 5505032 | tf_op jit(solution)/shard_map/ppermute | solution.py:152
  16.1 1.3 collective-permute-start.3
  17.4 18.8 %collective-permute-start.5 = (s32[3,32]{1,0:T(4,128)S(1)}, s32[3,32]{1,0:T(4,128)S(1)}, u32[]{:S(2)}, u32[]{:S(2)}) collective-permute-start(s32[3,32]{1,0:T(4,128)S(1)} %get-tuple-element.54), channel_id=1, source_target_pairs={{0,2},{1,3},{2,0},{3,1},{4,6},{5,7},{6,4},{7,5},{8,10},{9,11},{10,... | collective-permute-start | bytes 1160 | tf_op jit(solution)/shard_map/ppermute | solution.py:152
  36.2 1.9 %collective-permute-start.4 = (bf16[7,8,128,128]{3,2,1,0:T(8,128)(2,1)}, bf16[7,8,128,128]{3,2,1,0:T(8,128)(2,1)}, u32[]{:S(2)}, u32[]{:S(2)}) collective-permute-start(bf16[7,8,128,128]{3,2,1,0:T(8,128)(2,1)} %param.12), channel_id=1, source_target_pairs={{1,2},{2,1},{5,6},{6,5},{9,10},{10,9},{13,14},{14,13},{17,18},{18,... | collective-permute-start | bytes 5505032 | tf_op jit(solution)/shard_map/ppermute | solution.py:152
  38.3 0.6 copy.161
  40.2 2.0 %shard_map.94 = bf16[9,128,128]{2,1,0:T(8,128)(2,1)} custom-call(s32[8,6]{1,0:T(8,128)} %get-tuple-element.140.table, bf16[32,128,128]{2,1,0:T(8,128)(2,1)} %wave.5, bf16[1,128,128]{2,1,0:T(8,128)(2,1)} %pad_bitcast_fusion.facts), custom_call_target="tpu_custom_call" | custom-call | flops 1 | bytes 1 | tf_op jit(solution)/shard_map/pallas_call | solution.py:595
  42.5 4.6 %collective-permute-start.6 = (bf16[9,128,128]{2,1,0:T(8,128)(2,1)}, bf16[9,128,128]{2,1,0:T(8,128)(2,1)S(1)}, u32[]{:S(2)}, u32[]{:S(2)}) collective-permute-start(bf16[9,128,128]{2,1,0:T(8,128)(2,1)} %shard_map.94), channel_id=1, source_target_pairs={{0,4},{1,5},{2,6},{3,7},{12,8},{13,9},{14,10},{15,11},{16,20},{17,... | collective-permute-start | bytes 884744 | tf_op jit(solution)/shard_map/ppermute | solution.py:152
  47.9 3.0 %broadcast_select_fusion.right_mine = bf16[7,8,128,128]{3,2,1,0:T(8,128)(2,1)} fusion(bf16[7,8,128,128]{3,2,1,0:T(8,128)(2,1)} %param.12, bf16[7,8,128,128]{3,2,1,0:T(8,128)(2,1)} %collective-permute-done.4, pred[]{:T(512)} %eq.285), kind=kLoop, calls=%fused_computation | loop fusion | flops 917504 | bytes 5505025 | tf_op jit(solution)/shard_map/jit(_where)/select_n | solution.py:545
  50.9 3.9 %collective-permute-done.6.wave_own = bf16[9,128,128]{2,1,0:T(8,128)(2,1)S(1)} collective-permute-done((bf16[9,128,128]{2,1,0:T(8,128)(2,1)}, bf16[9,128,128]{2,1,0:T(8,128)(2,1)S(1)}, u32[]{:S(2)}, u32[]{:S(2)}) %collective-permute-start.6) | collective-permute-done | bytes 294944 | tf_op jit(solution)/shard_map/ppermute | solution.py:152
  54.9 7.7 %collective-permute-start.10 = (bf16[7,8,128,128]{3,2,1,0:T(8,128)(2,1)}, bf16[7,8,128,128]{3,2,1,0:T(8,128)(2,1)}, u32[]{:S(2)}, u32[]{:S(2)}) collective-permute-start(bf16[7,8,128,128]{3,2,1,0:T(8,128)(2,1)} %broadcast_select_fusion.right_mine), channel_id=1, source_target_pairs={{0,1},{1,0},{2,3},{3,2},{4,5},{5,4},{6,7},{7,6},{8,9},{9,8},{10,11... | collective-permute-start | bytes 5505032 | tf_op jit(solution)/shard_map/ppermute | solution.py:152
  62.5 0.8 collective-permute-start.7
  63.3 1.3 collective-permute-start.8
  64.6 11.5 %collective-permute-start.9 = (bf16[7,8,128,128]{3,2,1,0:T(8,128)(2,1)}, bf16[7,8,128,128]{3,2,1,0:T(8,128)(2,1)}, u32[]{:S(2)}, u32[]{:S(2)}) collective-permute-start(bf16[7,8,128,128]{3,2,1,0:T(8,128)(2,1)} %broadcast_select_fusion.right_mine), channel_id=1, source_target_pairs={{0,4},{1,5},{2,6},{3,7},{12,8},{13,9},{14,10},{15,11},{16,20},{17,... | collective-permute-start | bytes 5505032 | tf_op jit(solution)/shard_map/ppermute | solution.py:152
  76.7 9.5 %shard_map.95 = (f32[24,128,128]{2,1,0:T(8,128)}, f32[8,128,128]{2,1,0:T(8,128)}, bf16[8,128,896]{2,1,0:T(8,128)(2,1)}, f32[8,128]{1,0:T(8,128)}) custom-call(s32[32,6]{1,0:T(8,128)} %get-tuple-element.120.table, f32[16,896]{1,0:T(8,128)} %bitcast.117, bf16[32,128,128]{2,1,0:T(8,128)(2,1)} %wave.5, bf16[7,8,128,128]{3,2,1,0:T(8,128)(2,1)} %broadcast_select_fusion.right_mine, ...), custom_call_target="tpu_custom_call" | custom-call | flops 1 | bytes 1 | tf_op jit(solution)/shard_map/pallas_call | solution.py:655
  86.2 0.7 collective-permute-start.11
  86.9 13.8 %collective-permute-done.12.wave_in.wave_other = bf16[32,128,128]{2,1,0:T(8,128)(2,1)} collective-permute-done((bf16[32,128,128]{2,1,0:T(8,128)(2,1)S(1)}, bf16[32,128,128]{2,1,0:T(8,128)(2,1)}, u32[]{:S(2)}, u32[]{:S(2)}) %collective-permute-start.12) | collective-permute-done | bytes 1048608 | tf_op jit(solution)/shard_map/ppermute | solution.py:152
  100.7 9.4 %shard_map.96 = (bf16[24,128,128]{2,1,0:T(8,128)(2,1)}, bf16[8,128,128]{2,1,0:T(8,128)(2,1)}, bf16[8,128,896]{2,1,0:T(8,128)(2,1)}, f32[8,128]{1,0:T(8,128)}) custom-call(s32[32,6]{1,0:T(8,128)} %get-tuple-element.119.table, f32[16,896]{1,0:T(8,128)} %bitcast.118, bf16[32,128,128]{2,1,0:T(8,128)(2,1)} %collective-permute-done.12.wave_in.wave_other, ...), custom_call_target="tpu_custom_call" | custom-call | flops 1 | bytes 1 | tf_op jit(solution)/shard_map/pallas_call | solution.py:655
  110.1 3.0 %collective-permute-done.8.above = bf16[7,8,128,128]{3,2,1,0:T(8,128)(2,1)} collective-permute-done((bf16[7,8,128,128]{3,2,1,0:T(8,128)(2,1)}, bf16[7,8,128,128]{3,2,1,0:T(8,128)(2,1)}, u32[]{:S(2)}, u32[]{:S(2)}) %collective-permute-start.8) | collective-permute-done | bytes 1835040 | tf_op jit(solution)/shard_map/ppermute | solution.py:152
  113.2 1.2 collective-permute-done.9.right_mine
  114.3 1.9 %collective-permute-start.14 = (bf16[7,8,128,128]{3,2,1,0:T(8,128)(2,1)}, bf16[7,8,128,128]{3,2,1,0:T(8,128)(2,1)}, u32[]{:S(2)}, u32[]{:S(2)}) collective-permute-start(bf16[7,8,128,128]{3,2,1,0:T(8,128)(2,1)} %collective-permute-done.9.right_mine), channel_id=1, source_target_pairs={{4,5},{5,4},{6,7},{7,6},{8,9},{9,8},{10,11},{11,10},{20,21},{21,20... | collective-permute-start | bytes 5505032 | tf_op jit(solution)/shard_map/ppermute | solution.py:152
  116.5 1.7 %shard_map.97 = (bf16[8,128,128]{2,1,0:T(8,128)(2,1)}, bf16[8,128,128]{2,1,0:T(8,128)(2,1)S(1)}, f32[8,128]{1,0:T(8,128)S(1)}) custom-call(s32[3]{0:T(128)S(1)} %add_convert_fusion.4.flags, s32[16,6]{1,0:T(8,128)S(1)} %maximum_convert_fusion.table, f32[16,896]{1,0:T(8,128)S(1)} %bitcast.119, bf16[7,8,128,128]{3,2,1,0:T(8,128)(2,1)S(1)} %collective-permute-done.7.below, ...), custom_call_target="tpu_custom_call" | custom-call | flops 1 | bytes 1 | tf_op jit(solution)/shard_map/pallas_call | solution.py:696
  118.2 0.7 copy-done.12
  118.9 1.3 collective-permute-start.16
  120.2 0.7 copy.133.table
  120.9 1.5 collective-permute-start.17
  122.5 5.2 %shard_map.98 = (f32[8,128,128]{2,1,0:T(8,128)}, bf16[8,128,128]{2,1,0:T(8,128)(2,1)}, f32[8,128]{1,0:T(8,128)}) custom-call(s32[3]{0:T(128)} %copy-done.11, s32[16,6]{1,0:T(8,128)} %copy.133.table, bf16[8,128,896]{2,1,0:T(8,128)(2,1)} %get-tuple-element.83.carried_own, bf16[8,128,896]{2,1,0:T(8,128)(2,1)} %get-tuple-element.84.carried_other, ...), custom_call_target="tpu_custom_call" | custom-call | flops 137438953472 | bytes 1 | tf_op jit(solution)/shard_map/pallas_call | solution.py:715
  127.6 7.5 %collective-permute-done.13.got = bf16[24,128,128]{2,1,0:T(8,128)(2,1)} collective-permute-done((bf16[24,128,128]{2,1,0:T(8,128)(2,1)}, bf16[24,128,128]{2,1,0:T(8,128)(2,1)}, u32[]{:S(2)}, u32[]{:S(2)}) %collective-permute-start.13) | collective-permute-done | bytes 786464 | tf_op jit(solution)/shard_map/ppermute | solution.py:152
  135.5 1.9 %shard_map.99 = (f32[24,128,128]{2,1,0:T(8,128)S(1)}, f32[8,128]{1,0:T(8,128)S(1)}) custom-call(s32[32,3]{1,0:T(8,128)S(1)} %copy.134.table, f32[24,128,128]{2,1,0:T(8,128)S(1)} %copy-done.3, bf16[24,128,128]{2,1,0:T(8,128)(2,1)} %collective-permute-done.13.got, bf16[32,128,128]{2,1,0:T(8,128)(2,1)S(1)} %copy-done.1), custom_call_target="tpu_custom_call" | custom-call | flops 1 | bytes 1 | tf_op jit(solution)/shard_map/pallas_call | solution.py:734
  137.5 1.1 collective-permute-done.16.one
  138.6 4.5 %collective-permute-done.17.two = bf16[8,128,128]{2,1,0:T(8,128)(2,1)S(1)} collective-permute-done((bf16[8,128,128]{2,1,0:T(8,128)(2,1)}, bf16[8,128,128]{2,1,0:T(8,128)(2,1)S(1)}, u32[]{:S(2)}, u32[]{:S(2)}) %collective-permute-start.17) | collective-permute-done | bytes 262176 | tf_op jit(solution)/shard_map/ppermute | solution.py:152
  143.1 3.9 %collective-permute-done.15.last_got = bf16[8,128,128]{2,1,0:T(8,128)(2,1)S(1)} collective-permute-done((bf16[8,128,128]{2,1,0:T(8,128)(2,1)}, bf16[8,128,128]{2,1,0:T(8,128)(2,1)S(1)}, u32[]{:S(2)}, u32[]{:S(2)}) %collective-permute-start.15) | collective-permute-done | bytes 262176 | tf_op jit(solution)/shard_map/ppermute | solution.py:152
  147.1 2.0 %shard_map.101 = (f32[16,128,128]{2,1,0:T(8,128)S(1)}, f32[8,128]{1,0:T(8,128)S(1)}) custom-call(s32[32,3]{1,0:T(8,128)S(1)} %copy.135.table, f32[8,128]{1,0:T(8,128)S(1)} %get-tuple-element.89.sums_first, f32[8,128,128]{2,1,0:T(8,128)S(1)} %copy-done.5, bf16[8,128,128]{2,1,0:T(8,128)(2,1)S(1)} %collective-permute-done.15.last_got, ...), custom_call_target="tpu_custom_call" | custom-call | flops 1 | bytes 1 | tf_op jit(solution)/shard_map/pallas_call | solution.py:746
  150.3 0.8 collective-permute-start.20
  151.1 0.7 collective-permute-done.18
  151.8 1.5 collective-permute-done.19
  153.4 0.7 collective-permute-start.21
  154.0 3.2 %collective-permute-start.22 = (f32[32,128]{1,0:T(8,128)S(1)}, f32[32,128]{1,0:T(8,128)S(1)}, u32[]{:S(2)}, u32[]{:S(2)}) collective-permute-start(f32[32,128]{1,0:T(8,128)S(1)} %constant_dynamic-update-slice_fusion.sums), channel_id=1, source_target_pairs={{0,8},{1,9},{2,10},{3,11},{4,12},{5,13},{6,14},{7,15},{8,0},{9,1},... | collective-permute-start | bytes 49160 | tf_op jit(solution)/shard_map/ppermute | solution.py:152
  157.2 0.8 collective-permute-start.23
  158.0 2.2 %shard_map.102.image = f32[32,128,128]{2,1,0:T(8,128)S(1)} custom-call(s32[32,2]{1,0:T(8,128)S(1)} %copy-done.7, f32[24,128,128]{2,1,0:T(8,128)S(1)} %get-tuple-element.99.first_own, f32[16,128,128]{2,1,0:T(8,128)S(1)} %get-tuple-element.100.late_own, f32[24,128,128]{2,1,0:T(8,128)S(1)} %collective-permute-done.24.first_sib, ...), custom_call_target="tpu_custom_call" | custom-call | flops 1 | bytes 1 | tf_op jit(solution)/shard_map/pallas_call | solution.py:759
  160.3 2.5 %collective-permute-done.23.across = f32[32,128]{1,0:T(8,128)S(1)} collective-permute-done((f32[32,128]{1,0:T(8,128)S(1)}, f32[32,128]{1,0:T(8,128)S(1)}, u32[]{:S(2)}, u32[]{:S(2)}) %collective-permute-start.23) | collective-permute-done | bytes 16416 | tf_op jit(solution)/shard_map/ppermute | solution.py:152
  162.7 2.6 %shard_map.103 = (f32[32,128,128]{2,1,0:T(8,128)}, f32[32,128,128]{2,1,0:T(8,128)}, f32[1]{0:T(128)}) custom-call(f32[32,128]{1,0:T(8,128)S(1)} %constant_dynamic-update-slice_fusion.sums, f32[32,128]{1,0:T(8,128)S(1)} %collective-permute-done.21.near, f32[32,128]{1,0:T(8,128)S(1)} %collective-permute-done.22.far, ...), custom_call_target="tpu_custom_call" | custom-call | flops 1 | bytes 1 | tf_op jit(solution)/shard_map/pallas_call | solution.py:769
  (121 shorter events, 6.2 us)
Async XLA Ops:
  0.6 9.1 %collective-permute-start = (bf16[7,8,128,128]{3,2,1,0:T(8,128)(2,1)}, bf16[7,8,128,128]{3,2,1,0:T(8,128)(2,1)}, u32[]{:S(2)}, u32[]{:S(2)}) collective-permute-start(bf16[7,8,128,128]{3,2,1,0:T(8,128)(2,1)} %param.11), channel_id=1, source_target_pairs={{1,2},{2,1},{5,6},{6,5},{9,10},{10,9},{13,14},{14,13},{17,18},{18,... | collective-permute-start | bytes 5505032 | tf_op jit(solution)/shard_map/ppermute | solution.py:152
  2.6 7.1 %collective-permute-start.1 = (bf16[7,16]{1,0:T(8,128)(2,1)}, bf16[7,16]{1,0:T(8,128)(2,1)S(1)}, u32[]{:S(2)}, u32[]{:S(2)}) collective-permute-start(bf16[7,16]{1,0:T(8,128)(2,1)} %param.13), channel_id=1, source_target_pairs={{0,1},{1,0},{2,3},{3,2},{4,5},{5,4},{6,7},{7,6},{8,9},{9,8},{10,11... | collective-permute-start | bytes 680 | tf_op jit(solution)/shard_map/ppermute | solution.py:152
  9.7 28.5 %copy-start.14 = (bf16[7,16]{1,0:T(8,128)(2,1)S(1)}, bf16[7,16]{1,0:T(8,128)(2,1)}, u32[]{:S(2)}) copy-start(bf16[7,16]{1,0:T(8,128)(2,1)} %param.13) | copy-start | bytes 676
  11.4 39.5 %copy-start.13 = (bf16[7,8,128,128]{3,2,1,0:T(8,128)(2,1)}, bf16[7,8,128,128]{3,2,1,0:T(8,128)(2,1)S(1)}, u32[]{:S(2)}) copy-start(bf16[7,8,128,128]{3,2,1,0:T(8,128)(2,1)S(1)} %broadcast_select_fusion.1.left_mine) | copy-start | bytes 5505028
  11.4 43.4 %collective-permute-start.2 = (bf16[7,8,128,128]{3,2,1,0:T(8,128)(2,1)S(1)}, bf16[7,8,128,128]{3,2,1,0:T(8,128)(2,1)}, u32[]{:S(2)}, u32[]{:S(2)}) collective-permute-start(bf16[7,8,128,128]{3,2,1,0:T(8,128)(2,1)S(1)} %broadcast_select_fusion.1.left_mine), channel_id=1, source_target_pairs={{0,4},{1,5},{2,6},{3,7},{4,8},{5,9},{6,10},{7,11},{8,12},{9,13},{1... | collective-permute-start | bytes 5505032 | tf_op jit(solution)/shard_map/ppermute | solution.py:152
  16.1 38.7 %collective-permute-start.3 = (bf16[7,8,128,128]{3,2,1,0:T(8,128)(2,1)S(1)}, bf16[7,8,128,128]{3,2,1,0:T(8,128)(2,1)}, u32[]{:S(2)}, u32[]{:S(2)}) collective-permute-start(bf16[7,8,128,128]{3,2,1,0:T(8,128)(2,1)S(1)} %broadcast_select_fusion.1.left_mine), channel_id=1, source_target_pairs={{4,0},{5,1},{6,2},{7,3},{8,4},{9,5},{10,6},{11,7},{12,8},{13,9},{1... | collective-permute-start | bytes 5505032 | tf_op jit(solution)/shard_map/ppermute | solution.py:152
  17.4 21.5 %collective-permute-start.5 = (s32[3,32]{1,0:T(4,128)S(1)}, s32[3,32]{1,0:T(4,128)S(1)}, u32[]{:S(2)}, u32[]{:S(2)}) collective-permute-start(s32[3,32]{1,0:T(4,128)S(1)} %get-tuple-element.54), channel_id=1, source_target_pairs={{0,2},{1,3},{2,0},{3,1},{4,6},{5,7},{6,4},{7,5},{8,10},{9,11},{10,... | collective-permute-start | bytes 1160 | tf_op jit(solution)/shard_map/ppermute | solution.py:152
  36.2 11.7 %collective-permute-start.4 = (bf16[7,8,128,128]{3,2,1,0:T(8,128)(2,1)}, bf16[7,8,128,128]{3,2,1,0:T(8,128)(2,1)}, u32[]{:S(2)}, u32[]{:S(2)}) collective-permute-start(bf16[7,8,128,128]{3,2,1,0:T(8,128)(2,1)} %param.12), channel_id=1, source_target_pairs={{1,2},{2,1},{5,6},{6,5},{9,10},{10,9},{13,14},{14,13},{17,18},{18,... | collective-permute-start | bytes 5505032 | tf_op jit(solution)/shard_map/ppermute | solution.py:152
  42.5 12.3 %collective-permute-start.6 = (bf16[9,128,128]{2,1,0:T(8,128)(2,1)}, bf16[9,128,128]{2,1,0:T(8,128)(2,1)S(1)}, u32[]{:S(2)}, u32[]{:S(2)}) collective-permute-start(bf16[9,128,128]{2,1,0:T(8,128)(2,1)} %shard_map.94), channel_id=1, source_target_pairs={{0,4},{1,5},{2,6},{3,7},{12,8},{13,9},{14,10},{15,11},{16,20},{17,... | collective-permute-start | bytes 884744 | tf_op jit(solution)/shard_map/ppermute | solution.py:152
  47.2 0.7 copy-start.6
  47.9 28.2 %copy-start = (bf16[32,128,128]{2,1,0:T(8,128)(2,1)S(1)}, bf16[32,128,128]{2,1,0:T(8,128)(2,1)}, u32[]{:S(2)}) copy-start(bf16[32,128,128]{2,1,0:T(8,128)(2,1)} %wave.5) | copy-start | bytes 3145732
  54.9 21.9 %collective-permute-start.10 = (bf16[7,8,128,128]{3,2,1,0:T(8,128)(2,1)}, bf16[7,8,128,128]{3,2,1,0:T(8,128)(2,1)}, u32[]{:S(2)}, u32[]{:S(2)}) collective-permute-start(bf16[7,8,128,128]{3,2,1,0:T(8,128)(2,1)} %broadcast_select_fusion.right_mine), channel_id=1, source_target_pairs={{0,1},{1,0},{2,3},{3,2},{4,5},{5,4},{6,7},{7,6},{8,9},{9,8},{10,11... | collective-permute-start | bytes 5505032 | tf_op jit(solution)/shard_map/ppermute | solution.py:152
  62.5 47.6 %collective-permute-start.7 = (bf16[7,8,128,128]{3,2,1,0:T(8,128)(2,1)}, bf16[7,8,128,128]{3,2,1,0:T(8,128)(2,1)S(1)}, u32[]{:S(2)}, u32[]{:S(2)}) collective-permute-start(bf16[7,8,128,128]{3,2,1,0:T(8,128)(2,1)} %collective-permute-done.2.below), channel_id=1, source_target_pairs={{4,8},{5,9},{6,10},{7,11},{8,12},{9,13},{10,14},{11,15},{20,24},{2... | collective-permute-start | bytes 5505032 | tf_op jit(solution)/shard_map/ppermute | solution.py:152
  63.3 49.9 %collective-permute-start.8 = (bf16[7,8,128,128]{3,2,1,0:T(8,128)(2,1)}, bf16[7,8,128,128]{3,2,1,0:T(8,128)(2,1)}, u32[]{:S(2)}, u32[]{:S(2)}) collective-permute-start(bf16[7,8,128,128]{3,2,1,0:T(8,128)(2,1)} %collective-permute-done.3.above), channel_id=1, source_target_pairs={{4,0},{5,1},{6,2},{7,3},{8,4},{9,5},{10,6},{11,7},{20,16},{21,17},... | collective-permute-start | bytes 5505032 | tf_op jit(solution)/shard_map/ppermute | solution.py:152
  64.6 49.7 %collective-permute-start.9 = (bf16[7,8,128,128]{3,2,1,0:T(8,128)(2,1)}, bf16[7,8,128,128]{3,2,1,0:T(8,128)(2,1)}, u32[]{:S(2)}, u32[]{:S(2)}) collective-permute-start(bf16[7,8,128,128]{3,2,1,0:T(8,128)(2,1)} %broadcast_select_fusion.right_mine), channel_id=1, source_target_pairs={{0,4},{1,5},{2,6},{3,7},{12,8},{13,9},{14,10},{15,11},{16,20},{17,... | collective-permute-start | bytes 5505032 | tf_op jit(solution)/shard_map/ppermute | solution.py:152
  76.1 24.6 %collective-permute-start.12 = (bf16[32,128,128]{2,1,0:T(8,128)(2,1)S(1)}, bf16[32,128,128]{2,1,0:T(8,128)(2,1)}, u32[]{:S(2)}, u32[]{:S(2)}) collective-permute-start(bf16[32,128,128]{2,1,0:T(8,128)(2,1)S(1)} %copy-done), channel_id=1, source_target_pairs={{0,2},{1,3},{2,0},{3,1},{4,6},{5,7},{6,4},{7,5},{8,10},{9,11},{10,... | collective-permute-start | bytes 3145736 | tf_op jit(solution)/shard_map/ppermute | solution.py:152
  86.2 28.1 %collective-permute-start.11 = (bf16[9,128,128]{2,1,0:T(8,128)(2,1)S(1)}, bf16[9,128,128]{2,1,0:T(8,128)(2,1)S(1)}, u32[]{:S(2)}, u32[]{:S(2)}) collective-permute-start(bf16[9,128,128]{2,1,0:T(8,128)(2,1)S(1)} %collective-permute-done.6.wave_own), channel_id=1, source_target_pairs={{4,6},{5,7},{6,4},{7,5},{8,10},{9,11},{10,8},{11,9},{20,22},{21,23... | collective-permute-start | bytes 884744 | tf_op jit(solution)/shard_map/ppermute | solution.py:152
  100.7 15.8 %copy-start.4 = (f32[2,8,7,128]{3,1,2,0:T(8,128)S(1)}, f32[2,8,7,128]{3,1,2,0:T(8,128)}, u32[]{:S(2)}) copy-start(f32[2,8,7,128]{3,1,2,0:T(8,128)} %copy.161) | copy-start | bytes 172036
  110.1 8.1 %copy-start.2 = (bf16[7,8,128,128]{3,2,1,0:T(8,128)(2,1)}, bf16[7,8,128,128]{3,2,1,0:T(8,128)(2,1)S(1)}, u32[]{:S(2)}) copy-start(bf16[7,8,128,128]{3,2,1,0:T(8,128)(2,1)S(1)} %collective-permute-done.7.below) | copy-start | bytes 5505028
  114.3 2.2 %collective-permute-start.14 = (bf16[7,8,128,128]{3,2,1,0:T(8,128)(2,1)}, bf16[7,8,128,128]{3,2,1,0:T(8,128)(2,1)}, u32[]{:S(2)}, u32[]{:S(2)}) collective-permute-start(bf16[7,8,128,128]{3,2,1,0:T(8,128)(2,1)} %collective-permute-done.9.right_mine), channel_id=1, source_target_pairs={{4,5},{5,4},{6,7},{7,6},{8,9},{9,8},{10,11},{11,10},{20,21},{21,20... | collective-permute-start | bytes 5505032 | tf_op jit(solution)/shard_map/ppermute | solution.py:152
  116.3 1.9 %copy-start.11 = (s32[3]{0:T(128)}, s32[3]{0:T(128)S(1)}, u32[]{:S(2)}) copy-start(s32[3]{0:T(128)S(1)} %add_convert_fusion.4.flags) | copy-start | bytes 40
  116.5 18.6 %collective-permute-start.13 = (bf16[24,128,128]{2,1,0:T(8,128)(2,1)}, bf16[24,128,128]{2,1,0:T(8,128)(2,1)}, u32[]{:S(2)}, u32[]{:S(2)}) collective-permute-start(bf16[24,128,128]{2,1,0:T(8,128)(2,1)} %get-tuple-element.75), channel_id=1, source_target_pairs={{0,2},{1,3},{2,0},{3,1},{4,6},{5,7},{6,4},{7,5},{8,10},{9,11},{10,... | collective-permute-start | bytes 2359304 | tf_op jit(solution)/shard_map/ppermute | solution.py:152
  118.2 0.7 copy-start.12
  118.9 19.7 %collective-permute-start.16 = (bf16[8,128,128]{2,1,0:T(8,128)(2,1)}, bf16[8,128,128]{2,1,0:T(8,128)(2,1)S(1)}, u32[]{:S(2)}, u32[]{:S(2)}) collective-permute-start(bf16[8,128,128]{2,1,0:T(8,128)(2,1)} %get-tuple-element.81), channel_id=1, source_target_pairs={{4,0},{5,1},{6,2},{7,3},{8,12},{9,13},{10,14},{11,15},{20,16},{21,... | collective-permute-start | bytes 786440 | tf_op jit(solution)/shard_map/ppermute | solution.py:152
  120.9 14.6 %copy-start.1 = (bf16[32,128,128]{2,1,0:T(8,128)(2,1)S(1)}, bf16[32,128,128]{2,1,0:T(8,128)(2,1)}, u32[]{:S(2)}) copy-start(bf16[32,128,128]{2,1,0:T(8,128)(2,1)} %wave.5) | copy-start | bytes 3145732
  120.9 14.6 %copy-start.3 = (f32[24,128,128]{2,1,0:T(8,128)S(1)}, f32[24,128,128]{2,1,0:T(8,128)}, u32[]{:S(2)}) copy-start(f32[24,128,128]{2,1,0:T(8,128)} %get-tuple-element.74.own) | copy-start | bytes 4718596
  120.9 22.2 %collective-permute-start.17 = (bf16[8,128,128]{2,1,0:T(8,128)(2,1)}, bf16[8,128,128]{2,1,0:T(8,128)(2,1)S(1)}, u32[]{:S(2)}, u32[]{:S(2)}) collective-permute-start(bf16[8,128,128]{2,1,0:T(8,128)(2,1)} %copy-done.12), channel_id=1, source_target_pairs={{4,2},{5,3},{6,0},{7,1},{8,14},{9,15},{10,12},{11,13},{20,18},{21,... | collective-permute-start | bytes 786440 | tf_op jit(solution)/shard_map/ppermute | solution.py:152
  135.1 12.0 %collective-permute-start.15 = (bf16[8,128,128]{2,1,0:T(8,128)(2,1)}, bf16[8,128,128]{2,1,0:T(8,128)(2,1)S(1)}, u32[]{:S(2)}, u32[]{:S(2)}) collective-permute-start(bf16[8,128,128]{2,1,0:T(8,128)(2,1)} %get-tuple-element.90), channel_id=1, source_target_pairs={{0,2},{1,3},{2,0},{3,1},{4,6},{5,7},{6,4},{7,5},{8,10},{9,11},{10,... | collective-permute-start | bytes 786440 | tf_op jit(solution)/shard_map/ppermute | solution.py:152
  137.4 20.7 %collective-permute-start.24 = (f32[24,128,128]{2,1,0:T(8,128)S(1)}, f32[24,128,128]{2,1,0:T(8,128)S(1)}, u32[]{:S(2)}, u32[]{:S(2)}) collective-permute-start(f32[24,128,128]{2,1,0:T(8,128)S(1)} %get-tuple-element.99.first_own), channel_id=1, source_target_pairs={{0,1},{1,0},{2,3},{3,2},{4,5},{5,4},{6,7},{7,6},{8,9},{9,8},{10,11... | collective-permute-start | bytes 4718600 | tf_op jit(solution)/shard_map/ppermute | solution.py:152
  138.6 8.5 %copy-start.5 = (f32[8,128,128]{2,1,0:T(8,128)S(1)}, f32[8,128,128]{2,1,0:T(8,128)}, u32[]{:S(2)}) copy-start(f32[8,128,128]{2,1,0:T(8,128)} %get-tuple-element.87.last_own) | copy-start | bytes 1572868
  138.6 8.5 %copy-start.8 = (f32[8,128]{1,0:T(8,128)S(1)}, f32[8,128]{1,0:T(8,128)}, u32[]{:S(2)}) copy-start(f32[8,128]{1,0:T(8,128)} %get-tuple-element.93.map_a) | copy-start | bytes 12292
  138.6 8.5 %copy-start.9 = (f32[8,128]{1,0:T(8,128)S(1)}, f32[8,128]{1,0:T(8,128)}, u32[]{:S(2)}) copy-start(f32[8,128]{1,0:T(8,128)} %get-tuple-element.94.map_b) | copy-start | bytes 12292
  138.6 8.5 %copy-start.10 = (f32[8,128]{1,0:T(8,128)S(1)}, f32[8,128]{1,0:T(8,128)}, u32[]{:S(2)}) copy-start(f32[8,128]{1,0:T(8,128)} %get-tuple-element.96.map_d) | copy-start | bytes 12292
  143.1 14.9 %copy-start.7 = (s32[32,2]{1,0:T(8,128)S(1)}, s32[32,2]{1,0:T(8,128)}, u32[]{:S(2)}) copy-start(s32[32,2]{1,0:T(8,128)} %copy-done.6) | copy-start | bytes 772
  149.1 8.9 %collective-permute-start.25 = (f32[16,128,128]{2,1,0:T(8,128)S(1)}, f32[16,128,128]{2,1,0:T(8,128)S(1)}, u32[]{:S(2)}, u32[]{:S(2)}) collective-permute-start(f32[16,128,128]{2,1,0:T(8,128)S(1)} %get-tuple-element.100.late_own), channel_id=1, source_target_pairs={{0,1},{1,0},{2,3},{3,2},{4,5},{5,4},{6,7},{7,6},{8,9},{9,8},{10,11... | collective-permute-start | bytes 3145736 | tf_op jit(solution)/shard_map/ppermute | solution.py:152
  149.2 2.7 %collective-permute-start.18 = (f32[8,128]{1,0:T(8,128)S(1)}, f32[8,128]{1,0:T(8,128)S(1)}, u32[]{:S(2)}, u32[]{:S(2)}) collective-permute-start(f32[8,128]{1,0:T(8,128)S(1)} %get-tuple-element.97), channel_id=1, source_target_pairs={{0,1},{1,0},{2,3},{3,2},{4,5},{5,4},{6,7},{7,6},{8,9},{9,8},{10,11... | collective-permute-start | bytes 12296 | tf_op jit(solution)/shard_map/ppermute | solution.py:152
  149.7 3.6 %collective-permute-start.19 = (f32[8,128]{1,0:T(8,128)S(1)}, f32[8,128]{1,0:T(8,128)S(1)}, u32[]{:S(2)}, u32[]{:S(2)}) collective-permute-start(f32[8,128]{1,0:T(8,128)S(1)} %get-tuple-element.97), channel_id=1, source_target_pairs={{0,2},{1,3},{2,0},{3,1},{4,6},{5,7},{6,4},{7,5},{8,10},{9,11},{10,... | collective-permute-start | bytes 12296 | tf_op jit(solution)/shard_map/ppermute | solution.py:152
  150.3 3.1 %collective-permute-start.20 = (f32[8,128]{1,0:T(8,128)S(1)}, f32[8,128]{1,0:T(8,128)S(1)}, u32[]{:S(2)}, u32[]{:S(2)}) collective-permute-start(f32[8,128]{1,0:T(8,128)S(1)} %get-tuple-element.97), channel_id=1, source_target_pairs={{0,3},{1,2},{2,1},{3,0},{4,7},{5,6},{6,5},{7,4},{8,11},{9,10},{10,... | collective-permute-start | bytes 12296 | tf_op jit(solution)/shard_map/ppermute | solution.py:152
  153.4 6.9 %collective-permute-start.21 = (f32[32,128]{1,0:T(8,128)S(1)}, f32[32,128]{1,0:T(8,128)S(1)}, u32[]{:S(2)}, u32[]{:S(2)}) collective-permute-start(f32[32,128]{1,0:T(8,128)S(1)} %constant_dynamic-update-slice_fusion.sums), channel_id=1, source_target_pairs={{0,4},{1,5},{2,6},{3,7},{4,0},{5,1},{6,2},{7,3},{8,12},{9,13},{10,... | collective-permute-start | bytes 49160 | tf_op jit(solution)/shard_map/ppermute | solution.py:152
  154.0 6.2 %collective-permute-start.22 = (f32[32,128]{1,0:T(8,128)S(1)}, f32[32,128]{1,0:T(8,128)S(1)}, u32[]{:S(2)}, u32[]{:S(2)}) collective-permute-start(f32[32,128]{1,0:T(8,128)S(1)} %constant_dynamic-update-slice_fusion.sums), channel_id=1, source_target_pairs={{0,8},{1,9},{2,10},{3,11},{4,12},{5,13},{6,14},{7,15},{8,0},{9,1},... | collective-permute-start | bytes 49160 | tf_op jit(solution)/shard_map/ppermute | solution.py:152
  157.2 5.5 %collective-permute-start.23 = (f32[32,128]{1,0:T(8,128)S(1)}, f32[32,128]{1,0:T(8,128)S(1)}, u32[]{:S(2)}, u32[]{:S(2)}) collective-permute-start(f32[32,128]{1,0:T(8,128)S(1)} %constant_dynamic-update-slice_fusion.sums), channel_id=1, source_target_pairs={{0,12},{1,13},{2,14},{3,15},{4,8},{5,9},{6,10},{7,11},{8,4},{9,5},... | collective-permute-start | bytes 49160 | tf_op jit(solution)/shard_map/ppermute | solution.py:152

commit v5 on v4

--- a/solution.py
+++ b/solution.py
@@ -205,6 +205,18 @@
     return lax.fori_loop(0, rows, add, jnp.int32(0))
 
 
+def select_kernel(flags, straight_side, crossed_side, out, held, sems):
+    terms = held.shape[0]
+    outs = [pltpu.make_async_copy(held.at[t], out.at[t], sems.at[1, t]) for t in range(terms)]
+    for t in range(terms):
+        choose(flags[2] == 1, straight_side.at[t], crossed_side.at[t], held.at[t], sems.at[0, t])
+    for t in range(terms):
+        pltpu.make_async_copy(straight_side.at[t], held.at[t], sems.at[0, t]).wait()
+        outs[t].start()
+    for t in range(terms):
+        outs[t].wait()
+
+
 def near_kernel(
     table, weights_in, wave_in, right_mine, right_sib, left_mine, below, above,
     first, last, carried_out, correlation,
@@ -583,7 +595,13 @@
     above = hop(left_mine, down)
 
     right_n = move(after(right_environment, left_mine), DIAGONAL)
-    right_mine = mine_of(right_environment, right_n)
+    right_mine = call(
+        select_kernel,
+        jax.ShapeDtypeStruct(env, bf16),
+        [SMEM, HBM, HBM],
+        HBM,
+        [pltpu.VMEM(env, bf16), pltpu.SemaphoreType.DMA((2, terms))],
+    )(flags, right_environment, right_n)
     info_other = move(after(info, left_mine), COLUMN)
 
     block = jnp.arange(blocks)
@@ -640,13 +658,13 @@
     )
 
     held = (below, above, right_mine, wave_guest)
-    held += (table, far_table, weights, sources, first_table, late_table)
+    held += (table, far_table, weights, sources, first_table, late_table, flags)
     held = lax.optimization_barrier(held)
     below, above, right_mine, wave_guest = held[:4]
-    table, far_table, weights, sources, first_table, late_table = held[4:]
+    table, far_table, weights, sources, first_table, late_table, flags = held[4:]
+    right_guest = hop(right_mine, inward, outer)
     below_two = hop(below, up, inner)
     above_two = hop(above, down, inner)
-    right_guest = hop(right_mine, inward, outer)
     wave_other = move(after(wavefunction, right_mine), COLUMN)
     right_sib = move(right_mine, CORE)
     map_shape = jax.ShapeDtypeStruct((8, 128), f32)
@@ -680,17 +698,16 @@
     own, own_last, carried_own, map_own = near(0, wavefunction, f32)
     other, other_last, carried_other, map_other = near(1, wave_other, bf16)
     wave_guest_other = move(after(wave_guest, own), COLUMN_INNER)
-    held = (below_two, above_two, right_guest, wave_guest_other)
-    held += (own, own_last, carried_own, other, other_last, carried_other)
-    held = lax.optimization_barrier(held)
-    below_two, above_two, right_guest, wave_guest_other = held[:4]
-    own, own_last, carried_own, other, other_last, carried_other = held[4:]
-    first_got = move(other, COLUMN)
-    right_guest_sib = hop(right_guest, other_core, inner)
     guest_got = jnp.concatenate(
         [guests[most, :most, :6] for guests in (wave_guest, wave_guest_other)]
     ).astype(jnp.int32)
-
+    held = (right_guest, below_two, above_two, wave_guest_other)
+    held += (own, own_last, carried_own, other, other_last, carried_other, guest_got)
+    held = lax.optimization_barrier(held)
+    right_guest, below_two, above_two, wave_guest_other = held[:4]
+    own, own_last, carried_own, other, other_last, carried_other, guest_got = held[4:]
+    first_got = move(other, COLUMN)
+    right_guest_sib = hop(right_guest, other_core, inner)
     last = jax.ShapeDtypeStruct((most,) + square, f32)
     last_sent = jax.ShapeDtypeStruct((most,) + square, bf16)
     guest_own, guest_other, map_guest = call(
@@ -740,7 +757,7 @@
         vmem=VMEM_SMALL,
     )(first_table, own, after(first_got, last_own), wavefunction)
     first_sib = move(first_own, CORE)
-    guest_full = call(sum_kernel, last, [VMEM] * 2, VMEM, [], 2**37, vmem=VMEM_SMALL)(
+    guest_full = call(sum_kernel, last, [VMEM] * 2, VMEM, [], 2**30, vmem=VMEM_SMALL)(
         after(guest_straight, sums_first), guest_crossed
     )
     late, sums = call(
@@ -754,7 +771,8 @@
         late_table, sums_first, last_own, last_got, guest_full, wavefunction,
         map_own, map_other, map_guest, map_far,
     )
-    late_sib = move(late, CORE)
+    sums = jnp.concatenate([sums] + [move(sums, pairs) for pairs in (CORE, COLUMN, ACROSS)])
+    late_sib = move(after(late, sums), CORE)
     image_shape = jax.ShapeDtypeStruct((blocks,) + square, f32)
     kept = call(
         place_kernel,
@@ -764,7 +782,6 @@
         [],
         vmem=VMEM_SMALL,
     )(sources, first_own, late, first_sib, late_sib)
-    sums = jnp.concatenate([sums] + [move(sums, pairs) for pairs in (CORE, COLUMN, ACROSS)])
     sums = [sums] + [move(sums, pairs_of(lambda z, y, c: (z ^ n, y, c))) for n in (1, 2, 3)]
     image, correction, rayleigh = call(
         functools.partial(correction_kernel, blocks * 8 * dim * dim),

time: 166 us -> 164 us (0.988)
  Pallas kernels: 36.5 us -> 41.6 us
  starting transfers between devices: 70 us -> 66.5 us
  other arithmetic: 7.45 us -> 4.94 us
  waiting for transfers between devices: 43.7 us -> 42 us
    pallas_call x1 -> x2, Pallas kernels: 0.05 us -> 4.09 us  [the longest x1 3.09 us: on_device(): call(select_kernel, jax.ShapeDtypeStruct(env, bf16), [SMEM, HBM, HBM], HB...]
    ppermute x26, starting transfers between devices: 70 us -> 66.5 us  [move(): return lax.ppermute(array, BOTH, pairs)]
    select_n x2 -> x1, other arithmetic: 4.71 us -> 1.7 us  [mine_of(): return jnp.where(y == c, own, swapped)]
    ppermute x26, waiting for transfers between devices: 43.7 us -> 42 us  [move(): return lax.ppermute(array, BOTH, pairs)]
  transfers between devices with their start and end apart: 26 -> 26, of which waited for: 12 -> 10; matrix products, arithmetic and copies ran while one was open for 7% -> 6% of each run, Pallas kernels for 20% -> 24%
where the time goes in v5:
time: 164 us; the launch traced here: 163 us
  starting transfers between devices  66.5 us (41%)
  waiting for transfers between devices  42 us (26%)
  Pallas kernels  41.6 us (25%)
  local copies, waits for them, and re-layouts  5.83 us (4%)
  other arithmetic  4.94 us (3%)
    ppermute x26, starting transfers between devices, move(): return lax.ppermute(array, BOTH, pairs)  66.5 us
    ppermute x26, waiting for transfers between devices, move(): return lax.ppermute(array, BOTH, pairs)  42 us
    pallas_call x2, Pallas kernels, near(): call(near_kernel, (jax.ShapeDtypeStruct((first_slots,) + square, kind), j...  18.3 us
    pallas_call x1, Pallas kernels, on_device(): call(far_kernel, (last, last_sent, map_shape), [SMEM] * 2 + [HBM] * 8, (V...  6.71 us
  transfers between devices with their start and end apart: 26, of which 10 were waited for; matrix products, arithmetic and copies ran while one was open for 6% of the time, Pallas kernels for 24%

profile of v5, /device:TPU:0, one launch (start us, length us, event | category | flops | bytes accessed | tf_op | source)
XLA Modules:
  0.0 163.1 jit_solution(16398728156311464964)
XLA Ops:
  0.6 1.9 %collective-permute-start = (bf16[7,8,128,128]{3,2,1,0:T(8,128)(2,1)}, bf16[7,8,128,128]{3,2,1,0:T(8,128)(2,1)}, u32[]{:S(2)}, u32[]{:S(2)}) collective-permute-start(bf16[7,8,128,128]{3,2,1,0:T(8,128)(2,1)} %param.11), channel_id=1, source_target_pairs={{1,2},{2,1},{5,6},{6,5},{9,10},{10,9},{13,14},{14,13},{17,18},{18,... | collective-permute-start | bytes 5505032 | tf_op jit(solution)/shard_map/ppermute | solution.py:152
  2.6 3.1 %collective-permute-start.1 = (bf16[7,16]{1,0:T(8,128)(2,1)}, bf16[7,16]{1,0:T(8,128)(2,1)S(1)}, u32[]{:S(2)}, u32[]{:S(2)}) collective-permute-start(bf16[7,16]{1,0:T(8,128)(2,1)} %param.13), channel_id=1, source_target_pairs={{0,1},{1,0},{2,3},{3,2},{4,5},{5,4},{6,7},{7,6},{8,9},{9,8},{10,11... | collective-permute-start | bytes 680 | tf_op jit(solution)/shard_map/ppermute | solution.py:152
  5.7 0.7 subtract_bitcast_fusion
  6.4 0.7 pad_add_fusion
  7.4 0.7 stack.111
  8.3 0.7 fusion.39
  10.3 1.7 %broadcast_select_fusion.left_mine = bf16[7,8,128,128]{3,2,1,0:T(8,128)(2,1)S(1)} fusion(bf16[7,8,128,128]{3,2,1,0:T(8,128)(2,1)} %param.11, bf16[7,8,128,128]{3,2,1,0:T(8,128)(2,1)} %collective-permute-done, pred[]{:T(512)} %eq.284), kind=kLoop, calls=%fused_computation | loop fusion | flops 917504 | bytes 5505025 | tf_op jit(solution)/shard_map/jit(_where)/select_n | solution.py:557
  12.0 4.8 %collective-permute-start.2 = (bf16[7,8,128,128]{3,2,1,0:T(8,128)(2,1)S(1)}, bf16[7,8,128,128]{3,2,1,0:T(8,128)(2,1)}, u32[]{:S(2)}, u32[]{:S(2)}) collective-permute-start(bf16[7,8,128,128]{3,2,1,0:T(8,128)(2,1)S(1)} %broadcast_select_fusion.left_mine), channel_id=1, source_target_pairs={{0,4},{1,5},{2,6},{3,7},{4,8},{5,9},{6,10},{7,11},{8,12},{9,13},{1... | collective-permute-start | bytes 5505032 | tf_op jit(solution)/shard_map/ppermute | solution.py:152
  16.8 1.3 collective-permute-start.3
  18.1 18.2 %collective-permute-start.5 = (s32[3,32]{1,0:T(4,128)S(1)}, s32[3,32]{1,0:T(4,128)S(1)}, u32[]{:S(2)}, u32[]{:S(2)}) collective-permute-start(s32[3,32]{1,0:T(4,128)S(1)} %get-tuple-element.57), channel_id=1, source_target_pairs={{0,2},{1,3},{2,0},{3,1},{4,6},{5,7},{6,4},{7,5},{8,10},{9,11},{10,... | collective-permute-start | bytes 1160 | tf_op jit(solution)/shard_map/ppermute | solution.py:152
  36.3 1.9 %collective-permute-start.4 = (bf16[7,8,128,128]{3,2,1,0:T(8,128)(2,1)}, bf16[7,8,128,128]{3,2,1,0:T(8,128)(2,1)}, u32[]{:S(2)}, u32[]{:S(2)}) collective-permute-start(bf16[7,8,128,128]{3,2,1,0:T(8,128)(2,1)} %straight_side.1), channel_id=1, source_target_pairs={{1,2},{2,1},{5,6},{6,5},{9,10},{10,9},{13,14},{14,13},{17,18},{18,... | collective-permute-start | bytes 5505032 | tf_op jit(solution)/shard_map/ppermute | solution.py:152
  40.2 2.0 %shard_map.95 = bf16[9,128,128]{2,1,0:T(8,128)(2,1)} custom-call(s32[8,6]{1,0:T(8,128)} %get-tuple-element.146.table, bf16[32,128,128]{2,1,0:T(8,128)(2,1)} %wave.5, bf16[1,128,128]{2,1,0:T(8,128)(2,1)} %pad_bitcast_fusion.facts), custom_call_target="tpu_custom_call" | custom-call | flops 1 | bytes 1 | tf_op jit(solution)/shard_map/pallas_call | solution.py:613
  42.2 4.6 %collective-permute-start.6 = (bf16[9,128,128]{2,1,0:T(8,128)(2,1)}, bf16[9,128,128]{2,1,0:T(8,128)(2,1)S(1)}, u32[]{:S(2)}, u32[]{:S(2)}) collective-permute-start(bf16[9,128,128]{2,1,0:T(8,128)(2,1)} %shard_map.95), channel_id=1, source_target_pairs={{0,4},{1,5},{2,6},{3,7},{12,8},{13,9},{14,10},{15,11},{16,20},{17,... | collective-permute-start | bytes 884744 | tf_op jit(solution)/shard_map/ppermute | solution.py:152
  49.0 3.1 %shard_map.94.right_mine = bf16[7,8,128,128]{3,2,1,0:T(8,128)(2,1)} custom-call(s32[3]{0:T(128)} %add_convert_fusion.3.flags, bf16[7,8,128,128]{3,2,1,0:T(8,128)(2,1)} %straight_side.1, bf16[7,8,128,128]{3,2,1,0:T(8,128)(2,1)} %collective-permute-done.4.crossed_side), custom_call_target="tpu_custom_call" | custom-call | flops 1 | bytes 1 | tf_op jit(solution)/shard_map/pallas_call | solution.py:598
  52.1 2.4 %collective-permute-done.6.wave_own = bf16[9,128,128]{2,1,0:T(8,128)(2,1)S(1)} collective-permute-done((bf16[9,128,128]{2,1,0:T(8,128)(2,1)}, bf16[9,128,128]{2,1,0:T(8,128)(2,1)S(1)}, u32[]{:S(2)}, u32[]{:S(2)}) %collective-permute-start.6) | collective-permute-done | bytes 294944 | tf_op jit(solution)/shard_map/ppermute | solution.py:152
  54.6 8.1 %collective-permute-start.10 = (bf16[7,8,128,128]{3,2,1,0:T(8,128)(2,1)}, bf16[7,8,128,128]{3,2,1,0:T(8,128)(2,1)}, u32[]{:S(2)}, u32[]{:S(2)}) collective-permute-start(bf16[7,8,128,128]{3,2,1,0:T(8,128)(2,1)} %shard_map.94.right_mine), channel_id=1, source_target_pairs={{0,1},{1,0},{2,3},{3,2},{4,5},{5,4},{6,7},{7,6},{8,9},{9,8},{10,11... | collective-permute-start | bytes 5505032 | tf_op jit(solution)/shard_map/ppermute | solution.py:152
  62.6 5.8 %collective-permute-start.7 = (bf16[7,8,128,128]{3,2,1,0:T(8,128)(2,1)}, bf16[7,8,128,128]{3,2,1,0:T(8,128)(2,1)}, u32[]{:S(2)}, u32[]{:S(2)}) collective-permute-start(bf16[7,8,128,128]{3,2,1,0:T(8,128)(2,1)} %shard_map.94.right_mine), channel_id=1, source_target_pairs={{0,4},{1,5},{2,6},{3,7},{12,8},{13,9},{14,10},{15,11},{16,20},{17,... | collective-permute-start | bytes 5505032 | tf_op jit(solution)/shard_map/ppermute | solution.py:152
  68.5 0.8 collective-permute-start.8
  69.3 1.3 collective-permute-start.9
  70.6 1.7 %collective-permute-start.12 = (bf16[32,128,128]{2,1,0:T(8,128)(2,1)S(1)}, bf16[32,128,128]{2,1,0:T(8,128)(2,1)}, u32[]{:S(2)}, u32[]{:S(2)}) collective-permute-start(bf16[32,128,128]{2,1,0:T(8,128)(2,1)S(1)} %copy-done), channel_id=1, source_target_pairs={{0,2},{1,3},{2,0},{3,1},{4,6},{5,7},{6,4},{7,5},{8,10},{9,11},{10,... | collective-permute-start | bytes 3145736 | tf_op jit(solution)/shard_map/ppermute | solution.py:152
  72.9 9.2 %shard_map.96 = (f32[24,128,128]{2,1,0:T(8,128)}, f32[8,128,128]{2,1,0:T(8,128)}, bf16[8,128,896]{2,1,0:T(8,128)(2,1)}, f32[8,128]{1,0:T(8,128)}) custom-call(s32[32,6]{1,0:T(8,128)} %get-tuple-element.126.table, f32[16,896]{1,0:T(8,128)} %bitcast.117, bf16[32,128,128]{2,1,0:T(8,128)(2,1)} %wave.5, bf16[7,8,128,128]{3,2,1,0:T(8,128)(2,1)} %shard_map.94.right_mine, ...), custom_call_target="tpu_custom_call" | custom-call | flops 1 | bytes 1 | tf_op jit(solution)/shard_map/pallas_call | solution.py:673
  82.1 0.7 collective-permute-start.11
  82.8 13.1 %collective-permute-done.12.wave_in.wave_other = bf16[32,128,128]{2,1,0:T(8,128)(2,1)} collective-permute-done((bf16[32,128,128]{2,1,0:T(8,128)(2,1)S(1)}, bf16[32,128,128]{2,1,0:T(8,128)(2,1)}, u32[]{:S(2)}, u32[]{:S(2)}) %collective-permute-start.12) | collective-permute-done | bytes 1048608 | tf_op jit(solution)/shard_map/ppermute | solution.py:152
  95.9 9.1 %shard_map.97 = (bf16[24,128,128]{2,1,0:T(8,128)(2,1)}, bf16[8,128,128]{2,1,0:T(8,128)(2,1)}, bf16[8,128,896]{2,1,0:T(8,128)(2,1)}, f32[8,128]{1,0:T(8,128)}) custom-call(s32[32,6]{1,0:T(8,128)} %get-tuple-element.125.table, f32[16,896]{1,0:T(8,128)} %bitcast.118, bf16[32,128,128]{2,1,0:T(8,128)(2,1)} %collective-permute-done.12.wave_in.wave_other, ...), custom_call_target="tpu_custom_call" | custom-call | flops 1 | bytes 1 | tf_op jit(solution)/shard_map/pallas_call | solution.py:673
  105.0 1.9 %collective-permute-done.7.right_mine = bf16[7,8,128,128]{3,2,1,0:T(8,128)(2,1)} collective-permute-done((bf16[7,8,128,128]{3,2,1,0:T(8,128)(2,1)}, bf16[7,8,128,128]{3,2,1,0:T(8,128)(2,1)}, u32[]{:S(2)}, u32[]{:S(2)}) %collective-permute-start.7) | collective-permute-done | bytes 1835040 | tf_op jit(solution)/shard_map/ppermute | solution.py:152
  106.9 8.1 %collective-permute-done.9.above = bf16[7,8,128,128]{3,2,1,0:T(8,128)(2,1)} collective-permute-done((bf16[7,8,128,128]{3,2,1,0:T(8,128)(2,1)}, bf16[7,8,128,128]{3,2,1,0:T(8,128)(2,1)}, u32[]{:S(2)}, u32[]{:S(2)}) %collective-permute-start.9) | collective-permute-done | bytes 1835040 | tf_op jit(solution)/shard_map/ppermute | solution.py:152
  115.0 0.8 collective-permute-start.14
  116.1 1.7 %shard_map.98 = (bf16[8,128,128]{2,1,0:T(8,128)(2,1)}, bf16[8,128,128]{2,1,0:T(8,128)(2,1)S(1)}, f32[8,128]{1,0:T(8,128)S(1)}) custom-call(s32[3]{0:T(128)S(1)} %copy-done.8, s32[16,6]{1,0:T(8,128)S(1)} %maximum_convert_fusion.table, f32[16,896]{1,0:T(8,128)S(1)} %bitcast.119, bf16[7,8,128,128]{3,2,1,0:T(8,128)(2,1)S(1)} %collective-permute-done.8.below, ...), custom_call_target="tpu_custom_call" | custom-call | flops 1 | bytes 1 | tf_op jit(solution)/shard_map/pallas_call | solution.py:713
  117.8 1.3 collective-permute-start.16
  119.1 0.7 copy.133.table
  119.8 1.6 collective-permute-start.17
  121.3 6.7 %shard_map.99 = (f32[8,128,128]{2,1,0:T(8,128)}, bf16[8,128,128]{2,1,0:T(8,128)(2,1)}, f32[8,128]{1,0:T(8,128)}) custom-call(s32[3]{0:T(128)} %add_convert_fusion.3.flags, s32[16,6]{1,0:T(8,128)} %copy.133.table, bf16[8,128,896]{2,1,0:T(8,128)(2,1)} %get-tuple-element.88.carried_own, bf16[8,128,896]{2,1,0:T(8,128)(2,1)} %get-tuple-element.89.carried_other, ...), custom_call_target="tpu_custom_call" | custom-call | flops 137438953472 | bytes 1 | tf_op jit(solution)/shard_map/pallas_call | solution.py:732
  128.0 1.9 %collective-permute-start.15 = (bf16[8,128,128]{2,1,0:T(8,128)(2,1)}, bf16[8,128,128]{2,1,0:T(8,128)(2,1)S(1)}, u32[]{:S(2)}, u32[]{:S(2)}) collective-permute-start(bf16[8,128,128]{2,1,0:T(8,128)(2,1)} %get-tuple-element.95), channel_id=1, source_target_pairs={{0,2},{1,3},{2,0},{3,1},{4,6},{5,7},{6,4},{7,5},{8,10},{9,11},{10,... | collective-permute-start | bytes 786440 | tf_op jit(solution)/shard_map/ppermute | solution.py:152
  130.1 6.5 %collective-permute-done.13.got = bf16[24,128,128]{2,1,0:T(8,128)(2,1)} collective-permute-done((bf16[24,128,128]{2,1,0:T(8,128)(2,1)}, bf16[24,128,128]{2,1,0:T(8,128)(2,1)}, u32[]{:S(2)}, u32[]{:S(2)}) %collective-permute-start.13) | collective-permute-done | bytes 786464 | tf_op jit(solution)/shard_map/ppermute | solution.py:152
  136.7 2.1 %shard_map.100 = (f32[24,128,128]{2,1,0:T(8,128)S(1)}, f32[8,128]{1,0:T(8,128)S(1)}) custom-call(s32[32,3]{1,0:T(8,128)S(1)} %copy.134.table, f32[24,128,128]{2,1,0:T(8,128)S(1)} %copy-done.3, bf16[24,128,128]{2,1,0:T(8,128)(2,1)} %collective-permute-done.13.got, bf16[32,128,128]{2,1,0:T(8,128)(2,1)S(1)} %copy-done.1), custom_call_target="tpu_custom_call" | custom-call | flops 1 | bytes 1 | tf_op jit(solution)/shard_map/pallas_call | solution.py:751
  138.9 4.1 %collective-permute-done.17.two = bf16[8,128,128]{2,1,0:T(8,128)(2,1)} collective-permute-done((bf16[8,128,128]{2,1,0:T(8,128)(2,1)S(1)}, bf16[8,128,128]{2,1,0:T(8,128)(2,1)}, u32[]{:S(2)}, u32[]{:S(2)}) %collective-permute-start.17) | collective-permute-done | bytes 262176 | tf_op jit(solution)/shard_map/ppermute | solution.py:152
  143.0 1.0 shard_map.101.guest_full
  144.0 1.9 %collective-permute-done.15.last_got = bf16[8,128,128]{2,1,0:T(8,128)(2,1)S(1)} collective-permute-done((bf16[8,128,128]{2,1,0:T(8,128)(2,1)}, bf16[8,128,128]{2,1,0:T(8,128)(2,1)S(1)}, u32[]{:S(2)}, u32[]{:S(2)}) %collective-permute-start.15) | collective-permute-done | bytes 262176 | tf_op jit(solution)/shard_map/ppermute | solution.py:152
  146.0 1.9 %shard_map.102 = (f32[16,128,128]{2,1,0:T(8,128)S(1)}, f32[8,128]{1,0:T(8,128)S(1)}) custom-call(s32[32,3]{1,0:T(8,128)S(1)} %copy.135.table, f32[8,128]{1,0:T(8,128)S(1)} %get-tuple-element.94.sums_first, f32[8,128,128]{2,1,0:T(8,128)S(1)} %copy-done.5, bf16[8,128,128]{2,1,0:T(8,128)(2,1)S(1)} %collective-permute-done.15.last_got, ...), custom_call_target="tpu_custom_call" | custom-call | flops 1 | bytes 1 | tf_op jit(solution)/shard_map/pallas_call | solution.py:763
  148.0 0.8 collective-permute-start.19
  148.8 1.0 collective-permute-start.20
  149.9 1.8 %collective-permute-done.19 = f32[8,128]{1,0:T(8,128)S(1)} collective-permute-done((f32[8,128]{1,0:T(8,128)S(1)}, f32[8,128]{1,0:T(8,128)S(1)}, u32[]{:S(2)}, u32[]{:S(2)}) %collective-permute-start.19) | collective-permute-done | bytes 4128 | tf_op jit(solution)/shard_map/ppermute | solution.py:152
  152.0 1.8 %collective-permute-start.21 = (f32[32,128]{1,0:T(8,128)S(1)}, f32[32,128]{1,0:T(8,128)S(1)}, u32[]{:S(2)}, u32[]{:S(2)}) collective-permute-start(f32[32,128]{1,0:T(8,128)S(1)} %constant_dynamic-update-slice_fusion.sums), channel_id=1, source_target_pairs={{0,4},{1,5},{2,6},{3,7},{4,0},{5,1},{6,2},{7,3},{8,12},{9,13},{10,... | collective-permute-start | bytes 49160 | tf_op jit(solution)/shard_map/ppermute | solution.py:152
  153.8 1.2 collective-permute-start.22
  155.0 1.4 collective-permute-start.23
  156.4 2.2 %shard_map.103.image = f32[32,128,128]{2,1,0:T(8,128)S(1)} custom-call(s32[32,2]{1,0:T(8,128)S(1)} %copy-done.7, f32[24,128,128]{2,1,0:T(8,128)S(1)} %get-tuple-element.104.first_own, f32[16,128,128]{2,1,0:T(8,128)S(1)} %get-tuple-element.106.late_own, f32[24,128,128]{2,1,0:T(8,128)S(1)} %collective-permute-done.24.first_sib, ...), custom_call_target="tpu_custom_call" | custom-call | flops 1 | bytes 1 | tf_op jit(solution)/shard_map/pallas_call | solution.py:777
  158.7 1.9 %collective-permute-done.23.across = f32[32,128]{1,0:T(8,128)S(1)} collective-permute-done((f32[32,128]{1,0:T(8,128)S(1)}, f32[32,128]{1,0:T(8,128)S(1)}, u32[]{:S(2)}, u32[]{:S(2)}) %collective-permute-start.23) | collective-permute-done | bytes 16416 | tf_op jit(solution)/shard_map/ppermute | solution.py:152
  160.5 2.6 %shard_map.104 = (f32[32,128,128]{2,1,0:T(8,128)}, f32[32,128,128]{2,1,0:T(8,128)}, f32[1]{0:T(128)}) custom-call(f32[32,128]{1,0:T(8,128)S(1)} %constant_dynamic-update-slice_fusion.sums, f32[32,128]{1,0:T(8,128)S(1)} %collective-permute-done.21.near, f32[32,128]{1,0:T(8,128)S(1)} %collective-permute-done.22.far, ...), custom_call_target="tpu_custom_call" | custom-call | flops 1 | bytes 1 | tf_op jit(solution)/shard_map/pallas_call | solution.py:786
  (123 shorter events, 7.4 us)
Async XLA Ops:
  0.6 9.7 %collective-permute-start = (bf16[7,8,128,128]{3,2,1,0:T(8,128)(2,1)}, bf16[7,8,128,128]{3,2,1,0:T(8,128)(2,1)}, u32[]{:S(2)}, u32[]{:S(2)}) collective-permute-start(bf16[7,8,128,128]{3,2,1,0:T(8,128)(2,1)} %param.11), channel_id=1, source_target_pairs={{1,2},{2,1},{5,6},{6,5},{9,10},{10,9},{13,14},{14,13},{17,18},{18,... | collective-permute-start | bytes 5505032 | tf_op jit(solution)/shard_map/ppermute | solution.py:152
  2.6 7.7 %collective-permute-start.1 = (bf16[7,16]{1,0:T(8,128)(2,1)}, bf16[7,16]{1,0:T(8,128)(2,1)S(1)}, u32[]{:S(2)}, u32[]{:S(2)}) collective-permute-start(bf16[7,16]{1,0:T(8,128)(2,1)} %param.13), channel_id=1, source_target_pairs={{0,1},{1,0},{2,3},{3,2},{4,5},{5,4},{6,7},{7,6},{8,9},{9,8},{10,11... | collective-permute-start | bytes 680 | tf_op jit(solution)/shard_map/ppermute | solution.py:152
  10.3 27.9 %copy-start.15 = (bf16[7,16]{1,0:T(8,128)(2,1)S(1)}, bf16[7,16]{1,0:T(8,128)(2,1)}, u32[]{:S(2)}) copy-start(bf16[7,16]{1,0:T(8,128)(2,1)} %param.13) | copy-start | bytes 676
  12.0 40.1 %copy-start.12 = (bf16[7,8,128,128]{3,2,1,0:T(8,128)(2,1)}, bf16[7,8,128,128]{3,2,1,0:T(8,128)(2,1)S(1)}, u32[]{:S(2)}) copy-start(bf16[7,8,128,128]{3,2,1,0:T(8,128)(2,1)S(1)} %broadcast_select_fusion.left_mine) | copy-start | bytes 5505028
  12.0 42.5 %collective-permute-start.2 = (bf16[7,8,128,128]{3,2,1,0:T(8,128)(2,1)S(1)}, bf16[7,8,128,128]{3,2,1,0:T(8,128)(2,1)}, u32[]{:S(2)}, u32[]{:S(2)}) collective-permute-start(bf16[7,8,128,128]{3,2,1,0:T(8,128)(2,1)S(1)} %broadcast_select_fusion.left_mine), channel_id=1, source_target_pairs={{0,4},{1,5},{2,6},{3,7},{4,8},{5,9},{6,10},{7,11},{8,12},{9,13},{1... | collective-permute-start | bytes 5505032 | tf_op jit(solution)/shard_map/ppermute | solution.py:152
  16.8 37.8 %collective-permute-start.3 = (bf16[7,8,128,128]{3,2,1,0:T(8,128)(2,1)S(1)}, bf16[7,8,128,128]{3,2,1,0:T(8,128)(2,1)}, u32[]{:S(2)}, u32[]{:S(2)}) collective-permute-start(bf16[7,8,128,128]{3,2,1,0:T(8,128)(2,1)S(1)} %broadcast_select_fusion.left_mine), channel_id=1, source_target_pairs={{4,0},{5,1},{6,2},{7,3},{8,4},{9,5},{10,6},{11,7},{12,8},{13,9},{1... | collective-permute-start | bytes 5505032 | tf_op jit(solution)/shard_map/ppermute | solution.py:152
  18.1 21.0 %collective-permute-start.5 = (s32[3,32]{1,0:T(4,128)S(1)}, s32[3,32]{1,0:T(4,128)S(1)}, u32[]{:S(2)}, u32[]{:S(2)}) collective-permute-start(s32[3,32]{1,0:T(4,128)S(1)} %get-tuple-element.57), channel_id=1, source_target_pairs={{0,2},{1,3},{2,0},{3,1},{4,6},{5,7},{6,4},{7,5},{8,10},{9,11},{10,... | collective-permute-start | bytes 1160 | tf_op jit(solution)/shard_map/ppermute | solution.py:152
  36.3 12.7 %collective-permute-start.4 = (bf16[7,8,128,128]{3,2,1,0:T(8,128)(2,1)}, bf16[7,8,128,128]{3,2,1,0:T(8,128)(2,1)}, u32[]{:S(2)}, u32[]{:S(2)}) collective-permute-start(bf16[7,8,128,128]{3,2,1,0:T(8,128)(2,1)} %straight_side.1), channel_id=1, source_target_pairs={{1,2},{2,1},{5,6},{6,5},{9,10},{10,9},{13,14},{14,13},{17,18},{18,... | collective-permute-start | bytes 5505032 | tf_op jit(solution)/shard_map/ppermute | solution.py:152
  42.2 12.3 %collective-permute-start.6 = (bf16[9,128,128]{2,1,0:T(8,128)(2,1)}, bf16[9,128,128]{2,1,0:T(8,128)(2,1)S(1)}, u32[]{:S(2)}, u32[]{:S(2)}) collective-permute-start(bf16[9,128,128]{2,1,0:T(8,128)(2,1)} %shard_map.95), channel_id=1, source_target_pairs={{0,4},{1,5},{2,6},{3,7},{12,8},{13,9},{14,10},{15,11},{16,20},{17,... | collective-permute-start | bytes 884744 | tf_op jit(solution)/shard_map/ppermute | solution.py:152
  47.0 0.6 copy-start.6
  49.0 21.6 %copy-start = (bf16[32,128,128]{2,1,0:T(8,128)(2,1)S(1)}, bf16[32,128,128]{2,1,0:T(8,128)(2,1)}, u32[]{:S(2)}) copy-start(bf16[32,128,128]{2,1,0:T(8,128)(2,1)} %wave.5) | copy-start | bytes 3145732
  54.6 18.3 %collective-permute-start.10 = (bf16[7,8,128,128]{3,2,1,0:T(8,128)(2,1)}, bf16[7,8,128,128]{3,2,1,0:T(8,128)(2,1)}, u32[]{:S(2)}, u32[]{:S(2)}) collective-permute-start(bf16[7,8,128,128]{3,2,1,0:T(8,128)(2,1)} %shard_map.94.right_mine), channel_id=1, source_target_pairs={{0,1},{1,0},{2,3},{3,2},{4,5},{5,4},{6,7},{7,6},{8,9},{9,8},{10,11... | collective-permute-start | bytes 5505032 | tf_op jit(solution)/shard_map/ppermute | solution.py:152
  62.6 44.3 %collective-permute-start.7 = (bf16[7,8,128,128]{3,2,1,0:T(8,128)(2,1)}, bf16[7,8,128,128]{3,2,1,0:T(8,128)(2,1)}, u32[]{:S(2)}, u32[]{:S(2)}) collective-permute-start(bf16[7,8,128,128]{3,2,1,0:T(8,128)(2,1)} %shard_map.94.right_mine), channel_id=1, source_target_pairs={{0,4},{1,5},{2,6},{3,7},{12,8},{13,9},{14,10},{15,11},{16,20},{17,... | collective-permute-start | bytes 5505032 | tf_op jit(solution)/shard_map/ppermute | solution.py:152
  68.5 38.4 %collective-permute-start.8 = (bf16[7,8,128,128]{3,2,1,0:T(8,128)(2,1)}, bf16[7,8,128,128]{3,2,1,0:T(8,128)(2,1)S(1)}, u32[]{:S(2)}, u32[]{:S(2)}) collective-permute-start(bf16[7,8,128,128]{3,2,1,0:T(8,128)(2,1)} %collective-permute-done.2.below), channel_id=1, source_target_pairs={{4,8},{5,9},{6,10},{7,11},{8,12},{9,13},{10,14},{11,15},{20,24},{2... | collective-permute-start | bytes 5505032 | tf_op jit(solution)/shard_map/ppermute | solution.py:152
  69.3 45.8 %collective-permute-start.9 = (bf16[7,8,128,128]{3,2,1,0:T(8,128)(2,1)}, bf16[7,8,128,128]{3,2,1,0:T(8,128)(2,1)}, u32[]{:S(2)}, u32[]{:S(2)}) collective-permute-start(bf16[7,8,128,128]{3,2,1,0:T(8,128)(2,1)} %collective-permute-done.3.above), channel_id=1, source_target_pairs={{4,0},{5,1},{6,2},{7,3},{8,4},{9,5},{10,6},{11,7},{20,16},{21,17},... | collective-permute-start | bytes 5505032 | tf_op jit(solution)/shard_map/ppermute | solution.py:152
  70.6 25.3 %collective-permute-start.12 = (bf16[32,128,128]{2,1,0:T(8,128)(2,1)S(1)}, bf16[32,128,128]{2,1,0:T(8,128)(2,1)}, u32[]{:S(2)}, u32[]{:S(2)}) collective-permute-start(bf16[32,128,128]{2,1,0:T(8,128)(2,1)S(1)} %copy-done), channel_id=1, source_target_pairs={{0,2},{1,3},{2,0},{3,1},{4,6},{5,7},{6,4},{7,5},{8,10},{9,11},{10,... | collective-permute-start | bytes 3145736 | tf_op jit(solution)/shard_map/ppermute | solution.py:152
  82.1 22.9 %collective-permute-start.11 = (bf16[9,128,128]{2,1,0:T(8,128)(2,1)S(1)}, bf16[9,128,128]{2,1,0:T(8,128)(2,1)S(1)}, u32[]{:S(2)}, u32[]{:S(2)}) collective-permute-start(bf16[9,128,128]{2,1,0:T(8,128)(2,1)S(1)} %collective-permute-done.6.wave_own), channel_id=1, source_target_pairs={{4,6},{5,7},{6,4},{7,5},{8,10},{9,11},{10,8},{11,9},{20,22},{21,23... | collective-permute-start | bytes 884744 | tf_op jit(solution)/shard_map/ppermute | solution.py:152
  95.9 20.2 %copy-start.4 = (f32[2,8,7,128]{3,1,2,0:T(8,128)S(1)}, f32[2,8,7,128]{3,1,2,0:T(8,128)}, u32[]{:S(2)}) copy-start(f32[2,8,7,128]{3,1,2,0:T(8,128)} %copy.161) | copy-start | bytes 172036
  95.9 20.2 %copy-start.8 = (s32[3]{0:T(128)S(1)}, s32[3]{0:T(128)}, u32[]{:S(2)}) copy-start(s32[3]{0:T(128)} %add_convert_fusion.3.flags) | copy-start | bytes 40
  106.9 10.8 %copy-start.2 = (bf16[7,8,128,128]{3,2,1,0:T(8,128)(2,1)}, bf16[7,8,128,128]{3,2,1,0:T(8,128)(2,1)S(1)}, u32[]{:S(2)}) copy-start(bf16[7,8,128,128]{3,2,1,0:T(8,128)(2,1)S(1)} %collective-permute-done.8.below) | copy-start | bytes 5505028
  115.0 1.0 collective-permute-start.14
  115.8 20.9 %collective-permute-start.13 = (bf16[24,128,128]{2,1,0:T(8,128)(2,1)}, bf16[24,128,128]{2,1,0:T(8,128)(2,1)}, u32[]{:S(2)}, u32[]{:S(2)}) collective-permute-start(bf16[24,128,128]{2,1,0:T(8,128)(2,1)} %get-tuple-element.78), channel_id=1, source_target_pairs={{0,2},{1,3},{2,0},{3,1},{4,6},{5,7},{6,4},{7,5},{8,10},{9,11},{10,... | collective-permute-start | bytes 2359304 | tf_op jit(solution)/shard_map/ppermute | solution.py:152
  117.8 21.1 %collective-permute-start.16 = (bf16[8,128,128]{2,1,0:T(8,128)(2,1)}, bf16[8,128,128]{2,1,0:T(8,128)(2,1)S(1)}, u32[]{:S(2)}, u32[]{:S(2)}) collective-permute-start(bf16[8,128,128]{2,1,0:T(8,128)(2,1)} %get-tuple-element.86), channel_id=1, source_target_pairs={{4,0},{5,1},{6,2},{7,3},{8,12},{9,13},{10,14},{11,15},{20,16},{21,... | collective-permute-start | bytes 786440 | tf_op jit(solution)/shard_map/ppermute | solution.py:152
  119.7 10.2 %copy-start.14 = (s32[32,3]{0,1:T(4,128)S(1)}, s32[32,3]{0,1:T(4,128)}, u32[]{:S(2)}) copy-start(s32[32,3]{0,1:T(4,128)} %get-tuple-element.62) | copy-start | bytes 1156
  119.7 10.3 %copy-start.13 = (s32[32,3]{0,1:T(4,128)S(1)}, s32[32,3]{0,1:T(4,128)}, u32[]{:S(2)}) copy-start(s32[32,3]{0,1:T(4,128)} %get-tuple-element.61) | copy-start | bytes 1156
  119.7 16.9 %copy-start.1 = (bf16[32,128,128]{2,1,0:T(8,128)(2,1)S(1)}, bf16[32,128,128]{2,1,0:T(8,128)(2,1)}, u32[]{:S(2)}) copy-start(bf16[32,128,128]{2,1,0:T(8,128)(2,1)} %wave.5) | copy-start | bytes 3145732
  119.7 16.9 %copy-start.3 = (f32[24,128,128]{2,1,0:T(8,128)S(1)}, f32[24,128,128]{2,1,0:T(8,128)}, u32[]{:S(2)}) copy-start(f32[24,128,128]{2,1,0:T(8,128)} %get-tuple-element.77.own) | copy-start | bytes 4718596
  119.8 23.3 %collective-permute-start.17 = (bf16[8,128,128]{2,1,0:T(8,128)(2,1)S(1)}, bf16[8,128,128]{2,1,0:T(8,128)(2,1)}, u32[]{:S(2)}, u32[]{:S(2)}) collective-permute-start(bf16[8,128,128]{2,1,0:T(8,128)(2,1)S(1)} %get-tuple-element.97), channel_id=1, source_target_pairs={{4,2},{5,3},{6,0},{7,1},{8,14},{9,15},{10,12},{11,13},{20,18},{21,... | collective-permute-start | bytes 786440 | tf_op jit(solution)/shard_map/ppermute | solution.py:152
  128.0 17.9 %collective-permute-start.15 = (bf16[8,128,128]{2,1,0:T(8,128)(2,1)}, bf16[8,128,128]{2,1,0:T(8,128)(2,1)S(1)}, u32[]{:S(2)}, u32[]{:S(2)}) collective-permute-start(bf16[8,128,128]{2,1,0:T(8,128)(2,1)} %get-tuple-element.95), channel_id=1, source_target_pairs={{0,2},{1,3},{2,0},{3,1},{4,6},{5,7},{6,4},{7,5},{8,10},{9,11},{10,... | collective-permute-start | bytes 786440 | tf_op jit(solution)/shard_map/ppermute | solution.py:152
  138.8 17.6 %collective-permute-start.24 = (f32[24,128,128]{2,1,0:T(8,128)S(1)}, f32[24,128,128]{2,1,0:T(8,128)S(1)}, u32[]{:S(2)}, u32[]{:S(2)}) collective-permute-start(f32[24,128,128]{2,1,0:T(8,128)S(1)} %get-tuple-element.104.first_own), channel_id=1, source_target_pairs={{0,1},{1,0},{2,3},{3,2},{4,5},{5,4},{6,7},{7,6},{8,9},{9,8},{10,11... | collective-permute-start | bytes 4718600 | tf_op jit(solution)/shard_map/ppermute | solution.py:152
  138.9 7.1 %copy-start.5 = (f32[8,128,128]{2,1,0:T(8,128)S(1)}, f32[8,128,128]{2,1,0:T(8,128)}, u32[]{:S(2)}) copy-start(f32[8,128,128]{2,1,0:T(8,128)} %get-tuple-element.92.last_own) | copy-start | bytes 1572868
  138.9 7.1 %copy-start.9 = (f32[8,128]{1,0:T(8,128)S(1)}, f32[8,128]{1,0:T(8,128)}, u32[]{:S(2)}) copy-start(f32[8,128]{1,0:T(8,128)} %get-tuple-element.98.map_a) | copy-start | bytes 12292
  138.9 7.1 %copy-start.10 = (f32[8,128]{1,0:T(8,128)S(1)}, f32[8,128]{1,0:T(8,128)}, u32[]{:S(2)}) copy-start(f32[8,128]{1,0:T(8,128)} %get-tuple-element.99.map_b) | copy-start | bytes 12292
  138.9 7.1 %copy-start.11 = (f32[8,128]{1,0:T(8,128)S(1)}, f32[8,128]{1,0:T(8,128)}, u32[]{:S(2)}) copy-start(f32[8,128]{1,0:T(8,128)} %get-tuple-element.101.map_d) | copy-start | bytes 12292
  144.0 12.4 %copy-start.7 = (s32[32,2]{1,0:T(8,128)S(1)}, s32[32,2]{1,0:T(8,128)}, u32[]{:S(2)}) copy-start(s32[32,2]{1,0:T(8,128)} %copy-done.6) | copy-start | bytes 772
  147.9 1.9 %collective-permute-start.18 = (f32[8,128]{1,0:T(8,128)S(1)}, f32[8,128]{1,0:T(8,128)S(1)}, u32[]{:S(2)}, u32[]{:S(2)}) collective-permute-start(f32[8,128]{1,0:T(8,128)S(1)} %get-tuple-element.102), channel_id=1, source_target_pairs={{0,1},{1,0},{2,3},{3,2},{4,5},{5,4},{6,7},{7,6},{8,9},{9,8},{10,11... | collective-permute-start | bytes 12296 | tf_op jit(solution)/shard_map/ppermute | solution.py:152
  148.0 3.7 %collective-permute-start.19 = (f32[8,128]{1,0:T(8,128)S(1)}, f32[8,128]{1,0:T(8,128)S(1)}, u32[]{:S(2)}, u32[]{:S(2)}) collective-permute-start(f32[8,128]{1,0:T(8,128)S(1)} %get-tuple-element.102), channel_id=1, source_target_pairs={{0,2},{1,3},{2,0},{3,1},{4,6},{5,7},{6,4},{7,5},{8,10},{9,11},{10,... | collective-permute-start | bytes 12296 | tf_op jit(solution)/shard_map/ppermute | solution.py:152
  148.8 3.1 %collective-permute-start.20 = (f32[8,128]{1,0:T(8,128)S(1)}, f32[8,128]{1,0:T(8,128)S(1)}, u32[]{:S(2)}, u32[]{:S(2)}) collective-permute-start(f32[8,128]{1,0:T(8,128)S(1)} %get-tuple-element.102), channel_id=1, source_target_pairs={{0,3},{1,2},{2,1},{3,0},{4,7},{5,6},{6,5},{7,4},{8,11},{9,10},{10,... | collective-permute-start | bytes 12296 | tf_op jit(solution)/shard_map/ppermute | solution.py:152
  151.9 4.5 %collective-permute-start.25 = (f32[16,128,128]{2,1,0:T(8,128)S(1)}, f32[16,128,128]{2,1,0:T(8,128)S(1)}, u32[]{:S(2)}, u32[]{:S(2)}) collective-permute-start(f32[16,128,128]{2,1,0:T(8,128)S(1)} %get-tuple-element.106.late_own), channel_id=1, source_target_pairs={{0,1},{1,0},{2,3},{3,2},{4,5},{5,4},{6,7},{7,6},{8,9},{9,8},{10,11... | collective-permute-start | bytes 3145736 | tf_op jit(solution)/shard_map/ppermute | solution.py:152
  152.0 6.6 %collective-permute-start.21 = (f32[32,128]{1,0:T(8,128)S(1)}, f32[32,128]{1,0:T(8,128)S(1)}, u32[]{:S(2)}, u32[]{:S(2)}) collective-permute-start(f32[32,128]{1,0:T(8,128)S(1)} %constant_dynamic-update-slice_fusion.sums), channel_id=1, source_target_pairs={{0,4},{1,5},{2,6},{3,7},{4,0},{5,1},{6,2},{7,3},{8,12},{9,13},{10,... | collective-permute-start | bytes 49160 | tf_op jit(solution)/shard_map/ppermute | solution.py:152
  153.8 4.9 %collective-permute-start.22 = (f32[32,128]{1,0:T(8,128)S(1)}, f32[32,128]{1,0:T(8,128)S(1)}, u32[]{:S(2)}, u32[]{:S(2)}) collective-permute-start(f32[32,128]{1,0:T(8,128)S(1)} %constant_dynamic-update-slice_fusion.sums), channel_id=1, source_target_pairs={{0,8},{1,9},{2,10},{3,11},{4,12},{5,13},{6,14},{7,15},{8,0},{9,1},... | collective-permute-start | bytes 49160 | tf_op jit(solution)/shard_map/ppermute | solution.py:152
  155.0 5.5 %collective-permute-start.23 = (f32[32,128]{1,0:T(8,128)S(1)}, f32[32,128]{1,0:T(8,128)S(1)}, u32[]{:S(2)}, u32[]{:S(2)}) collective-permute-start(f32[32,128]{1,0:T(8,128)S(1)} %constant_dynamic-update-slice_fusion.sums), channel_id=1, source_target_pairs={{0,12},{1,13},{2,14},{3,15},{4,8},{5,9},{6,10},{7,11},{8,4},{9,5},... | collective-permute-start | bytes 49160 | tf_op jit(solution)/shard_map/ppermute | solution.py:152

commit v6 on v5

--- a/solution.py
+++ b/solution.py
@@ -594,7 +594,7 @@
     below = hop(left_mine, up)
     above = hop(left_mine, down)
 
-    right_n = move(after(right_environment, left_mine), DIAGONAL)
+    right_n = move(after(right_environment, left_n), DIAGONAL)
     right_mine = call(
         select_kernel,
         jax.ShapeDtypeStruct(env, bf16),

time: 164 us -> 164 us (level)
    pallas_call x1, Pallas kernels: 6.71 us -> 4.99 us  [on_device(): call(far_kernel, (last, last_sent, map_shape), [SMEM] * 2 + [HBM] * 8, (V...]
  transfers between devices with their start and end apart: 26 -> 26, of which waited for: 10 -> 9; matrix products, arithmetic and copies ran while one was open for 6% -> 6% of each run, Pallas kernels for 24% -> 24%
where the time goes in v6:
time: 164 us; the launch traced here: 163 us
  starting transfers between devices  66.9 us (41%)
  waiting for transfers between devices  41.8 us (25%)
  Pallas kernels  41.3 us (25%)
  local copies, waits for them, and re-layouts  5.83 us (4%)
  other arithmetic  4.94 us (3%)
    ppermute x26, starting transfers between devices, move(): return lax.ppermute(array, BOTH, pairs)  66.9 us
    ppermute x26, waiting for transfers between devices, move(): return lax.ppermute(array, BOTH, pairs)  41.8 us
    pallas_call x2, Pallas kernels, near(): call(near_kernel, (jax.ShapeDtypeStruct((first_slots,) + square, kind), j...  19.8 us
    pallas_call x1, Pallas kernels, on_device(): call(far_kernel, (last, last_sent, map_shape), [SMEM] * 2 + [HBM] * 8, (V...  4.99 us
  transfers between devices with their start and end apart: 26, of which 9 were waited for; matrix products, arithmetic and copies ran while one was open for 6% of the time, Pallas kernels for 24%

profile of v6, /device:TPU:0, one launch (start us, length us, event | category | flops | bytes accessed | tf_op | source)
XLA Modules:
  0.0 163.0 jit_solution(16398728156311464964)
XLA Ops:
  0.6 1.9 %collective-permute-start = (bf16[7,8,128,128]{3,2,1,0:T(8,128)(2,1)}, bf16[7,8,128,128]{3,2,1,0:T(8,128)(2,1)}, u32[]{:S(2)}, u32[]{:S(2)}) collective-permute-start(bf16[7,8,128,128]{3,2,1,0:T(8,128)(2,1)} %param.11), channel_id=1, source_target_pairs={{1,2},{2,1},{5,6},{6,5},{9,10},{10,9},{13,14},{14,13},{17,18},{18,... | collective-permute-start | bytes 5505032 | tf_op jit(solution)/shard_map/ppermute | solution.py:152
  2.6 3.1 %collective-permute-start.1 = (bf16[7,16]{1,0:T(8,128)(2,1)}, bf16[7,16]{1,0:T(8,128)(2,1)S(1)}, u32[]{:S(2)}, u32[]{:S(2)}) collective-permute-start(bf16[7,16]{1,0:T(8,128)(2,1)} %param.13), channel_id=1, source_target_pairs={{0,1},{1,0},{2,3},{3,2},{4,5},{5,4},{6,7},{7,6},{8,9},{9,8},{10,11... | collective-permute-start | bytes 680 | tf_op jit(solution)/shard_map/ppermute | solution.py:152
  5.7 0.7 subtract_bitcast_fusion
  6.4 0.7 pad_add_fusion
  7.4 0.7 stack.111
  8.3 0.7 fusion.39
  10.3 1.7 %broadcast_select_fusion.left_mine = bf16[7,8,128,128]{3,2,1,0:T(8,128)(2,1)S(1)} fusion(bf16[7,8,128,128]{3,2,1,0:T(8,128)(2,1)} %param.11, bf16[7,8,128,128]{3,2,1,0:T(8,128)(2,1)} %collective-permute-done, pred[]{:T(512)} %eq.284), kind=kLoop, calls=%fused_computation | loop fusion | flops 917504 | bytes 5505025 | tf_op jit(solution)/shard_map/jit(_where)/select_n | solution.py:557
  12.0 4.8 %collective-permute-start.2 = (bf16[7,8,128,128]{3,2,1,0:T(8,128)(2,1)S(1)}, bf16[7,8,128,128]{3,2,1,0:T(8,128)(2,1)}, u32[]{:S(2)}, u32[]{:S(2)}) collective-permute-start(bf16[7,8,128,128]{3,2,1,0:T(8,128)(2,1)S(1)} %broadcast_select_fusion.left_mine), channel_id=1, source_target_pairs={{0,4},{1,5},{2,6},{3,7},{4,8},{5,9},{6,10},{7,11},{8,12},{9,13},{1... | collective-permute-start | bytes 5505032 | tf_op jit(solution)/shard_map/ppermute | solution.py:152
  16.8 1.3 collective-permute-start.3
  18.1 18.2 %collective-permute-start.5 = (s32[3,32]{1,0:T(4,128)S(1)}, s32[3,32]{1,0:T(4,128)S(1)}, u32[]{:S(2)}, u32[]{:S(2)}) collective-permute-start(s32[3,32]{1,0:T(4,128)S(1)} %get-tuple-element.57), channel_id=1, source_target_pairs={{0,2},{1,3},{2,0},{3,1},{4,6},{5,7},{6,4},{7,5},{8,10},{9,11},{10,... | collective-permute-start | bytes 1160 | tf_op jit(solution)/shard_map/ppermute | solution.py:152
  36.3 1.9 %collective-permute-start.4 = (bf16[7,8,128,128]{3,2,1,0:T(8,128)(2,1)}, bf16[7,8,128,128]{3,2,1,0:T(8,128)(2,1)}, u32[]{:S(2)}, u32[]{:S(2)}) collective-permute-start(bf16[7,8,128,128]{3,2,1,0:T(8,128)(2,1)} %straight_side.1), channel_id=1, source_target_pairs={{1,2},{2,1},{5,6},{6,5},{9,10},{10,9},{13,14},{14,13},{17,18},{18,... | collective-permute-start | bytes 5505032 | tf_op jit(solution)/shard_map/ppermute | solution.py:152
  38.4 0.6 copy.161
  40.2 2.0 %shard_map.95 = bf16[9,128,128]{2,1,0:T(8,128)(2,1)} custom-call(s32[8,6]{1,0:T(8,128)} %get-tuple-element.146.table, bf16[32,128,128]{2,1,0:T(8,128)(2,1)} %wave.5, bf16[1,128,128]{2,1,0:T(8,128)(2,1)} %pad_bitcast_fusion.facts), custom_call_target="tpu_custom_call" | custom-call | flops 1 | bytes 1 | tf_op jit(solution)/shard_map/pallas_call | solution.py:613
  42.2 4.6 %collective-permute-start.6 = (bf16[9,128,128]{2,1,0:T(8,128)(2,1)}, bf16[9,128,128]{2,1,0:T(8,128)(2,1)S(1)}, u32[]{:S(2)}, u32[]{:S(2)}) collective-permute-start(bf16[9,128,128]{2,1,0:T(8,128)(2,1)} %shard_map.95), channel_id=1, source_target_pairs={{0,4},{1,5},{2,6},{3,7},{12,8},{13,9},{14,10},{15,11},{16,20},{17,... | collective-permute-start | bytes 884744 | tf_op jit(solution)/shard_map/ppermute | solution.py:152
  49.0 3.1 %shard_map.94.right_mine = bf16[7,8,128,128]{3,2,1,0:T(8,128)(2,1)} custom-call(s32[3]{0:T(128)} %add_convert_fusion.3.flags, bf16[7,8,128,128]{3,2,1,0:T(8,128)(2,1)} %straight_side.1, bf16[7,8,128,128]{3,2,1,0:T(8,128)(2,1)} %collective-permute-done.4.crossed_side), custom_call_target="tpu_custom_call" | custom-call | flops 1 | bytes 1 | tf_op jit(solution)/shard_map/pallas_call | solution.py:598
  52.1 2.4 %collective-permute-done.6.wave_own = bf16[9,128,128]{2,1,0:T(8,128)(2,1)S(1)} collective-permute-done((bf16[9,128,128]{2,1,0:T(8,128)(2,1)}, bf16[9,128,128]{2,1,0:T(8,128)(2,1)S(1)}, u32[]{:S(2)}, u32[]{:S(2)}) %collective-permute-start.6) | collective-permute-done | bytes 294944 | tf_op jit(solution)/shard_map/ppermute | solution.py:152
  54.6 8.1 %collective-permute-start.10 = (bf16[7,8,128,128]{3,2,1,0:T(8,128)(2,1)}, bf16[7,8,128,128]{3,2,1,0:T(8,128)(2,1)}, u32[]{:S(2)}, u32[]{:S(2)}) collective-permute-start(bf16[7,8,128,128]{3,2,1,0:T(8,128)(2,1)} %shard_map.94.right_mine), channel_id=1, source_target_pairs={{0,1},{1,0},{2,3},{3,2},{4,5},{5,4},{6,7},{7,6},{8,9},{9,8},{10,11... | collective-permute-start | bytes 5505032 | tf_op jit(solution)/shard_map/ppermute | solution.py:152
  62.6 5.8 %collective-permute-start.7 = (bf16[7,8,128,128]{3,2,1,0:T(8,128)(2,1)}, bf16[7,8,128,128]{3,2,1,0:T(8,128)(2,1)}, u32[]{:S(2)}, u32[]{:S(2)}) collective-permute-start(bf16[7,8,128,128]{3,2,1,0:T(8,128)(2,1)} %shard_map.94.right_mine), channel_id=1, source_target_pairs={{0,4},{1,5},{2,6},{3,7},{12,8},{13,9},{14,10},{15,11},{16,20},{17,... | collective-permute-start | bytes 5505032 | tf_op jit(solution)/shard_map/ppermute | solution.py:152
  68.5 0.8 collective-permute-start.8
  69.3 1.3 collective-permute-start.9
  70.6 1.7 %collective-permute-start.12 = (bf16[32,128,128]{2,1,0:T(8,128)(2,1)S(1)}, bf16[32,128,128]{2,1,0:T(8,128)(2,1)}, u32[]{:S(2)}, u32[]{:S(2)}) collective-permute-start(bf16[32,128,128]{2,1,0:T(8,128)(2,1)S(1)} %copy-done), channel_id=1, source_target_pairs={{0,2},{1,3},{2,0},{3,1},{4,6},{5,7},{6,4},{7,5},{8,10},{9,11},{10,... | collective-permute-start | bytes 3145736 | tf_op jit(solution)/shard_map/ppermute | solution.py:152
  72.9 10.5 %shard_map.96 = (f32[24,128,128]{2,1,0:T(8,128)}, f32[8,128,128]{2,1,0:T(8,128)}, bf16[8,128,896]{2,1,0:T(8,128)(2,1)}, f32[8,128]{1,0:T(8,128)}) custom-call(s32[32,6]{1,0:T(8,128)} %get-tuple-element.126.table, f32[16,896]{1,0:T(8,128)} %bitcast.117, bf16[32,128,128]{2,1,0:T(8,128)(2,1)} %wave.5, bf16[7,8,128,128]{3,2,1,0:T(8,128)(2,1)} %shard_map.94.right_mine, ...), custom_call_target="tpu_custom_call" | custom-call | flops 1 | bytes 1 | tf_op jit(solution)/shard_map/pallas_call | solution.py:673
  83.4 0.7 collective-permute-start.11
  84.1 11.8 %collective-permute-done.12.wave_in.wave_other = bf16[32,128,128]{2,1,0:T(8,128)(2,1)} collective-permute-done((bf16[32,128,128]{2,1,0:T(8,128)(2,1)S(1)}, bf16[32,128,128]{2,1,0:T(8,128)(2,1)}, u32[]{:S(2)}, u32[]{:S(2)}) %collective-permute-start.12) | collective-permute-done | bytes 1048608 | tf_op jit(solution)/shard_map/ppermute | solution.py:152
  95.9 9.3 %shard_map.97 = (bf16[24,128,128]{2,1,0:T(8,128)(2,1)}, bf16[8,128,128]{2,1,0:T(8,128)(2,1)}, bf16[8,128,896]{2,1,0:T(8,128)(2,1)}, f32[8,128]{1,0:T(8,128)}) custom-call(s32[32,6]{1,0:T(8,128)} %get-tuple-element.125.table, f32[16,896]{1,0:T(8,128)} %bitcast.118, bf16[32,128,128]{2,1,0:T(8,128)(2,1)} %collective-permute-done.12.wave_in.wave_other, ...), custom_call_target="tpu_custom_call" | custom-call | flops 1 | bytes 1 | tf_op jit(solution)/shard_map/pallas_call | solution.py:673
  105.3 1.7 %collective-permute-done.7.right_mine = bf16[7,8,128,128]{3,2,1,0:T(8,128)(2,1)} collective-permute-done((bf16[7,8,128,128]{3,2,1,0:T(8,128)(2,1)}, bf16[7,8,128,128]{3,2,1,0:T(8,128)(2,1)}, u32[]{:S(2)}, u32[]{:S(2)}) %collective-permute-start.7) | collective-permute-done | bytes 1835040 | tf_op jit(solution)/shard_map/ppermute | solution.py:152
  106.9 8.1 %collective-permute-done.9.above = bf16[7,8,128,128]{3,2,1,0:T(8,128)(2,1)} collective-permute-done((bf16[7,8,128,128]{3,2,1,0:T(8,128)(2,1)}, bf16[7,8,128,128]{3,2,1,0:T(8,128)(2,1)}, u32[]{:S(2)}, u32[]{:S(2)}) %collective-permute-start.9) | collective-permute-done | bytes 1835040 | tf_op jit(solution)/shard_map/ppermute | solution.py:152
  115.0 0.8 collective-permute-start.14
  116.1 1.7 %shard_map.98 = (bf16[8,128,128]{2,1,0:T(8,128)(2,1)}, bf16[8,128,128]{2,1,0:T(8,128)(2,1)S(1)}, f32[8,128]{1,0:T(8,128)S(1)}) custom-call(s32[3]{0:T(128)S(1)} %copy-done.8, s32[16,6]{1,0:T(8,128)S(1)} %maximum_convert_fusion.table, f32[16,896]{1,0:T(8,128)S(1)} %bitcast.119, bf16[7,8,128,128]{3,2,1,0:T(8,128)(2,1)S(1)} %collective-permute-done.8.below, ...), custom_call_target="tpu_custom_call" | custom-call | flops 1 | bytes 1 | tf_op jit(solution)/shard_map/pallas_call | solution.py:713
  117.8 1.3 collective-permute-start.16
  119.1 0.7 copy.133.table
  119.8 1.6 collective-permute-start.17
  121.3 5.0 %shard_map.99 = (f32[8,128,128]{2,1,0:T(8,128)}, bf16[8,128,128]{2,1,0:T(8,128)(2,1)}, f32[8,128]{1,0:T(8,128)}) custom-call(s32[3]{0:T(128)} %add_convert_fusion.3.flags, s32[16,6]{1,0:T(8,128)} %copy.133.table, bf16[8,128,896]{2,1,0:T(8,128)(2,1)} %get-tuple-element.88.carried_own, bf16[8,128,896]{2,1,0:T(8,128)(2,1)} %get-tuple-element.89.carried_other, ...), custom_call_target="tpu_custom_call" | custom-call | flops 137438953472 | bytes 1 | tf_op jit(solution)/shard_map/pallas_call | solution.py:732
  126.3 1.9 %collective-permute-start.15 = (bf16[8,128,128]{2,1,0:T(8,128)(2,1)}, bf16[8,128,128]{2,1,0:T(8,128)(2,1)S(1)}, u32[]{:S(2)}, u32[]{:S(2)}) collective-permute-start(bf16[8,128,128]{2,1,0:T(8,128)(2,1)} %get-tuple-element.95), channel_id=1, source_target_pairs={{0,2},{1,3},{2,0},{3,1},{4,6},{5,7},{6,4},{7,5},{8,10},{9,11},{10,... | collective-permute-start | bytes 786440 | tf_op jit(solution)/shard_map/ppermute | solution.py:152
  128.4 8.3 %collective-permute-done.13.got = bf16[24,128,128]{2,1,0:T(8,128)(2,1)} collective-permute-done((bf16[24,128,128]{2,1,0:T(8,128)(2,1)}, bf16[24,128,128]{2,1,0:T(8,128)(2,1)}, u32[]{:S(2)}, u32[]{:S(2)}) %collective-permute-start.13) | collective-permute-done | bytes 786464 | tf_op jit(solution)/shard_map/ppermute | solution.py:152
  136.7 1.9 %shard_map.100 = (f32[24,128,128]{2,1,0:T(8,128)S(1)}, f32[8,128]{1,0:T(8,128)S(1)}) custom-call(s32[32,3]{1,0:T(8,128)S(1)} %copy.134.table, f32[24,128,128]{2,1,0:T(8,128)S(1)} %copy-done.3, bf16[24,128,128]{2,1,0:T(8,128)(2,1)} %collective-permute-done.13.got, bf16[32,128,128]{2,1,0:T(8,128)(2,1)S(1)} %copy-done.1), custom_call_target="tpu_custom_call" | custom-call | flops 1 | bytes 1 | tf_op jit(solution)/shard_map/pallas_call | solution.py:751
  138.7 4.3 %collective-permute-done.17.two = bf16[8,128,128]{2,1,0:T(8,128)(2,1)} collective-permute-done((bf16[8,128,128]{2,1,0:T(8,128)(2,1)S(1)}, bf16[8,128,128]{2,1,0:T(8,128)(2,1)}, u32[]{:S(2)}, u32[]{:S(2)}) %collective-permute-start.17) | collective-permute-done | bytes 262176 | tf_op jit(solution)/shard_map/ppermute | solution.py:152
  143.0 1.0 shard_map.101.guest_full
  144.0 1.9 %collective-permute-done.15.last_got = bf16[8,128,128]{2,1,0:T(8,128)(2,1)S(1)} collective-permute-done((bf16[8,128,128]{2,1,0:T(8,128)(2,1)}, bf16[8,128,128]{2,1,0:T(8,128)(2,1)S(1)}, u32[]{:S(2)}, u32[]{:S(2)}) %collective-permute-start.15) | collective-permute-done | bytes 262176 | tf_op jit(solution)/shard_map/ppermute | solution.py:152
  146.0 2.0 %shard_map.102 = (f32[16,128,128]{2,1,0:T(8,128)S(1)}, f32[8,128]{1,0:T(8,128)S(1)}) custom-call(s32[32,3]{1,0:T(8,128)S(1)} %copy.135.table, f32[8,128]{1,0:T(8,128)S(1)} %get-tuple-element.94.sums_first, f32[8,128,128]{2,1,0:T(8,128)S(1)} %copy-done.5, bf16[8,128,128]{2,1,0:T(8,128)(2,1)S(1)} %collective-permute-done.15.last_got, ...), custom_call_target="tpu_custom_call" | custom-call | flops 1 | bytes 1 | tf_op jit(solution)/shard_map/pallas_call | solution.py:763
  148.6 1.3 collective-permute-start.20
  149.9 1.8 %collective-permute-done.19 = f32[8,128]{1,0:T(8,128)S(1)} collective-permute-done((f32[8,128]{1,0:T(8,128)S(1)}, f32[8,128]{1,0:T(8,128)S(1)}, u32[]{:S(2)}, u32[]{:S(2)}) %collective-permute-start.19) | collective-permute-done | bytes 4128 | tf_op jit(solution)/shard_map/ppermute | solution.py:152
  151.8 2.4 %collective-permute-start.21 = (f32[32,128]{1,0:T(8,128)S(1)}, f32[32,128]{1,0:T(8,128)S(1)}, u32[]{:S(2)}, u32[]{:S(2)}) collective-permute-start(f32[32,128]{1,0:T(8,128)S(1)} %constant_dynamic-update-slice_fusion.sums), channel_id=1, source_target_pairs={{0,4},{1,5},{2,6},{3,7},{4,0},{5,1},{6,2},{7,3},{8,12},{9,13},{10,... | collective-permute-start | bytes 49160 | tf_op jit(solution)/shard_map/ppermute | solution.py:152
  154.2 0.7 collective-permute-start.22
  154.9 1.8 %collective-permute-start.23 = (f32[32,128]{1,0:T(8,128)S(1)}, f32[32,128]{1,0:T(8,128)S(1)}, u32[]{:S(2)}, u32[]{:S(2)}) collective-permute-start(f32[32,128]{1,0:T(8,128)S(1)} %constant_dynamic-update-slice_fusion.sums), channel_id=1, source_target_pairs={{0,12},{1,13},{2,14},{3,15},{4,8},{5,9},{6,10},{7,11},{8,4},{9,5},... | collective-permute-start | bytes 49160 | tf_op jit(solution)/shard_map/ppermute | solution.py:152
  156.7 2.2 %shard_map.103.image = f32[32,128,128]{2,1,0:T(8,128)S(1)} custom-call(s32[32,2]{1,0:T(8,128)S(1)} %copy-done.7, f32[24,128,128]{2,1,0:T(8,128)S(1)} %get-tuple-element.104.first_own, f32[16,128,128]{2,1,0:T(8,128)S(1)} %get-tuple-element.106.late_own, f32[24,128,128]{2,1,0:T(8,128)S(1)} %collective-permute-done.24.first_sib, ...), custom_call_target="tpu_custom_call" | custom-call | flops 1 | bytes 1 | tf_op jit(solution)/shard_map/pallas_call | solution.py:777
  158.9 1.5 collective-permute-done.23.across
  160.4 2.6 %shard_map.104 = (f32[32,128,128]{2,1,0:T(8,128)}, f32[32,128,128]{2,1,0:T(8,128)}, f32[1]{0:T(128)}) custom-call(f32[32,128]{1,0:T(8,128)S(1)} %constant_dynamic-update-slice_fusion.sums, f32[32,128]{1,0:T(8,128)S(1)} %collective-permute-done.21.near, f32[32,128]{1,0:T(8,128)S(1)} %collective-permute-done.22.far, ...), custom_call_target="tpu_custom_call" | custom-call | flops 1 | bytes 1 | tf_op jit(solution)/shard_map/pallas_call | solution.py:786
  (123 shorter events, 7.1 us)
Async XLA Ops:
  0.6 9.7 %collective-permute-start = (bf16[7,8,128,128]{3,2,1,0:T(8,128)(2,1)}, bf16[7,8,128,128]{3,2,1,0:T(8,128)(2,1)}, u32[]{:S(2)}, u32[]{:S(2)}) collective-permute-start(bf16[7,8,128,128]{3,2,1,0:T(8,128)(2,1)} %param.11), channel_id=1, source_target_pairs={{1,2},{2,1},{5,6},{6,5},{9,10},{10,9},{13,14},{14,13},{17,18},{18,... | collective-permute-start | bytes 5505032 | tf_op jit(solution)/shard_map/ppermute | solution.py:152
  2.6 7.7 %collective-permute-start.1 = (bf16[7,16]{1,0:T(8,128)(2,1)}, bf16[7,16]{1,0:T(8,128)(2,1)S(1)}, u32[]{:S(2)}, u32[]{:S(2)}) collective-permute-start(bf16[7,16]{1,0:T(8,128)(2,1)} %param.13), channel_id=1, source_target_pairs={{0,1},{1,0},{2,3},{3,2},{4,5},{5,4},{6,7},{7,6},{8,9},{9,8},{10,11... | collective-permute-start | bytes 680 | tf_op jit(solution)/shard_map/ppermute | solution.py:152
  10.3 27.9 %copy-start.15 = (bf16[7,16]{1,0:T(8,128)(2,1)S(1)}, bf16[7,16]{1,0:T(8,128)(2,1)}, u32[]{:S(2)}) copy-start(bf16[7,16]{1,0:T(8,128)(2,1)} %param.13) | copy-start | bytes 676
  12.0 40.1 %copy-start.12 = (bf16[7,8,128,128]{3,2,1,0:T(8,128)(2,1)}, bf16[7,8,128,128]{3,2,1,0:T(8,128)(2,1)S(1)}, u32[]{:S(2)}) copy-start(bf16[7,8,128,128]{3,2,1,0:T(8,128)(2,1)S(1)} %broadcast_select_fusion.left_mine) | copy-start | bytes 5505028
  12.0 42.5 %collective-permute-start.2 = (bf16[7,8,128,128]{3,2,1,0:T(8,128)(2,1)S(1)}, bf16[7,8,128,128]{3,2,1,0:T(8,128)(2,1)}, u32[]{:S(2)}, u32[]{:S(2)}) collective-permute-start(bf16[7,8,128,128]{3,2,1,0:T(8,128)(2,1)S(1)} %broadcast_select_fusion.left_mine), channel_id=1, source_target_pairs={{0,4},{1,5},{2,6},{3,7},{4,8},{5,9},{6,10},{7,11},{8,12},{9,13},{1... | collective-permute-start | bytes 5505032 | tf_op jit(solution)/shard_map/ppermute | solution.py:152
  16.8 37.8 %collective-permute-start.3 = (bf16[7,8,128,128]{3,2,1,0:T(8,128)(2,1)S(1)}, bf16[7,8,128,128]{3,2,1,0:T(8,128)(2,1)}, u32[]{:S(2)}, u32[]{:S(2)}) collective-permute-start(bf16[7,8,128,128]{3,2,1,0:T(8,128)(2,1)S(1)} %broadcast_select_fusion.left_mine), channel_id=1, source_target_pairs={{4,0},{5,1},{6,2},{7,3},{8,4},{9,5},{10,6},{11,7},{12,8},{13,9},{1... | collective-permute-start | bytes 5505032 | tf_op jit(solution)/shard_map/ppermute | solution.py:152
  18.1 21.0 %collective-permute-start.5 = (s32[3,32]{1,0:T(4,128)S(1)}, s32[3,32]{1,0:T(4,128)S(1)}, u32[]{:S(2)}, u32[]{:S(2)}) collective-permute-start(s32[3,32]{1,0:T(4,128)S(1)} %get-tuple-element.57), channel_id=1, source_target_pairs={{0,2},{1,3},{2,0},{3,1},{4,6},{5,7},{6,4},{7,5},{8,10},{9,11},{10,... | collective-permute-start | bytes 1160 | tf_op jit(solution)/shard_map/ppermute | solution.py:152
  36.3 12.7 %collective-permute-start.4 = (bf16[7,8,128,128]{3,2,1,0:T(8,128)(2,1)}, bf16[7,8,128,128]{3,2,1,0:T(8,128)(2,1)}, u32[]{:S(2)}, u32[]{:S(2)}) collective-permute-start(bf16[7,8,128,128]{3,2,1,0:T(8,128)(2,1)} %straight_side.1), channel_id=1, source_target_pairs={{1,2},{2,1},{5,6},{6,5},{9,10},{10,9},{13,14},{14,13},{17,18},{18,... | collective-permute-start | bytes 5505032 | tf_op jit(solution)/shard_map/ppermute | solution.py:152
  42.2 12.3 %collective-permute-start.6 = (bf16[9,128,128]{2,1,0:T(8,128)(2,1)}, bf16[9,128,128]{2,1,0:T(8,128)(2,1)S(1)}, u32[]{:S(2)}, u32[]{:S(2)}) collective-permute-start(bf16[9,128,128]{2,1,0:T(8,128)(2,1)} %shard_map.95), channel_id=1, source_target_pairs={{0,4},{1,5},{2,6},{3,7},{12,8},{13,9},{14,10},{15,11},{16,20},{17,... | collective-permute-start | bytes 884744 | tf_op jit(solution)/shard_map/ppermute | solution.py:152
  47.0 0.6 copy-start.6
  49.0 21.6 %copy-start = (bf16[32,128,128]{2,1,0:T(8,128)(2,1)S(1)}, bf16[32,128,128]{2,1,0:T(8,128)(2,1)}, u32[]{:S(2)}) copy-start(bf16[32,128,128]{2,1,0:T(8,128)(2,1)} %wave.5) | copy-start | bytes 3145732
  54.6 18.3 %collective-permute-start.10 = (bf16[7,8,128,128]{3,2,1,0:T(8,128)(2,1)}, bf16[7,8,128,128]{3,2,1,0:T(8,128)(2,1)}, u32[]{:S(2)}, u32[]{:S(2)}) collective-permute-start(bf16[7,8,128,128]{3,2,1,0:T(8,128)(2,1)} %shard_map.94.right_mine), channel_id=1, source_target_pairs={{0,1},{1,0},{2,3},{3,2},{4,5},{5,4},{6,7},{7,6},{8,9},{9,8},{10,11... | collective-permute-start | bytes 5505032 | tf_op jit(solution)/shard_map/ppermute | solution.py:152
  62.6 44.3 %collective-permute-start.7 = (bf16[7,8,128,128]{3,2,1,0:T(8,128)(2,1)}, bf16[7,8,128,128]{3,2,1,0:T(8,128)(2,1)}, u32[]{:S(2)}, u32[]{:S(2)}) collective-permute-start(bf16[7,8,128,128]{3,2,1,0:T(8,128)(2,1)} %shard_map.94.right_mine), channel_id=1, source_target_pairs={{0,4},{1,5},{2,6},{3,7},{12,8},{13,9},{14,10},{15,11},{16,20},{17,... | collective-permute-start | bytes 5505032 | tf_op jit(solution)/shard_map/ppermute | solution.py:152
  68.5 38.4 %collective-permute-start.8 = (bf16[7,8,128,128]{3,2,1,0:T(8,128)(2,1)}, bf16[7,8,128,128]{3,2,1,0:T(8,128)(2,1)S(1)}, u32[]{:S(2)}, u32[]{:S(2)}) collective-permute-start(bf16[7,8,128,128]{3,2,1,0:T(8,128)(2,1)} %collective-permute-done.2.below), channel_id=1, source_target_pairs={{4,8},{5,9},{6,10},{7,11},{8,12},{9,13},{10,14},{11,15},{20,24},{2... | collective-permute-start | bytes 5505032 | tf_op jit(solution)/shard_map/ppermute | solution.py:152
  69.3 45.8 %collective-permute-start.9 = (bf16[7,8,128,128]{3,2,1,0:T(8,128)(2,1)}, bf16[7,8,128,128]{3,2,1,0:T(8,128)(2,1)}, u32[]{:S(2)}, u32[]{:S(2)}) collective-permute-start(bf16[7,8,128,128]{3,2,1,0:T(8,128)(2,1)} %collective-permute-done.3.above), channel_id=1, source_target_pairs={{4,0},{5,1},{6,2},{7,3},{8,4},{9,5},{10,6},{11,7},{20,16},{21,17},... | collective-permute-start | bytes 5505032 | tf_op jit(solution)/shard_map/ppermute | solution.py:152
  70.6 25.3 %collective-permute-start.12 = (bf16[32,128,128]{2,1,0:T(8,128)(2,1)S(1)}, bf16[32,128,128]{2,1,0:T(8,128)(2,1)}, u32[]{:S(2)}, u32[]{:S(2)}) collective-permute-start(bf16[32,128,128]{2,1,0:T(8,128)(2,1)S(1)} %copy-done), channel_id=1, source_target_pairs={{0,2},{1,3},{2,0},{3,1},{4,6},{5,7},{6,4},{7,5},{8,10},{9,11},{10,... | collective-permute-start | bytes 3145736 | tf_op jit(solution)/shard_map/ppermute | solution.py:152
  83.4 21.8 %collective-permute-start.11 = (bf16[9,128,128]{2,1,0:T(8,128)(2,1)S(1)}, bf16[9,128,128]{2,1,0:T(8,128)(2,1)S(1)}, u32[]{:S(2)}, u32[]{:S(2)}) collective-permute-start(bf16[9,128,128]{2,1,0:T(8,128)(2,1)S(1)} %collective-permute-done.6.wave_own), channel_id=1, source_target_pairs={{4,6},{5,7},{6,4},{7,5},{8,10},{9,11},{10,8},{11,9},{20,22},{21,23... | collective-permute-start | bytes 884744 | tf_op jit(solution)/shard_map/ppermute | solution.py:152
  95.9 20.2 %copy-start.4 = (f32[2,8,7,128]{3,1,2,0:T(8,128)S(1)}, f32[2,8,7,128]{3,1,2,0:T(8,128)}, u32[]{:S(2)}) copy-start(f32[2,8,7,128]{3,1,2,0:T(8,128)} %copy.161) | copy-start | bytes 172036
  95.9 20.2 %copy-start.8 = (s32[3]{0:T(128)S(1)}, s32[3]{0:T(128)}, u32[]{:S(2)}) copy-start(s32[3]{0:T(128)} %add_convert_fusion.3.flags) | copy-start | bytes 40
  106.9 10.8 %copy-start.2 = (bf16[7,8,128,128]{3,2,1,0:T(8,128)(2,1)}, bf16[7,8,128,128]{3,2,1,0:T(8,128)(2,1)S(1)}, u32[]{:S(2)}) copy-start(bf16[7,8,128,128]{3,2,1,0:T(8,128)(2,1)S(1)} %collective-permute-done.8.below) | copy-start | bytes 5505028
  115.0 1.0 collective-permute-start.14
  115.8 20.9 %collective-permute-start.13 = (bf16[24,128,128]{2,1,0:T(8,128)(2,1)}, bf16[24,128,128]{2,1,0:T(8,128)(2,1)}, u32[]{:S(2)}, u32[]{:S(2)}) collective-permute-start(bf16[24,128,128]{2,1,0:T(8,128)(2,1)} %get-tuple-element.78), channel_id=1, source_target_pairs={{0,2},{1,3},{2,0},{3,1},{4,6},{5,7},{6,4},{7,5},{8,10},{9,11},{10,... | collective-permute-start | bytes 2359304 | tf_op jit(solution)/shard_map/ppermute | solution.py:152
  117.8 20.9 %collective-permute-start.16 = (bf16[8,128,128]{2,1,0:T(8,128)(2,1)}, bf16[8,128,128]{2,1,0:T(8,128)(2,1)S(1)}, u32[]{:S(2)}, u32[]{:S(2)}) collective-permute-start(bf16[8,128,128]{2,1,0:T(8,128)(2,1)} %get-tuple-element.86), channel_id=1, source_target_pairs={{4,0},{5,1},{6,2},{7,3},{8,12},{9,13},{10,14},{11,15},{20,16},{21,... | collective-permute-start | bytes 786440 | tf_op jit(solution)/shard_map/ppermute | solution.py:152
  119.7 8.5 %copy-start.14 = (s32[32,3]{0,1:T(4,128)S(1)}, s32[32,3]{0,1:T(4,128)}, u32[]{:S(2)}) copy-start(s32[32,3]{0,1:T(4,128)} %get-tuple-element.62) | copy-start | bytes 1156
  119.7 8.6 %copy-start.13 = (s32[32,3]{0,1:T(4,128)S(1)}, s32[32,3]{0,1:T(4,128)}, u32[]{:S(2)}) copy-start(s32[32,3]{0,1:T(4,128)} %get-tuple-element.61) | copy-start | bytes 1156
  119.7 16.9 %copy-start.1 = (bf16[32,128,128]{2,1,0:T(8,128)(2,1)S(1)}, bf16[32,128,128]{2,1,0:T(8,128)(2,1)}, u32[]{:S(2)}) copy-start(bf16[32,128,128]{2,1,0:T(8,128)(2,1)} %wave.5) | copy-start | bytes 3145732
  119.7 16.9 %copy-start.3 = (f32[24,128,128]{2,1,0:T(8,128)S(1)}, f32[24,128,128]{2,1,0:T(8,128)}, u32[]{:S(2)}) copy-start(f32[24,128,128]{2,1,0:T(8,128)} %get-tuple-element.77.own) | copy-start | bytes 4718596
  119.8 23.3 %collective-permute-start.17 = (bf16[8,128,128]{2,1,0:T(8,128)(2,1)S(1)}, bf16[8,128,128]{2,1,0:T(8,128)(2,1)}, u32[]{:S(2)}, u32[]{:S(2)}) collective-permute-start(bf16[8,128,128]{2,1,0:T(8,128)(2,1)S(1)} %get-tuple-element.97), channel_id=1, source_target_pairs={{4,2},{5,3},{6,0},{7,1},{8,14},{9,15},{10,12},{11,13},{20,18},{21,... | collective-permute-start | bytes 786440 | tf_op jit(solution)/shard_map/ppermute | solution.py:152
  126.3 19.6 %collective-permute-start.15 = (bf16[8,128,128]{2,1,0:T(8,128)(2,1)}, bf16[8,128,128]{2,1,0:T(8,128)(2,1)S(1)}, u32[]{:S(2)}, u32[]{:S(2)}) collective-permute-start(bf16[8,128,128]{2,1,0:T(8,128)(2,1)} %get-tuple-element.95), channel_id=1, source_target_pairs={{0,2},{1,3},{2,0},{3,1},{4,6},{5,7},{6,4},{7,5},{8,10},{9,11},{10,... | collective-permute-start | bytes 786440 | tf_op jit(solution)/shard_map/ppermute | solution.py:152
  138.6 18.1 %collective-permute-start.24 = (f32[24,128,128]{2,1,0:T(8,128)S(1)}, f32[24,128,128]{2,1,0:T(8,128)S(1)}, u32[]{:S(2)}, u32[]{:S(2)}) collective-permute-start(f32[24,128,128]{2,1,0:T(8,128)S(1)} %get-tuple-element.104.first_own), channel_id=1, source_target_pairs={{0,1},{1,0},{2,3},{3,2},{4,5},{5,4},{6,7},{7,6},{8,9},{9,8},{10,11... | collective-permute-start | bytes 4718600 | tf_op jit(solution)/shard_map/ppermute | solution.py:152
  138.7 7.3 %copy-start.5 = (f32[8,128,128]{2,1,0:T(8,128)S(1)}, f32[8,128,128]{2,1,0:T(8,128)}, u32[]{:S(2)}) copy-start(f32[8,128,128]{2,1,0:T(8,128)} %get-tuple-element.92.last_own) | copy-start | bytes 1572868
  138.7 7.3 %copy-start.9 = (f32[8,128]{1,0:T(8,128)S(1)}, f32[8,128]{1,0:T(8,128)}, u32[]{:S(2)}) copy-start(f32[8,128]{1,0:T(8,128)} %get-tuple-element.98.map_a) | copy-start | bytes 12292
  138.7 7.3 %copy-start.10 = (f32[8,128]{1,0:T(8,128)S(1)}, f32[8,128]{1,0:T(8,128)}, u32[]{:S(2)}) copy-start(f32[8,128]{1,0:T(8,128)} %get-tuple-element.99.map_b) | copy-start | bytes 12292
  138.7 7.3 %copy-start.11 = (f32[8,128]{1,0:T(8,128)S(1)}, f32[8,128]{1,0:T(8,128)}, u32[]{:S(2)}) copy-start(f32[8,128]{1,0:T(8,128)} %get-tuple-element.101.map_d) | copy-start | bytes 12292
  144.0 12.7 %copy-start.7 = (s32[32,2]{1,0:T(8,128)S(1)}, s32[32,2]{1,0:T(8,128)}, u32[]{:S(2)}) copy-start(s32[32,2]{1,0:T(8,128)} %copy-done.6) | copy-start | bytes 772
  148.0 1.9 %collective-permute-start.18 = (f32[8,128]{1,0:T(8,128)S(1)}, f32[8,128]{1,0:T(8,128)S(1)}, u32[]{:S(2)}, u32[]{:S(2)}) collective-permute-start(f32[8,128]{1,0:T(8,128)S(1)} %get-tuple-element.102), channel_id=1, source_target_pairs={{0,1},{1,0},{2,3},{3,2},{4,5},{5,4},{6,7},{7,6},{8,9},{9,8},{10,11... | collective-permute-start | bytes 12296 | tf_op jit(solution)/shard_map/ppermute | solution.py:152
  148.0 3.7 %collective-permute-start.19 = (f32[8,128]{1,0:T(8,128)S(1)}, f32[8,128]{1,0:T(8,128)S(1)}, u32[]{:S(2)}, u32[]{:S(2)}) collective-permute-start(f32[8,128]{1,0:T(8,128)S(1)} %get-tuple-element.102), channel_id=1, source_target_pairs={{0,2},{1,3},{2,0},{3,1},{4,6},{5,7},{6,4},{7,5},{8,10},{9,11},{10,... | collective-permute-start | bytes 12296 | tf_op jit(solution)/shard_map/ppermute | solution.py:152
  148.6 3.1 %collective-permute-start.20 = (f32[8,128]{1,0:T(8,128)S(1)}, f32[8,128]{1,0:T(8,128)S(1)}, u32[]{:S(2)}, u32[]{:S(2)}) collective-permute-start(f32[8,128]{1,0:T(8,128)S(1)} %get-tuple-element.102), channel_id=1, source_target_pairs={{0,3},{1,2},{2,1},{3,0},{4,7},{5,6},{6,5},{7,4},{8,11},{9,10},{10,... | collective-permute-start | bytes 12296 | tf_op jit(solution)/shard_map/ppermute | solution.py:152
  151.7 4.9 %collective-permute-start.25 = (f32[16,128,128]{2,1,0:T(8,128)S(1)}, f32[16,128,128]{2,1,0:T(8,128)S(1)}, u32[]{:S(2)}, u32[]{:S(2)}) collective-permute-start(f32[16,128,128]{2,1,0:T(8,128)S(1)} %get-tuple-element.106.late_own), channel_id=1, source_target_pairs={{0,1},{1,0},{2,3},{3,2},{4,5},{5,4},{6,7},{7,6},{8,9},{9,8},{10,11... | collective-permute-start | bytes 3145736 | tf_op jit(solution)/shard_map/ppermute | solution.py:152
  151.8 7.1 %collective-permute-start.21 = (f32[32,128]{1,0:T(8,128)S(1)}, f32[32,128]{1,0:T(8,128)S(1)}, u32[]{:S(2)}, u32[]{:S(2)}) collective-permute-start(f32[32,128]{1,0:T(8,128)S(1)} %constant_dynamic-update-slice_fusion.sums), channel_id=1, source_target_pairs={{0,4},{1,5},{2,6},{3,7},{4,0},{5,1},{6,2},{7,3},{8,12},{9,13},{10,... | collective-permute-start | bytes 49160 | tf_op jit(solution)/shard_map/ppermute | solution.py:152
  154.2 4.7 %collective-permute-start.22 = (f32[32,128]{1,0:T(8,128)S(1)}, f32[32,128]{1,0:T(8,128)S(1)}, u32[]{:S(2)}, u32[]{:S(2)}) collective-permute-start(f32[32,128]{1,0:T(8,128)S(1)} %constant_dynamic-update-slice_fusion.sums), channel_id=1, source_target_pairs={{0,8},{1,9},{2,10},{3,11},{4,12},{5,13},{6,14},{7,15},{8,0},{9,1},... | collective-permute-start | bytes 49160 | tf_op jit(solution)/shard_map/ppermute | solution.py:152
  154.9 5.5 %collective-permute-start.23 = (f32[32,128]{1,0:T(8,128)S(1)}, f32[32,128]{1,0:T(8,128)S(1)}, u32[]{:S(2)}, u32[]{:S(2)}) collective-permute-start(f32[32,128]{1,0:T(8,128)S(1)} %constant_dynamic-update-slice_fusion.sums), channel_id=1, source_target_pairs={{0,12},{1,13},{2,14},{3,15},{4,8},{5,9},{6,10},{7,11},{8,4},{9,5},... | collective-permute-start | bytes 49160 | tf_op jit(solution)/shard_map/ppermute | solution.py:152
